TPU v7x, 32 devices: a whole 2x2x4 slice. The times are simulated.
32 devices in a mesh: dp: 8 (over y, x, core), ctx: 4 (over z).
Axes of the slice: x: 2, y: 2, z: 4, core: 2. Of those that a mesh axis runs over, the one named last changes fastest.
Arguments:
- inputs: bfloat16 [8, 2048, 1280], P('dp', 'ctx'), may hold values from -6 to 6
- teacher: bfloat16 [8, 2048, 1280], P('dp', 'ctx'), may hold values from -6 to 6
- lengths: int32 [8], P('dp'), may hold values from 512 to 2048, as said below
- query_weight: bfloat16 [1280, 1280], P(('dp', 'ctx')), may hold values from -0.15625 to 0.15625
- key_weight: bfloat16 [1280, 1280], P(('dp', 'ctx')), may hold values from -0.15625 to 0.15625
- value_projection: bfloat16 [1280, 1280], P(('dp', 'ctx')), may hold values from -0.15625 to 0.15625
- output_weight: bfloat16 [1280, 1280], P(('dp', 'ctx')), may hold values from -0.15625 to 0.15625
- score_gain: bfloat16 [1280], P(('dp', 'ctx')), may hold values from 1 to 1.59375
- attention_step: bfloat16 [1280], P(('dp', 'ctx')), may hold values from 0.19921875 to 0.59765625
- up_weight: bfloat16 [1280, 5120], P(('dp', 'ctx')), may hold values from -0.15625 to 0.15625
- gate_weight: bfloat16 [1280, 5120], P(('dp', 'ctx')), may hold values from -0.15625 to 0.15625
- down_weight: bfloat16 [5120, 1280], P(('dp', 'ctx')), may hold values from -0.078125 to 0.078125
- up_scale: bfloat16 [5120], P(('dp', 'ctx')), may hold values from 0.5 to 2
- gate_scale: bfloat16 [5120], P(('dp', 'ctx')), may hold values from 0.5 to 2
- swiglu_step: bfloat16 [1280], P(('dp', 'ctx')), may hold values from 0.19921875 to 0.59765625
Outputs:
- layer_out: bfloat16 [8, 2048, 1280], P('dp', 'ctx')
- distill_loss_mean: float32 [], replicated
- input_grad: float32 [8, 2048, 1280], P('dp', 'ctx')
- query_grad: float32 [1280, 1280], P(('dp', 'ctx'))
- key_grad: float32 [1280, 1280], P(('dp', 'ctx'))
- value_grad: float32 [1280, 1280], P(('dp', 'ctx'))
- output_grad: float32 [1280, 1280], P(('dp', 'ctx'))
- score_gain_grad: float32 [1280], P(('dp', 'ctx'))
- attention_step_grad: float32 [1280], P(('dp', 'ctx'))
- up_grad: float32 [1280, 5120], P(('dp', 'ctx'))
- gate_grad: float32 [1280, 5120], P(('dp', 'ctx'))
- down_grad: float32 [5120, 1280], P(('dp', 'ctx'))
- up_scale_grad: float32 [5120], P(('dp', 'ctx'))
- gate_scale_gradient: float32 [5120], P(('dp', 'ctx'))
- swiglu_step_grad: float32 [1280], P(('dp', 'ctx'))
Inputs may be any that keep to these rules, and one draw needn't show every extreme that they name: `lengths`: each slot's valid tokens are its first positions; at least one slot is full in every draw.
All inputs are finite; a program needn't handle non-finite values.
Results may differ from a plain program's by a relative error of at most 0.019.
Values may be sent and summed in bfloat16 or wider, within the bound.
No kernel may reach another device: no remote copies, remote signals or barrier semaphores. Data moves between devices by JAX's collectives and lax.ppermute only.
A program may use at most 320 MiB of HBM per device.

v0:
```python
import jax
import jax.numpy as jnp
from jax import lax
from jax.sharding import PartitionSpec as P

HD = 64


eps = 1e-06
loss_scale = 32768.0


def normalize(value_rows):
    return value_rows * lax.rsqrt(jnp.mean(value_rows * value_rows, axis=-1, keepdims=True) + eps)


def norm_back(value_rows, normed, grad):
    factor = lax.rsqrt(jnp.mean(value_rows * value_rows, axis=-1, keepdims=True) + eps)
    return factor * (grad - normed * jnp.mean(grad * normed, axis=-1, keepdims=True))


def matmul(left, right):
    return jnp.dot(left, right, preferred_element_type=jnp.float32)


def left_tdot(left, right):
    return lax.dot_general(
        left, right, (((0,), (0,)), ((), ())), preferred_element_type=jnp.float32
    )


def right_tdot(left, right):
    return lax.dot_general(
        left, right, (((1,), (1,)), ((), ())), preferred_element_type=jnp.float32
    )


def block_scores(queries, keys, query_pos, key_pos, lens):
    scores = jnp.einsum(
        "sqhd,skhd->shqk", queries, keys, preferred_element_type=jnp.float32
    ) * HD ** (-0.5)
    allowed = (key_pos[None, None, :] <= query_pos[None, :, None]) & (
        key_pos[None, None, :] < lens[:, None, None]
    )
    return (scores, allowed[:, None])


def per_device(
    inputs,
    teacher,
    lengths,
    query_weight,
    key_weight,
    value_projection,
    output_weight,
    score_gain,
    attention_step,
    up_weight,
    gate_weight,
    down_weight,
    up_scale,
    gate_scale,
    swiglu_step,
):
    seqs, local, width = inputs.shape
    full_len = local * lax.axis_size("ctx")
    rows = seqs * local
    heads = width // HD
    key_block = min(512, full_len)
    query_pos = lax.axis_index("ctx") * local + jnp.arange(local, dtype=jnp.int32)
    valid = (query_pos[None, :] < lengths[:, None]).astype(jnp.float32).reshape(rows, 1)
    count_local = jnp.sum(valid)
    full_query, full_key, full_value, full_output, full_gain, full_astep = (
        lax.all_gather(query_weight, ("dp", "ctx"), axis=0, tiled=True),
        lax.all_gather(key_weight, ("dp", "ctx"), axis=0, tiled=True),
        lax.all_gather(value_projection, ("dp", "ctx"), axis=0, tiled=True),
        lax.all_gather(output_weight, ("dp", "ctx"), axis=0, tiled=True),
        lax.all_gather(score_gain, ("dp", "ctx"), axis=0, tiled=True),
        lax.all_gather(attention_step, ("dp", "ctx"), axis=0, tiled=True),
    )
    states = inputs.reshape(rows, width)
    resid = states.astype(jnp.float32)
    queries = matmul(states, full_query)
    keys_raw = matmul(states, full_key)
    values_raw = matmul(states, full_value)
    gains = full_gain.astype(jnp.float32).reshape(heads, HD)
    query_norm = normalize(queries.reshape(rows, heads, HD))
    key_norm = normalize(keys_raw.reshape(rows, heads, HD))
    q_heads = (gains * query_norm).astype(jnp.bfloat16).reshape(seqs, local, heads, HD)
    k_flat = (gains * key_norm).astype(jnp.bfloat16).reshape(seqs, local, width)
    v_flat = values_raw.astype(jnp.bfloat16).reshape(seqs, local, width)

    def key_step(carry, key_piece, value_piece, key_pos):
        top, total, accum = carry
        count_keys = key_piece.shape[1]
        scores, allowed = block_scores(
            q_heads, key_piece.reshape(seqs, count_keys, heads, HD), query_pos, key_pos, lengths
        )
        scores = jnp.where(allowed, scores, -1e30)
        top_new = jnp.maximum(top, jnp.max(scores, axis=-1))
        weights = jnp.where(allowed, jnp.exp(scores - top_new[..., None]), 0.0)
        factor = jnp.exp(top - top_new)
        total = total * factor + jnp.sum(weights, axis=-1)
        accum = accum * jnp.transpose(factor, (0, 2, 1))[..., None] + jnp.einsum(
            "shqk,skhd->sqhd",
            weights.astype(jnp.bfloat16),
            value_piece.reshape(seqs, count_keys, heads, HD),
            preferred_element_type=jnp.float32,
        )
        return (top_new, total, accum)

    init = (
        jnp.full((seqs, heads, local), -1e30, jnp.float32),
        jnp.zeros((seqs, heads, local), jnp.float32),
        jnp.zeros((seqs, local, heads, HD), jnp.float32),
    )
    carry = init
    key_piece = lax.all_gather(k_flat, "ctx", axis=1, tiled=True)
    value_piece = lax.all_gather(v_flat, "ctx", axis=1, tiled=True)
    count_keys = key_piece.shape[1]

    def inner(state, index):
        offset = index * key_block
        key_part = lax.dynamic_slice_in_dim(key_piece, offset, key_block, 1)
        value_part = lax.dynamic_slice_in_dim(value_piece, offset, key_block, 1)
        positions = offset + jnp.arange(key_block, dtype=jnp.int32)
        return (key_step(state, key_part, value_part, positions), None)

    carry, unused = lax.scan(inner, carry, jnp.arange(count_keys // key_block, dtype=jnp.int32))
    top, total, accum = carry
    mixed = accum / jnp.transpose(total, (0, 2, 1))[..., None]
    log_total = top + jnp.log(total)
    mixed_low = mixed.reshape(rows, width).astype(jnp.bfloat16)
    branch = matmul(mixed_low, full_output)
    branch_norm = normalize(branch)
    astep = full_astep.astype(jnp.float32)
    first = resid + astep * (branch_norm - resid)
    middle = normalize(first)
    middle_low = middle.astype(jnp.bfloat16)
    full_up, full_gate, full_down, full_uscale, complete_gate_scale, full_mstep = (
        lax.all_gather(up_weight, ("dp", "ctx"), axis=0, tiled=True),
        lax.all_gather(gate_weight, ("dp", "ctx"), axis=0, tiled=True),
        lax.all_gather(down_weight, ("dp", "ctx"), axis=0, tiled=True),
        lax.all_gather(up_scale, ("dp", "ctx"), axis=0, tiled=True),
        lax.all_gather(gate_scale, ("dp", "ctx"), axis=0, tiled=True),
        lax.all_gather(swiglu_step, ("dp", "ctx"), axis=0, tiled=True),
    )
    upper = matmul(middle_low, full_up)
    gating = matmul(middle_low, full_gate)
    scale_up = full_uscale.astype(jnp.float32)
    scale_gate = complete_gate_scale.astype(jnp.float32)
    upper_scaled = upper * scale_up
    gate_arg = gating * scale_gate
    gate_act = jax.nn.silu(gate_arg)
    hidden = (upper_scaled * gate_act).astype(jnp.bfloat16)
    lower = matmul(hidden, full_down)
    lower_norm = normalize(lower)
    mstep = full_mstep.astype(jnp.float32)
    second = middle + mstep * (lower_norm - middle)
    final = normalize(second)
    target = teacher.reshape(rows, width).astype(jnp.float32)
    diff = final - target
    err_local = jnp.sum(valid * diff * diff)
    err_total, count = lax.psum((err_local, count_local), ("dp", "ctx"))
    cot = loss_scale * 2.0 / count * valid * diff
    full_up, full_gate, full_down, full_uscale, complete_gate_scale, full_mstep = (
        lax.all_gather(up_weight, ("dp", "ctx"), axis=0, tiled=True),
        lax.all_gather(gate_weight, ("dp", "ctx"), axis=0, tiled=True),
        lax.all_gather(down_weight, ("dp", "ctx"), axis=0, tiled=True),
        lax.all_gather(up_scale, ("dp", "ctx"), axis=0, tiled=True),
        lax.all_gather(gate_scale, ("dp", "ctx"), axis=0, tiled=True),
        lax.all_gather(swiglu_step, ("dp", "ctx"), axis=0, tiled=True),
    )
    d_second = norm_back(second, final, cot)
    d_middle = d_second * (1.0 - mstep)
    grad_mstep = jnp.sum(d_second * (lower_norm - middle), axis=0)
    d_lower = norm_back(lower, lower_norm, d_second * mstep).astype(jnp.bfloat16)
    grad_down = left_tdot(hidden, d_lower)
    d_hidden = right_tdot(d_lower, full_down)
    d_upper = d_hidden * gate_act
    sigmoid_gate = jax.nn.sigmoid(gate_arg)
    d_gate_arg = d_hidden * upper_scaled * (sigmoid_gate * (1.0 + gate_arg * (1.0 - sigmoid_gate)))
    grad_uscale = jnp.sum(d_upper * upper, axis=0)
    grad_gscale = jnp.sum(d_gate_arg * gating, axis=0)
    d_up_low = (d_upper * scale_up).astype(jnp.bfloat16)
    d_gate_low = (d_gate_arg * scale_gate).astype(jnp.bfloat16)
    d_middle = d_middle + right_tdot(d_up_low, full_up) + right_tdot(d_gate_low, full_gate)
    grad_up = left_tdot(middle_low, d_up_low)
    grad_gate = left_tdot(middle_low, d_gate_low)
    up_grad, gate_grad, down_grad, up_scale_grad, gate_scale_gradient, swiglu_step_grad = (
        lax.psum_scatter(grad_up, ("dp", "ctx"), scatter_dimension=0, tiled=True),
        lax.psum_scatter(grad_gate, ("dp", "ctx"), scatter_dimension=0, tiled=True),
        lax.psum_scatter(grad_down, ("dp", "ctx"), scatter_dimension=0, tiled=True),
        lax.psum_scatter(grad_uscale, ("dp", "ctx"), scatter_dimension=0, tiled=True),
        lax.psum_scatter(grad_gscale, ("dp", "ctx"), scatter_dimension=0, tiled=True),
        lax.psum_scatter(grad_mstep, ("dp", "ctx"), scatter_dimension=0, tiled=True),
    )
    d_first = norm_back(first, middle, d_middle)
    input_grad = d_first * (1.0 - astep)
    grad_astep = jnp.sum(d_first * (branch_norm - resid), axis=0)
    d_branch = norm_back(branch, branch_norm, d_first * astep).astype(jnp.bfloat16)
    full_query, full_key, full_value, full_output, full_gain, full_astep = (
        lax.all_gather(query_weight, ("dp", "ctx"), axis=0, tiled=True),
        lax.all_gather(key_weight, ("dp", "ctx"), axis=0, tiled=True),
        lax.all_gather(value_projection, ("dp", "ctx"), axis=0, tiled=True),
        lax.all_gather(output_weight, ("dp", "ctx"), axis=0, tiled=True),
        lax.all_gather(score_gain, ("dp", "ctx"), axis=0, tiled=True),
        lax.all_gather(attention_step, ("dp", "ctx"), axis=0, tiled=True),
    )
    gains = full_gain.astype(jnp.float32).reshape(heads, HD)
    grad_output = left_tdot(mixed_low, d_branch)
    d_mixed = right_tdot(d_branch, full_output).astype(jnp.bfloat16)
    d_mixed_heads = d_mixed.reshape(seqs, local, heads, HD)
    delta = jnp.transpose(jnp.sum(d_mixed_heads.astype(jnp.float32) * mixed, axis=-1), (0, 2, 1))
    whole_keys, whole_values = (
        lax.all_gather(k_flat, "ctx", axis=1, tiled=True),
        lax.all_gather(v_flat, "ctx", axis=1, tiled=True),
    )

    def query_terms(index):
        offset = index * key_block
        key_part = lax.dynamic_slice_in_dim(whole_keys, offset, key_block, 1).reshape(
            seqs, key_block, heads, HD
        )
        value_part = lax.dynamic_slice_in_dim(whole_values, offset, key_block, 1).reshape(
            seqs, key_block, heads, HD
        )
        key_pos = offset + jnp.arange(key_block, dtype=jnp.int32)
        scores, allowed = block_scores(q_heads, key_part, query_pos, key_pos, lengths)
        probs = jnp.where(allowed, jnp.exp(scores - log_total[..., None]), 0.0)
        d_probs = jnp.einsum(
            "sqhd,skhd->shqk", d_mixed_heads, value_part, preferred_element_type=jnp.float32
        )
        d_scores = (probs * (d_probs - delta[..., None])).astype(jnp.bfloat16)
        d_query_part = jnp.einsum(
            "shqk,skhd->sqhd", d_scores, key_part, preferred_element_type=jnp.float32
        )
        return (offset, probs, d_scores, d_query_part)

    def key_back(carry, index):
        d_query_acc, d_key_all, d_value_all = carry
        offset, probs, d_scores, d_query_part = query_terms(index)
        d_query_acc = d_query_acc + d_query_part
        d_key_part = jnp.einsum(
            "shqk,sqhd->skhd", d_scores, q_heads, preferred_element_type=jnp.float32
        ) * HD ** (-0.5)
        d_value_part = jnp.einsum(
            "shqk,sqhd->skhd",
            probs.astype(jnp.bfloat16),
            d_mixed_heads,
            preferred_element_type=jnp.float32,
        )
        d_key_all = lax.dynamic_update_slice_in_dim(
            d_key_all, d_key_part.reshape(seqs, key_block, width), offset, 1
        )
        d_value_all = lax.dynamic_update_slice_in_dim(
            d_value_all, d_value_part.reshape(seqs, key_block, width), offset, 1
        )
        return ((d_query_acc, d_key_all, d_value_all), None)

    start_carry = (
        jnp.zeros((seqs, local, heads, HD), jnp.float32),
        jnp.zeros((seqs, full_len, width), jnp.float32),
        jnp.zeros((seqs, full_len, width), jnp.float32),
    )
    (d_query_heads, d_key_all, d_value_all), unused = lax.scan(
        key_back, start_carry, jnp.arange(full_len // key_block, dtype=jnp.int32)
    )
    d_key_local, d_value_local = (
        lax.psum_scatter(
            d_key_all.astype(jnp.bfloat16), "ctx", scatter_dimension=1, tiled=True
        ).astype(jnp.float32),
        lax.psum_scatter(
            d_value_all.astype(jnp.bfloat16), "ctx", scatter_dimension=1, tiled=True
        ).astype(jnp.float32),
    )
    d_key_heads = d_key_local.reshape(rows, heads, HD)
    d_value_local = d_value_local.reshape(rows, width)
    d_query_heads = (d_query_heads * HD ** (-0.5)).reshape(rows, heads, HD)
    grad_gain = jnp.sum(d_query_heads * query_norm, axis=0) + jnp.sum(
        d_key_heads * key_norm, axis=0
    )
    d_query_low = (
        norm_back(queries.reshape(rows, heads, HD), query_norm, d_query_heads * gains)
        .reshape(rows, width)
        .astype(jnp.bfloat16)
    )
    d_key_low = (
        norm_back(keys_raw.reshape(rows, heads, HD), key_norm, d_key_heads * gains)
        .reshape(rows, width)
        .astype(jnp.bfloat16)
    )
    d_value_low = d_value_local.astype(jnp.bfloat16)
    input_grad = (
        input_grad
        + right_tdot(d_query_low, full_query)
        + right_tdot(d_key_low, full_key)
        + right_tdot(d_value_low, full_value)
    )
    grad_query = left_tdot(states, d_query_low)
    grad_key = left_tdot(states, d_key_low)
    grad_value = left_tdot(states, d_value_low)
    query_grad, key_grad, value_grad, output_grad, score_gain_grad, attention_step_grad = (
        lax.psum_scatter(grad_query, ("dp", "ctx"), scatter_dimension=0, tiled=True),
        lax.psum_scatter(grad_key, ("dp", "ctx"), scatter_dimension=0, tiled=True),
        lax.psum_scatter(grad_value, ("dp", "ctx"), scatter_dimension=0, tiled=True),
        lax.psum_scatter(grad_output, ("dp", "ctx"), scatter_dimension=0, tiled=True),
        lax.psum_scatter(grad_gain.reshape(width), ("dp", "ctx"), scatter_dimension=0, tiled=True),
        lax.psum_scatter(grad_astep, ("dp", "ctx"), scatter_dimension=0, tiled=True),
    )
    distill_loss_mean = err_total / count
    layer_out = final.astype(jnp.bfloat16).reshape(seqs, local, width)
    return (
        layer_out,
        distill_loss_mean,
        input_grad.reshape(seqs, local, width),
        query_grad,
        key_grad,
        value_grad,
        output_grad,
        score_gain_grad,
        attention_step_grad,
        up_grad,
        gate_grad,
        down_grad,
        up_scale_grad,
        gate_scale_gradient,
        swiglu_step_grad,
    )


def solution(mesh):
    placed = (
        P("dp", "ctx", None),
        P("dp", "ctx", None),
        P("dp"),
        P(("dp", "ctx"), None),
        P(("dp", "ctx"), None),
        P(("dp", "ctx"), None),
        P(("dp", "ctx"), None),
        P(("dp", "ctx")),
        P(("dp", "ctx")),
        P(("dp", "ctx"), None),
        P(("dp", "ctx"), None),
        P(("dp", "ctx"), None),
        P(("dp", "ctx")),
        P(("dp", "ctx")),
        P(("dp", "ctx")),
    )
    return jax.shard_map(
        per_device,
        mesh=mesh,
        in_specs=placed,
        out_specs=(
            P("dp", "ctx", None),
            P(),
            P("dp", "ctx", None),
            P(("dp", "ctx"), None),
            P(("dp", "ctx"), None),
            P(("dp", "ctx"), None),
            P(("dp", "ctx"), None),
            P(("dp", "ctx")),
            P(("dp", "ctx")),
            P(("dp", "ctx"), None),
            P(("dp", "ctx"), None),
            P(("dp", "ctx"), None),
            P(("dp", "ctx")),
            P(("dp", "ctx")),
            P(("dp", "ctx")),
        ),
        check_vma=False,
    )
```

profile of v0, /device:TPU:0, one launch (start us, length us, event | category | flops | bytes accessed | tf_op | source)
XLA Modules:
  0.0 3595.2 jit_solution(1335169165440818971)
XLA Ops:
  9.5 63.4 %all-gather.17.cloned.1.call-done = bf16[1280,1280]{1,0:T(8,128)(2,1)} async-done(((bf16[40,1280]{1,0:T(8,128)(2,1)}), bf16[1280,1280]{1,0:T(8,128)(2,1)}) %all-gather.17.cloned.1.call-update) | async-done | bytes 3276816 | tf_op jit(solution)/shard_map/all_gather | solution.py:76
  79.5 39.0 %all-reduce.11 = (bf16[1280]{0:T(1024)(128)(2,1)S(1)}, bf16[1280]{0:T(1024)(128)(2,1)S(1)}, bf16[5120]{0:T(1024)(128)(2,1)S(1)}, bf16[5120]{0:T(1024)(128)(2,1)S(1)}, bf16[1280]{0:T(1024)(128)(2,1)S(1)}) all-reduce(bf16[1280]{0:T(1024)(128)(2,1)S(1)} %dynamic-update-slice.1, ...), channel_id=1, replica_groups=mesh['dp'=8,'ctx'=4] {'dp','ctx'}, use_global_device_ids=true, to_apply=%add.1 | all-reduce | flops 14080 | bytes 56320
  139.6 55.5 %all-gather.11.cloned.1.call-done = bf16[1280,1280]{1,0:T(8,128)(2,1)} async-done(((bf16[40,1280]{1,0:T(8,128)(2,1)}), bf16[1280,1280]{1,0:T(8,128)(2,1)}) %all-gather.11.cloned.1.call-update) | async-done | bytes 3276816 | tf_op jit(solution)/shard_map/all_gather | solution.py:75
  215.5 41.5 %psum.15 = f32[]{:T(128)} all-reduce(f32[]{:T(128)} %fusion.56), channel_id=1, replica_groups=mesh['dp'=8,'ctx'=4] {'dp','ctx'}, use_global_device_ids=true, to_apply=%region_13.14 | all-reduce | flops 1 | bytes 8 | tf_op jit(solution)/shard_map/psum | solution.py:164
  258.9 35.6 all-gather.27.cloned.1.call-done
  302.4 90.5 %all-gather.13.cloned.1.call-done = bf16[1,2048,1280]{1,2,0:T(8,128)(2,1)} async-done(((bf16[1,512,1280]{1,2,0:T(8,128)(2,1)}), bf16[1,2048,1280]{1,2,0:T(8,128)(2,1)}) %all-gather.13.cloned.1.call-update) | async-done | bytes 5242896 | tf_op jit(solution)/shard_map/all_gather | solution.py:118
  392.9 156.0 %while.30 = (s32[]{:T(128)}, f32[1,20,512]{2,1,0:T(8,128)S(1)}, f32[1,20,512]{2,1,0:T(8,128)}, f32[1,512,20,64]{1,3,2,0:T(8,128)}, s32[4]{0:T(128)S(1)}, /*index...) while((s32[]{:T(128)}, f32[1,20,512]{2,1,0:T(8,128)S(1)}, ...), condition=%wide.region_5.6_spmd.clone, body=%wide.region_2.5_spmd.clone.sunk | while | flops 1412888576 | bytes 164636064 | solution.py:129
  574.1 79.1 %all-gather.21.cloned.1.call-done = bf16[1280,5120]{1,0:T(8,128)(2,1)} async-done(((bf16[40,5120]{1,0:T(8,128)(2,1)}), bf16[1280,5120]{1,0:T(8,128)(2,1)}) %all-gather.21.cloned.1.call-update) | async-done | bytes 13107216 | tf_op jit(solution)/shard_map/all_gather | solution.py:141
  653.2 17.7 multiply_convert_fusion.2
  670.9 81.9 %all-gather.25.cloned.1.call-done = bf16[5120,1280]{1,0:T(8,128)(2,1)} async-done(((bf16[160,1280]{1,0:T(8,128)(2,1)}), bf16[5120,1280]{1,0:T(8,128)(2,1)}) %all-gather.25.cloned.1.call-update) | async-done | bytes 13107216 | tf_op jit(solution)/shard_map/all_gather | solution.py:143
  771.6 23.5 multiply_reduce_fusion
  846.5 216.9 %while.31 = (s32[]{:T(128)}, f32[1,512,20,64]{1,3,2,0:T(8,128)}, bf16[1,2048,1280]{1,2,0:T(8,128)(2,1)}, bf16[1,2048,1280]{1,2,0:T(8,128)(2,1)}, s32[4]{0:T(128)...) while((s32[]{:T(128)}, f32[1,512,20,64]{1,3,2,0:T(8,128)}, ...), condition=%wide.region_20.21_spmd.clone, body=%wide.region_19.20_spmd.clone.sunk | while | flops 3411019776 | bytes 122815744 | solution.py:266
  1070.4 85.2 %reduce-scatter.16.cloned.1.call-done = bf16[1,512,1280]{1,2,0:T(8,128)(2,1)} async-done(((bf16[1,2048,1280]{1,2,0:T(8,128)(2,1)}), bf16[1,512,1280]{1,2,0:T(8,128)(2,1)}) %reduce-scatter.16.cloned.1.call-update) | async-done | bytes 1310736 | tf_op jit(solution)/shard_map/reduce_scatter | solution.py:270
  1192.5 59.7 %reduce-scatter.18.cloned.1.call-done = bf16[1,512,1280]{1,2,0:T(8,128)(2,1)} async-done(((bf16[1,2048,1280]{1,2,0:T(8,128)(2,1)}), bf16[1,512,1280]{1,2,0:T(8,128)(2,1)}) %reduce-scatter.18.cloned.1.call-update) | async-done | bytes 1310736 | tf_op jit(solution)/shard_map/reduce_scatter | solution.py:273
  1267.5 16.4 fusion.40
  1300.7 16.0 fusion.60
  1317.4 44.2 %all-reduce.10 = (f32[]{:T(128)}, f32[1280]{0:T(1024)S(1)}, f32[1280]{0:T(1024)S(1)}, f32[5120]{0:T(1024)S(1)}, f32[5120]{0:T(1024)S(1)}, /*index=5*/f32[1280]{0:T(1024)S(1)}) all-reduce(f32[]{:T(128)} %get-tuple-element.349, f32[1280]{0:T(1024)S(1)} %add.211, ...), channel_id=1, replica_groups=mesh['dp'=8,'ctx'=4] {'dp','ctx'}, use_global_device_ids=true, to_apply=%region_11.12 | all-reduce | flops 14081 | bytes 112648 | tf_op jit(solution)/shard_map/psum | solution.py:164
  1376.2 39.7 %reduce-scatter.20.cloned.1.call-done = f32[40,1280]{1,0:T(8,128)} async-done(((f32[1280,1280]{1,0:T(8,128)}), f32[40,1280]{1,0:T(8,128)}) %reduce-scatter.20.cloned.1.call-update) | async-done | bytes 204816 | tf_op jit(solution)/shard_map/reduce_scatter | solution.py:307
  1415.9 161.7 %reduce-scatter.28.cloned.1.call-done = f32[40,1280]{1,0:T(8,128)} async-done(((f32[1280,1280]{1,0:T(8,128)}), f32[40,1280]{1,0:T(8,128)}) %reduce-scatter.28.cloned.1.call-update) | async-done | bytes 204816
  1577.6 162.5 %reduce-scatter.30.cloned.1.call-done = f32[40,1280]{1,0:T(8,128)} async-done(((f32[1280,1280]{1,0:T(8,128)}), f32[40,1280]{1,0:T(8,128)}) %reduce-scatter.30.cloned.1.call-update) | async-done | bytes 204816
  1740.1 161.3 %reduce-scatter.32.cloned.1.call-done = f32[40,1280]{1,0:T(8,128)} async-done(((f32[1280,1280]{1,0:T(8,128)}), f32[40,1280]{1,0:T(8,128)}) %reduce-scatter.32.cloned.1.call-update) | async-done | bytes 204816
  1901.4 562.5 %reduce-scatter.24.cloned.1.call-done = f32[40,5120]{1,0:T(8,128)} async-done(((f32[1280,5120]{1,0:T(8,128)}), f32[40,5120]{1,0:T(8,128)}) %reduce-scatter.24.cloned.1.call-update) | async-done | bytes 819216 | tf_op jit(solution)/shard_map/reduce_scatter | solution.py:192
  2463.9 561.5 %reduce-scatter.22.cloned.1.call-done = f32[40,5120]{1,0:T(8,128)} async-done(((f32[1280,5120]{1,0:T(8,128)}), f32[40,5120]{1,0:T(8,128)}) %reduce-scatter.22.cloned.1.call-update) | async-done | bytes 819216 | tf_op jit(solution)/shard_map/reduce_scatter | solution.py:191
  3025.5 561.6 %reduce-scatter.26.cloned.1.call-done = f32[160,1280]{1,0:T(8,128)} async-done(((f32[5120,1280]{1,0:T(8,128)}), f32[160,1280]{1,0:T(8,128)}) %reduce-scatter.26.cloned.1.call-update) | async-done | bytes 819216 | tf_op jit(solution)/shard_map/reduce_scatter | solution.py:193
  (398 shorter events, 610.2 us)
Async XLA Ops:
  7.2 65.7 %all-gather.17.cloned.1.call-start = ((), (), s32[]{:S(2)}) async-start(), calls=%async_computation.12 | async-start | bytes 3379200 | tf_op jit(solution)/shard_map/all_gather | solution.py:76
  7.9 126.1 %all-gather.15.cloned.1.call-start = ((), (), s32[]{:S(2)}) async-start(), calls=%async_computation.11 | async-start | bytes 3379200 | tf_op jit(solution)/shard_map/all_gather | solution.py:74
  8.7 186.4 %all-gather.11.cloned.1.call-start = ((), (), s32[]{:S(2)}) async-start(), calls=%async_computation.9 | async-start | bytes 3379200 | tf_op jit(solution)/shard_map/all_gather | solution.py:75
  9.4 285.0 %all-gather.27.cloned.1.call-start = ((), (), s32[]{:S(2)}) async-start(), calls=%async_computation.23 | async-start | bytes 6553600 | tf_op jit(solution)/shard_map/all_gather | solution.py:119
  78.2 314.8 %all-gather.13.cloned.1.call-start = ((), (), s32[]{:S(2)}) async-start(), calls=%async_computation.10 | async-start | bytes 6553600 | tf_op jit(solution)/shard_map/all_gather | solution.py:118
  118.6 95.0 %copy-start.59 = (bf16[1280]{0:T(1024)(128)(2,1)}, bf16[1280]{0:T(1024)(128)(2,1)S(1)}, u32[]{:S(2)}) copy-start(bf16[1280]{0:T(1024)(128)(2,1)S(1)} %get-tuple-element.403) | copy-start | bytes 7684
  209.5 341.6 %all-gather.19.cloned.1.call-start = ((), (), s32[]{:S(2)}) async-start(), calls=%async_computation.13 | async-start | bytes 3379200 | tf_op jit(solution)/shard_map/all_gather | solution.py:77
  210.1 349.1 %all-gather.23.cloned.1.call-start = ((), (), s32[]{:S(2)}) async-start(), calls=%async_computation.15 | async-start | bytes 13516800 | tf_op jit(solution)/shard_map/all_gather | solution.py:142
  210.8 442.3 %all-gather.21.cloned.1.call-start = ((), (), s32[]{:S(2)}) async-start(), calls=%async_computation.14 | async-start | bytes 13516800 | tf_op jit(solution)/shard_map/all_gather | solution.py:141
  211.6 541.2 %all-gather.25.cloned.1.call-start = ((), (), s32[]{:S(2)}) async-start(), calls=%async_computation.16 | async-start | bytes 13516800 | tf_op jit(solution)/shard_map/all_gather | solution.py:143
  212.3 943.2 %reduce-scatter.16.cloned.1.call-start = ((), (), s32[]{:S(2)}) async-start(), calls=%async_computation.17 | async-start | bytes 6553600 | tf_op jit(solution)/shard_map/reduce_scatter | solution.py:270
  213.6 342.2 %copy-start.45 = (f32[1280]{0:T(1024)}, f32[1280]{0:T(1024)S(1)}, u32[]{:S(2)}) copy-start(f32[1280]{0:T(1024)S(1)} %convert_element_type.125) | copy-start | bytes 15364
  213.6 596.1 %copy-start.56 = (f32[5120]{0:T(1024)}, f32[5120]{0:T(1024)S(1)}, u32[]{:S(2)}) copy-start(f32[5120]{0:T(1024)S(1)} %convert_element_type.134) | copy-start | bytes 61444
  559.2 94.0 %copy-start.58 = (f32[5120]{0:T(1024)S(1)}, f32[5120]{0:T(1024)}, u32[]{:S(2)}) copy-start(f32[5120]{0:T(1024)} %convert_element_type.133) | copy-start | bytes 61444
  1063.5 188.7 %reduce-scatter.18.cloned.1.call-start = ((), (), s32[]{:S(2)}) async-start(), calls=%async_computation.18 | async-start | bytes 6553600 | tf_op jit(solution)/shard_map/reduce_scatter | solution.py:273
  1064.2 351.7 %reduce-scatter.20.cloned.1.call-start = ((), (), s32[]{:S(2)}) async-start(), calls=%async_computation.19 | async-start | bytes 6758400 | tf_op jit(solution)/shard_map/reduce_scatter | solution.py:307
  1070.1 88.9 %copy-start.1 = (f32[1,512,20,64]{1,3,2,0:T(8,128)S(1)}, f32[1,512,20,64]{1,3,2,0:T(8,128)}, u32[]{:S(2)}) copy-start(f32[1,512,20,64]{1,3,2,0:T(8,128)} %get-tuple-element.141) | copy-start | bytes 7864324
  1070.1 88.9 %copy-start.40 = (f32[512,20]{0,1:T(8,128)S(1)}, f32[512,20]{0,1:T(8,128)}, u32[]{:S(2)}) copy-start(f32[512,20]{0,1:T(8,128)} %copy-done.39) | copy-start | bytes 122884
  1070.1 507.5 %reduce-scatter.28.cloned.1.call-start = ((), (), s32[]{:S(2)}) async-start(), calls=%async_computation.24 | async-start | bytes 6758400
  1178.0 562.1 %reduce-scatter.30.cloned.1.call-start = ((), (), s32[]{:S(2)}) async-start(), calls=%async_computation.25 | async-start | bytes 6758400
  1192.4 709.0 %reduce-scatter.32.cloned.1.call-start = ((), (), s32[]{:S(2)}) async-start(), calls=%async_computation.26 | async-start | bytes 6758400
  1266.2 1197.7 %reduce-scatter.24.cloned.1.call-start = ((), (), s32[]{:S(2)}) async-start(), calls=%async_computation.21 | async-start | bytes 27033600 | tf_op jit(solution)/shard_map/reduce_scatter | solution.py:192
  1284.0 1741.5 %reduce-scatter.22.cloned.1.call-start = ((), (), s32[]{:S(2)}) async-start(), calls=%async_computation.20 | async-start | bytes 27033600 | tf_op jit(solution)/shard_map/reduce_scatter | solution.py:191
  1299.4 2287.6 %reduce-scatter.26.cloned.1.call-start = ((), (), s32[]{:S(2)}) async-start(), calls=%async_computation.22 | async-start | bytes 27033600 | tf_op jit(solution)/shard_map/reduce_scatter | solution.py:193
  (83 other events, 1044.9 us)
Sparse Core Ops, SparseCore 0:
  10.8 62.0 all-gather.16
  75.7 58.1 all-gather.14
  136.8 58.2 all-gather.10
  196.5 97.9 all-gather.26
  296.5 96.4 all-gather.12
  395.6 57.6 all-gather.18
  456.2 97.3 all-gather.22
  556.4 96.6 all-gather.20
  656.0 96.6 all-gather.24
  1063.6 91.9 reduce-scatter.15
  1157.9 94.2 reduce-scatter.17
  1254.9 160.9 reduce-scatter.19
  1418.8 158.8 reduce-scatter.27
  1580.4 159.7 reduce-scatter.29
  1742.9 158.5 reduce-scatter.31
  1904.2 559.6 reduce-scatter.23
  2466.7 558.7 reduce-scatter.21
  3028.2 558.7 reduce-scatter.25
where the time goes:
time: 3600 us
  waiting for transfers between devices  2780 us (77%)
  matrix products  472 us (13%)
  blocking collectives  125 us (3%)
  local copies, waits for them, and re-layouts  118 us (3%)
  other arithmetic  70.9 us (2%)
    reduce_scatter x1, waiting for transfers between devices, per_device(): lax.psum_scatter(grad_gate, ('dp', 'ctx'), scatter_dimension=0, tiled=True)  562 us
    reduce_scatter x1, waiting for transfers between devices, per_device(): lax.psum_scatter(grad_down, ('dp', 'ctx'), scatter_dimension=0, tiled=True)  562 us
    reduce_scatter x1, waiting for transfers between devices, per_device(): lax.psum_scatter(grad_up, ('dp', 'ctx'), scatter_dimension=0, tiled=True)  562 us
    unnamed x21, waiting for transfers between devices  491 us
    all_gather x1, waiting for transfers between devices, per_device(): key_piece = lax.all_gather(k_flat, 'ctx', axis=1, tiled=True)  90.5 us
    psum x2, blocking collectives, per_device(): err_total, count = lax.psum((err_local, count_local), ('dp', 'ctx'))  85.7 us
    reduce_scatter x1, waiting for transfers between devices, per_device(): lax.psum_scatter(d_key_all.astype(jnp.bfloat16), 'ctx', scatter_dimension...  85.2 us
    all_gather x1, waiting for transfers between devices, per_device(): lax.all_gather(down_weight, ('dp', 'ctx'), axis=0, tiled=True)  81.9 us
  transfers between devices with their start and end apart: 18, of which 16 were waited for; matrix products, arithmetic and copies ran while one was open for 9% of the time, Pallas kernels for 0%

commit v1 on v0

--- a/solution.py
+++ b/solution.py
@@ -1,6 +1,10 @@
+import functools
+
 import jax
 import jax.numpy as jnp
 from jax import lax
+from jax.experimental import pallas as pl
+from jax.experimental.pallas import tpu as pltpu
 from jax.sharding import PartitionSpec as P
 
 HD = 64
@@ -43,6 +47,513 @@
         key_pos[None, None, :] < lens[:, None, None]
     )
     return (scores, allowed[:, None])
+
+
+BLK = 512
+LANES = 128
+
+
+def head_cols(ref, rows, offset):
+    base = offset // LANES * LANES
+    pair = ref[rows, base : base + LANES]
+    return pair[:, offset - base : offset - base + HD]
+
+
+def split3(v):
+    hi = v.astype(jnp.bfloat16)
+    rest = v - hi.astype(jnp.float32)
+    mid = rest.astype(jnp.bfloat16)
+    low = (rest - mid.astype(jnp.float32)).astype(jnp.bfloat16)
+    return hi, mid, low
+
+
+def attend_kernel(heads, length_ref, qkv_ref, gain_ref, mixed_ref, low_ref, qa_ref, ka_ref, va_ref, out_ref):
+    tokens = qkv_ref.shape[0]
+    width = heads * HD
+    length = length_ref[0]
+    lane = lax.broadcasted_iota(jnp.int32, (BLK, HD), 1)
+
+    def prepare(block, carry):
+        start = pl.multiple_of(block * BLK, BLK)
+        rows = pl.ds(start, BLK)
+        inside = (lax.broadcasted_iota(jnp.int32, (BLK, 1), 0) + start < length).astype(jnp.float32)
+        ones = jnp.where(lane < 3, inside, 0.0).astype(jnp.bfloat16)
+        nothing = jnp.zeros((BLK, HD), jnp.bfloat16)
+        for head in range(heads):
+            gain = gain_ref[:, head * HD : (head + 1) * HD]
+            q = head_cols(qkv_ref, rows, head * HD)
+            k = head_cols(qkv_ref, rows, width + head * HD)
+            v = head_cols(qkv_ref, rows, 2 * width + head * HD)
+            qn = q * lax.rsqrt(jnp.mean(q * q, axis=-1, keepdims=True) + eps)
+            kn = k * lax.rsqrt(jnp.mean(k * k, axis=-1, keepdims=True) + eps)
+            qs = (gain * qn).astype(jnp.bfloat16) * jnp.bfloat16(HD**-0.5)
+            ks = (gain * kn * inside).astype(jnp.bfloat16)
+            vs = (v * inside).astype(jnp.bfloat16)
+            qa_ref[head, rows, :] = jnp.concatenate([qs, nothing], axis=1)
+            ka_ref[head, rows, :] = jnp.concatenate([ks, ones], axis=1)
+            va_ref[head, rows, :] = jnp.concatenate([vs, ones], axis=1)
+        return carry
+
+    lax.fori_loop(0, tokens // BLK, prepare, 0)
+    causal = lax.broadcasted_iota(jnp.int32, (BLK, BLK), 1) <= lax.broadcasted_iota(jnp.int32, (BLK, BLK), 0)
+
+    def per_head(head, carry):
+        for qi in range(tokens // BLK):
+            rows = pl.ds(qi * BLK, BLK)
+            q = qa_ref[head, rows, :]
+            acc = jnp.zeros((BLK, LANES), jnp.float32)
+            for ki in range(qi + 1):
+                keys = pl.ds(ki * BLK, BLK)
+                scores = lax.dot_general(
+                    q, ka_ref[head, keys, :], (((1,), (1,)), ((), ())), preferred_element_type=jnp.float32
+                )
+                weights = jnp.exp(scores)
+                if ki == qi:
+                    weights = jnp.where(causal, weights, 0.0)
+                acc = acc + jnp.dot(
+                    weights.astype(jnp.bfloat16), va_ref[head, keys, :], preferred_element_type=jnp.float32
+                )
+            total = acc[:, HD : HD + 1]
+            out_ref[head, rows, :] = acc / total
+            hi, mid, low = split3(-jnp.log(total))
+            extra = jnp.where(lane == 0, hi, jnp.where(lane == 1, mid, jnp.where(lane == 2, low, jnp.zeros_like(low))))
+            qa_ref[head, rows, :] = jnp.concatenate([q[:, :HD], extra], axis=1)
+        return carry
+
+    lax.fori_loop(0, heads, per_head, 0)
+
+    def finish(block, carry):
+        rows = pl.ds(pl.multiple_of(block * BLK, BLK), BLK)
+        whole = jnp.concatenate([out_ref[head, rows, :][:, :HD] for head in range(heads)], axis=1)
+        mixed_ref[rows, :] = whole
+        low_ref[rows, :] = whole.astype(jnp.bfloat16)
+        return carry
+
+    lax.fori_loop(0, tokens // BLK, finish, 0)
+
+
+def attend(qkv, gain, length):
+    tokens, three = qkv.shape
+    width = three // 3
+    heads = width // HD
+    vmem = pl.BlockSpec(memory_space=pltpu.VMEM)
+    aug = jax.ShapeDtypeStruct((heads, tokens, LANES), jnp.bfloat16)
+    return pl.pallas_call(
+        functools.partial(attend_kernel, heads),
+        out_shape=(
+            jax.ShapeDtypeStruct((tokens, width), jnp.float32),
+            jax.ShapeDtypeStruct((tokens, width), jnp.bfloat16),
+            aug,
+            aug,
+            aug,
+        ),
+        in_specs=[pl.BlockSpec(memory_space=pltpu.SMEM), vmem, vmem],
+        out_specs=(vmem,) * 5,
+        scratch_shapes=[pltpu.VMEM((heads, tokens, LANES), jnp.float32)],
+        compiler_params=pltpu.CompilerParams(vmem_limit_bytes=56 << 20),
+        cost_estimate=pl.CostEstimate(
+            flops=16 * heads * tokens * tokens * HD // 2, bytes_accessed=24 << 20, transcendentals=heads * tokens * tokens // 2
+        ),
+        name="attend",
+    )(length, qkv, gain)
+
+
+def attend_back_kernel(
+    heads, length_ref, qkv_ref, gain_ref, mixed_ref, cot_ref, qa_ref, ka_ref, va_ref,
+    grads_ref, gain_grad_ref, doa_ref, dq_ref, dk_ref, dv_ref,
+):
+    tokens = qkv_ref.shape[0]
+    width = heads * HD
+    length = length_ref[0]
+    lane = lax.broadcasted_iota(jnp.int32, (BLK, HD), 1)
+
+    def prepare(block, carry):
+        rows = pl.ds(pl.multiple_of(block * BLK, BLK), BLK)
+        for head in range(heads):
+            d_mixed = head_cols(cot_ref, rows, head * HD)
+            mixed = head_cols(mixed_ref, rows, head * HD)
+            delta = jnp.sum(d_mixed.astype(jnp.float32) * mixed, axis=-1, keepdims=True)
+            hi, mid, low = split3(-delta)
+            extra = jnp.where(lane == 0, hi, jnp.where(lane == 1, mid, jnp.where(lane == 2, low, jnp.zeros_like(low))))
+            doa_ref[head, rows, :] = jnp.concatenate([d_mixed, extra], axis=1)
+        return carry
+
+    lax.fori_loop(0, tokens // BLK, prepare, 0)
+    causal = lax.broadcasted_iota(jnp.int32, (BLK, BLK), 0) <= lax.broadcasted_iota(jnp.int32, (BLK, BLK), 1)
+
+    def per_head(head, carry):
+        for ki in range(tokens // BLK):
+            keys = pl.ds(ki * BLK, BLK)
+            k = ka_ref[head, keys, :]
+            v = va_ref[head, keys, :]
+            dk = jnp.zeros((BLK, LANES), jnp.float32)
+            dv = jnp.zeros((BLK, LANES), jnp.float32)
+            for qi in range(ki, tokens // BLK):
+                rows = pl.ds(qi * BLK, BLK)
+                q = qa_ref[head, rows, :]
+                d_out = doa_ref[head, rows, :]
+                scores = lax.dot_general(k, q, (((1,), (1,)), ((), ())), preferred_element_type=jnp.float32)
+                probs = jnp.exp(scores)
+                if ki == qi:
+                    probs = jnp.where(causal, probs, 0.0)
+                d_probs = lax.dot_general(v, d_out, (((1,), (1,)), ((), ())), preferred_element_type=jnp.float32)
+                d_scores = (probs * d_probs).astype(jnp.bfloat16)
+                dv = dv + jnp.dot(probs.astype(jnp.bfloat16), d_out, preferred_element_type=jnp.float32)
+                dk = dk + jnp.dot(d_scores, q, preferred_element_type=jnp.float32)
+                dq = lax.dot_general(d_scores, k, (((0,), (0,)), ((), ())), preferred_element_type=jnp.float32)
+                if ki == 0:
+                    dq_ref[head, rows, :] = dq
+                else:
+                    dq_ref[head, rows, :] += dq
+            dk_ref[head, keys, :] = dk
+            dv_ref[head, keys, :] = dv
+        return carry
+
+    lax.fori_loop(0, heads, per_head, 0)
+
+    def finish(block, sums):
+        start = pl.multiple_of(block * BLK, BLK)
+        rows = pl.ds(start, BLK)
+        inside = lax.broadcasted_iota(jnp.int32, (BLK, 1), 0) + start < length
+        dqs, dks, dvs, sums_new = [], [], [], []
+        for head in range(heads):
+            gain = gain_ref[:, head * HD : (head + 1) * HD]
+            part = sums[head]
+            for offset, ref, outs, scale in ((0, dq_ref, dqs, HD**-0.5), (width, dk_ref, dks, 1.0)):
+                raw = head_cols(qkv_ref, rows, offset + head * HD)
+                factor = lax.rsqrt(jnp.mean(raw * raw, axis=-1, keepdims=True) + eps)
+                normed = raw * factor
+                grad = ref[head, rows, :][:, :HD] * scale
+                part = part + jnp.sum(grad * normed, axis=0, keepdims=True)
+                scaled = grad * gain
+                outs.append(
+                    (factor * (scaled - normed * jnp.mean(scaled * normed, axis=-1, keepdims=True))).astype(jnp.bfloat16)
+                )
+            dvs.append(jnp.where(inside, dv_ref[head, rows, :][:, :HD], 0.0).astype(jnp.bfloat16))
+            sums_new.append(part)
+        grads_ref[rows, :] = jnp.concatenate(dqs + dks + dvs, axis=1)
+        return tuple(sums_new)
+
+    sums = lax.fori_loop(
+        0, tokens // BLK, finish, tuple(jnp.zeros((1, HD), jnp.float32) for _ in range(heads))
+    )
+    gain_grad_ref[...] = jnp.concatenate(sums, axis=1)
+
+
+def attend_back(qkv, gain, length, mixed, d_mixed, qa, ka, va):
+    tokens, three = qkv.shape
+    width = three // 3
+    heads = width // HD
+    vmem = pl.BlockSpec(memory_space=pltpu.VMEM)
+    aug = pltpu.VMEM((heads, tokens, LANES), jnp.float32)
+    return pl.pallas_call(
+        functools.partial(attend_back_kernel, heads),
+        out_shape=(
+            jax.ShapeDtypeStruct((tokens, three), jnp.bfloat16),
+            jax.ShapeDtypeStruct((1, width), jnp.float32),
+        ),
+        in_specs=[pl.BlockSpec(memory_space=pltpu.SMEM)] + [vmem] * 7,
+        out_specs=(vmem,) * 2,
+        scratch_shapes=[pltpu.VMEM((heads, tokens, LANES), jnp.bfloat16), aug, aug, aug],
+        compiler_params=pltpu.CompilerParams(vmem_limit_bytes=60 << 20),
+        cost_estimate=pl.CostEstimate(
+            flops=40 * heads * tokens * tokens * HD // 2, bytes_accessed=24 << 20, transcendentals=heads * tokens * tokens // 2
+        ),
+        name="attend_back",
+    )(length, qkv, gain, mixed, d_mixed, qa, ka, va)
+
+
+CORE, XAX, YAX = 1, 2, 4
+
+
+def swap_dp(v, bit):
+    return lax.ppermute(v, "dp", [(i, i ^ bit) for i in range(8)])
+
+
+def swap_z(v, mask):
+    return lax.ppermute(v, "ctx", [(i, i ^ mask) for i in range(4)])
+
+
+def pick(v, index, axis=0):
+    return lax.dynamic_index_in_dim(v, index, axis, keepdims=False)
+
+
+def gather_z(shard):
+    far = swap_z(shard, 2)
+    return {0: shard, 1: swap_z(shard, 1), 2: far, 3: swap_z(far, 1)}
+
+
+def gather_chips(shard, flip):
+    pieces = {}
+    for mz, piece in gather_z(shard).items():
+        y_first = (mz % 2 == 0) != flip
+        first, second = (YAX, XAX) if y_first else (XAX, YAX)
+        across = swap_dp(piece, first)
+        for key, value in (
+            (0, piece),
+            (first, across),
+            (second, swap_dp(piece, second)),
+            (first | second, swap_dp(across, second)),
+        ):
+            pieces[(key // YAX, key // XAX % 2, mz)] = value
+    return pieces
+
+
+def assemble(pieces, coords, shape, place):
+    keys = sorted(pieces)
+
+    def kernel(coord_ref, *refs):
+        out_ref, sems = refs[len(keys)], refs[len(keys) + 1]
+        copies = []
+        for at, key in enumerate(keys):
+            where = place(*[jnp.bitwise_xor(coord_ref[d], key[d]) for d in range(len(key))])
+            copies.append(pltpu.make_async_copy(refs[at], out_ref.at[where], sems.at[at]))
+        for copy in copies:
+            copy.start()
+        for copy in copies:
+            copy.wait()
+
+    some = pieces[keys[0]]
+    return pl.pallas_call(
+        kernel,
+        out_shape=jax.ShapeDtypeStruct(shape, some.dtype),
+        in_specs=[pl.BlockSpec(memory_space=pltpu.SMEM)] + [pl.BlockSpec(memory_space=pl.ANY)] * len(keys),
+        out_specs=pl.BlockSpec(memory_space=pltpu.VMEM),
+        scratch_shapes=[pltpu.SemaphoreType.DMA((len(keys),))],
+        compiler_params=pltpu.CompilerParams(vmem_limit_bytes=40 << 20),
+        cost_estimate=pl.CostEstimate(flops=0, bytes_accessed=2 * len(keys) * some.size * some.dtype.itemsize, transcendentals=0),
+        name="assemble",
+    )(coords, *[pieces[key] for key in keys])
+
+
+def add_low(a, b):
+    return (a.astype(jnp.float32) + b.astype(jnp.float32)).astype(jnp.bfloat16)
+
+
+def reduce_z(parts, z):
+    relay = swap_z(pick(parts, z ^ 3), 1)
+    far = add_low(pick(parts, z ^ 2), relay)
+    near = swap_z(pick(parts, z ^ 1), 1)
+    far = swap_z(far, 2)
+    return pick(parts, z).astype(jnp.float32) + near.astype(jnp.float32) + far.astype(jnp.float32)
+
+
+def reduce_xy(parts, x, y, x_first):
+    if x_first:
+        half = add_low(pick(parts, x, 1), swap_dp(pick(parts, 1 - x, 1), XAX))
+        return add_low(pick(half, y), swap_dp(pick(half, 1 - y), YAX))
+    half = add_low(pick(parts, y), swap_dp(pick(parts, 1 - y), YAX))
+    return add_low(pick(half, x), swap_dp(pick(half, 1 - x), XAX))
+
+
+def by_core(c, own, other, axis=0):
+    return jnp.where(c == 0, jnp.stack([own, other], axis), jnp.stack([other, own], axis))
+
+
+def on_cores(
+    inputs,
+    teacher,
+    lengths,
+    query_weight,
+    key_weight,
+    value_projection,
+    output_weight,
+    score_gain,
+    attention_step,
+    up_weight,
+    gate_weight,
+    down_weight,
+    up_scale,
+    gate_scale,
+    swiglu_step,
+):
+    local, width = inputs.shape[1:]
+    share = query_weight.shape[0]
+    hidden_share = down_weight.shape[0]
+    heads_width = width // 4
+    tokens = local * 4
+    low = jnp.bfloat16
+    f32 = jnp.float32
+    dp, z = lax.axis_index("dp"), lax.axis_index("ctx")
+    c, x, y = dp % 2, dp // 2 % 2, dp // 4
+    chip = jnp.stack([y, x, z]).astype(jnp.int32)
+    line = z.astype(jnp.int32).reshape(1)
+    states = inputs.reshape(local, width)
+
+    shards = jnp.stack([query_weight, key_weight, value_projection], 1).reshape(share, 3, 4, heads_width)
+    shards = shards.transpose(2, 0, 1, 3).reshape(4, share, 3 * heads_width)
+    pieces = {(m,): swap_z(pick(shards, z ^ m), m) if m else pick(shards, z) for m in range(4)}
+    rows_qkv = assemble(pieces, line, (4, share, 3 * heads_width), lambda zz: (zz,)).reshape(2, 2 * share, 3 * heads_width)
+    pieces = {}
+    for half, (first, second) in enumerate(((XAX, YAX), (YAX, XAX))):
+        piece = rows_qkv[half]
+        across = swap_dp(piece, first)
+        for key, value in ((0, piece), (first, across), (second, swap_dp(piece, second)), (first | second, swap_dp(across, second))):
+            for core in (0, 1):
+                pieces[(key // YAX, key // XAX % 2, core, half)] = swap_dp(value, CORE) if core else value
+    full_qkv = assemble(
+        pieces,
+        jnp.stack([y, x, c, jnp.zeros_like(c)]).astype(jnp.int32),
+        (2, 2, 2, 2, 2 * share, 3 * heads_width),
+        lambda yy, xx, cc, half: (yy, xx, cc, half),
+    ).reshape(width, 3 * heads_width)
+
+    whole_states = assemble(
+        {(m,): piece for m, piece in gather_z(states).items()}, line, (4, local, width), lambda zz: (zz,)
+    ).reshape(tokens, width)
+
+    length_parts = jnp.stack([lengths[0] // 64, lengths[0] % 64]).astype(low)
+    small = jnp.concatenate([score_gain, attention_step, up_scale, gate_scale, swiglu_step, length_parts])
+    small = jnp.pad(small, (0, width - small.shape[0])).reshape(1, width)
+    misc_rows = share + 8
+    misc = jnp.concatenate([output_weight, small, jnp.zeros((7, width), low)], 0)
+    misc = assemble(gather_chips(misc, False), chip, (2, 2, 4, misc_rows, width), lambda yy, xx, zz: (yy, xx, zz))
+    misc = by_core(c, misc, swap_dp(misc, CORE), 2)
+    full_output = misc[:, :, :, :, :share].reshape(width, width)
+    vectors = misc[:, :, :, :, share]
+    cuts = [0]
+    for size in (share, share, hidden_share, hidden_share, share, 2):
+        cuts.append(cuts[-1] + size)
+    full_gain, full_astep, full_uscale, full_gscale, full_mstep, full_lengths = (
+        vectors[..., a:b].astype(f32) for a, b in zip(cuts[:-1], cuts[1:])
+    )
+    count = jnp.sum(full_lengths[:, :, :, 0] * jnp.array([64.0, 1.0], f32))
+    astep = full_astep.reshape(width)
+    mstep = full_mstep.reshape(width)
+    scale_up = pick(full_uscale, c, 2).reshape(-1)
+    scale_gate = pick(full_gscale, c, 2).reshape(-1)
+    gain = pick(full_gain.reshape(4, 1, heads_width), z)
+
+    def halves(weight):
+        cut = weight.reshape(share, 4, 2, hidden_share * 4)
+        return cut[:, :, 0].reshape(share, -1), cut[:, :, 1].reshape(share, -1)
+
+    up_halves, gate_halves = halves(up_weight), halves(gate_weight)
+    half0 = jnp.concatenate([up_halves[0], gate_halves[0]], 1)
+    half1 = jnp.concatenate([up_halves[1], gate_halves[1]], 1)
+    own, other = jnp.where(c == 0, half0, half1), jnp.where(c == 0, half1, half0)
+    shard = by_core(c, own, swap_dp(other, CORE))
+    wide = half0.shape[1]
+    hidden_half = wide // 2
+    full_wide = assemble(
+        gather_chips(shard, False), chip, (2, 2, 2, 4, share, wide), lambda yy, xx, zz: (yy, xx, slice(None), zz)
+    ).reshape(width, wide)
+    full_down = assemble(
+        gather_chips(down_weight, True), chip, (2, 2, 4, hidden_share, width), lambda yy, xx, zz: (yy, xx, zz)
+    ).reshape(hidden_half, width)
+
+    qkv = matmul(whole_states, full_qkv)
+    mixed, mixed_heads, qa, ka, va = attend(qkv, gain, lengths)
+    blocks = mixed_heads.reshape(4, local, heads_width)
+    pieces = {(m,): swap_z(pick(blocks, z ^ m), m) if m else pick(blocks, z) for m in range(4)}
+    mixed_low = assemble(pieces, line, (4, local, heads_width), lambda zz: (zz,)).transpose(1, 0, 2).reshape(local, width)
+    branch = matmul(mixed_low, full_output)
+    resid = states.astype(f32)
+    branch_norm = normalize(branch)
+    first = resid + astep * (branch_norm - resid)
+    middle = normalize(first)
+
+    middle_low = middle.astype(low)
+    middle_both = jnp.concatenate([middle_low, swap_dp(middle_low, CORE)], 0)
+    both = matmul(middle_both, full_wide)
+    upper, gating = both[:, :hidden_half], both[:, hidden_half:]
+    upper_scaled = upper * scale_up
+    gate_arg = gating * scale_gate
+    gate_act = jax.nn.silu(gate_arg)
+    hidden = (upper_scaled * gate_act).astype(low)
+    lower = matmul(hidden, full_down)
+    lower = lower[:local] + swap_dp(lower[local:], CORE)
+    lower_norm = normalize(lower)
+    second = middle + mstep * (lower_norm - middle)
+    final = normalize(second)
+
+    query_pos = z * local + jnp.arange(local, dtype=jnp.int32)
+    valid = (query_pos < lengths[0]).astype(f32).reshape(local, 1)
+    diff = final - teacher.reshape(local, width).astype(f32)
+    err_local = jnp.sum(valid * diff * diff)
+    cot = loss_scale * 2.0 / count * valid * diff
+
+    d_second = norm_back(second, final, cot)
+    d_middle = d_second * (1.0 - mstep)
+    grad_mstep = jnp.sum(d_second * (lower_norm - middle), axis=0)
+    d_lower = norm_back(lower, lower_norm, d_second * mstep).astype(low)
+    d_lower_both = jnp.concatenate([d_lower, swap_dp(d_lower, CORE)], 0)
+    grad_down = left_tdot(hidden, d_lower_both).astype(low).reshape(2, 2, 4, 2, hidden_share // 2, width)
+    down_grad = jnp.concatenate(
+        [reduce_z(reduce_xy(grad_down[:, :, :, part], x, y, part == 0), z) for part in range(2)], 0
+    )
+    d_hidden = right_tdot(d_lower_both, full_down)
+    d_upper = d_hidden * gate_act
+    sigmoid_gate = jax.nn.sigmoid(gate_arg)
+    d_gate_arg = d_hidden * upper_scaled * (sigmoid_gate * (1.0 + gate_arg * (1.0 - sigmoid_gate)))
+    grad_uscale = jnp.sum(d_upper * upper, axis=0)
+    grad_gscale = jnp.sum(d_gate_arg * gating, axis=0)
+    d_wide = jnp.concatenate([(d_upper * scale_up).astype(low), (d_gate_arg * scale_gate).astype(low)], 1)
+    grad_wide = left_tdot(middle_both, d_wide).astype(low).reshape(2, 2, 2, 4, share, wide)
+    wide_rows = [reduce_z(reduce_xy(grad_wide[:, :, core], x, y, core == 0), z) for core in range(2)]
+    own = jnp.where(c == 0, wide_rows[0], wide_rows[1])
+    other = swap_dp(jnp.where(c == 0, wide_rows[1], wide_rows[0]), CORE)
+    wide_grad = by_core(c, own.reshape(share, 2, 4, -1), other.reshape(share, 2, 4, -1), 3)
+    up_grad = wide_grad[:, 0].reshape(up_weight.shape)
+    gate_grad = wide_grad[:, 1].reshape(up_weight.shape)
+    d_both = right_tdot(d_wide, full_wide)
+    d_middle = d_middle + d_both[:local] + swap_dp(d_both[local:], CORE)
+
+    d_first = norm_back(first, middle, d_middle)
+    input_grad = d_first * (1.0 - astep)
+    grad_astep = jnp.sum(d_first * (branch_norm - resid), axis=0)
+    d_branch = norm_back(branch, branch_norm, d_first * astep).astype(low)
+    d_mixed = right_tdot(d_branch, full_output).astype(low)
+    blocks = d_mixed.reshape(local, 4, heads_width).transpose(1, 0, 2)
+    pieces = {(m,): swap_z(pick(blocks, z ^ m), m) if m else pick(blocks, z) for m in range(4)}
+    d_mixed = assemble(pieces, line, (4, local, heads_width), lambda zz: (zz,)).reshape(tokens, heads_width)
+    grad_output = left_tdot(mixed_low, d_branch).astype(low).reshape(2, 2, 2, 4, share, width)
+    grad_output = add_low(pick(grad_output, c, 2), swap_dp(pick(grad_output, 1 - c, 2), CORE))
+    output_grad = reduce_z(reduce_xy(grad_output, x, y, True), z)
+    d_qkv, grad_gain = attend_back(qkv, gain, lengths, mixed, d_mixed, qa, ka, va)
+    d_states = right_tdot(d_qkv, full_qkv).astype(low).reshape(4, local, width)
+    input_grad = input_grad + reduce_z(d_states, z)
+    grad_qkv = left_tdot(whole_states, d_qkv).astype(low).reshape(2, 2, 2, 2, 2 * share, 3 * heads_width)
+    grad_qkv = add_low(pick(grad_qkv, c, 2), swap_dp(pick(grad_qkv, 1 - c, 2), CORE))
+    rows_qkv = jnp.stack([reduce_xy(grad_qkv[:, :, half], x, y, half == 0) for half in range(2)])
+    rows_qkv = rows_qkv.reshape(4, share, 3 * heads_width)
+    pieces = {(m,): swap_z(pick(rows_qkv, z ^ m), m) if m else pick(rows_qkv, z) for m in range(4)}
+    columns = assemble(pieces, line, (4, share, 3 * heads_width), lambda zz: (zz,))
+    columns = columns.reshape(4, share, 3, heads_width).transpose(2, 1, 0, 3).reshape(3, share, width).astype(f32)
+
+    gain_all = lax.dynamic_update_slice(jnp.zeros((4, heads_width), f32), grad_gain, (z, 0)).reshape(32, share)
+    scales = jnp.concatenate([grad_uscale.reshape(2, 2, 4, hidden_share), grad_gscale.reshape(2, 2, 4, hidden_share)], -1)
+    scales = jnp.where((jnp.arange(2) == c)[None, None, :, None, None], scales[:, :, None], 0.0).reshape(32, -1)
+    packed = jnp.concatenate(
+        [gain_all, grad_astep.reshape(32, share), scales, grad_mstep.reshape(32, share), jnp.full((32, 1), err_local)], 1
+    )
+    packed = jnp.pad(packed, ((0, 0), (0, 512 - packed.shape[1]))).reshape(2, 2, 2, 4, 4, 128)
+    packed = pick(packed, c, 2) + swap_dp(pick(packed, 1 - c, 2), CORE)
+    packed = pick(packed, x, 1) + swap_dp(pick(packed, 1 - x, 1), XAX)
+    packed = pick(packed, y) + swap_dp(pick(packed, 1 - y), YAX)
+    packed = (
+        pick(packed, z)
+        + swap_z(pick(packed, z ^ 1), 1)
+        + swap_z(pick(packed, z ^ 2), 2)
+        + swap_z(pick(packed, z ^ 3), 3)
+    ).reshape(512)
+    return (
+        final.astype(low)[None],
+        packed[cuts[5]] / count,
+        input_grad[None],
+        columns[0],
+        columns[1],
+        columns[2],
+        output_grad,
+        packed[: cuts[1]],
+        packed[cuts[1] : cuts[2]],
+        up_grad,
+        gate_grad,
+        down_grad,
+        packed[cuts[2] : cuts[3]],
+        packed[cuts[3] : cuts[4]],
+        packed[cuts[4] : cuts[5]],
+    )
 
 
 def per_device(
@@ -347,8 +858,9 @@
         P(("dp", "ctx")),
         P(("dp", "ctx")),
     )
+    on_one = on_cores if dict(mesh.shape) == {"dp": 8, "ctx": 4} else per_device
     return jax.shard_map(
-        per_device,
+        on_one,
         mesh=mesh,
         in_specs=placed,
         out_specs=(

time: 3600 us -> 1060 us (0.29)
  waiting for transfers between devices: 2780 us -> 415 us
  matrix products: 472 us -> 134 us
  starting transfers between devices: 1.33 us -> 156 us
  blocking collectives: 125 us -> 0 us
  Pallas kernels: 0 us -> 123 us
    reduce_scatter x6 -> x0, waiting for transfers between devices: 1870 us -> none  [the longest x1 562 us: per_device(): lax.psum_scatter(grad_gate, ('dp', 'ctx'), scatter_dimension=0, tiled=True)]
    unnamed x21 -> x0, waiting for transfers between devices: 491 us -> none
    all_gather x9 -> x0, waiting for transfers between devices: 421 us -> none  [the longest x1 90.5 us: per_device(): key_piece = lax.all_gather(k_flat, 'ctx', axis=1, tiled=True)]
    ppermute x0 -> x121, waiting for transfers between devices: none -> 415 us  [the longest x76 217 us: swap_dp(): return lax.ppermute(v, 'dp', [(i, i ^ bit) for i in range(8)])]
    dot_general x28 -> x0, matrix products: 279 us -> none  [the longest x8 81.2 us: block_scores(): jnp.einsum('sqhd,skhd->shqk', queries, keys, preferred_element_type=jnp.f...]
    ppermute x0 -> x121, starting transfers between devices: none -> 156 us  [the longest x76 86.7 us: swap_dp(): return lax.ppermute(v, 'dp', [(i, i ^ bit) for i in range(8)])]
    pallas_call x0 -> x11, Pallas kernels: none -> 123 us  [the longest x1 65.1 us: attend_back(): pl.pallas_call(functools.partial(attend_back_kernel, heads), out_shape=(j...]
    psum x2 -> x0, blocking collectives: 85.7 us -> none  [per_device(): err_total, count = lax.psum((err_local, count_local), ('dp', 'ctx'))]
  transfers between devices with their start and end apart: 18 -> 121, of which waited for: 16 -> 42; matrix products, arithmetic and copies ran while one was open for 9% -> 22% of each run, Pallas kernels for 0% -> 12%
where the time goes in v1:
time: 1060 us; the launch traced here: 1050 us
  waiting for transfers between devices  415 us (39%)
  starting transfers between devices  156 us (15%)
  local copies, waits for them, and re-layouts  141 us (13%)
  matrix products  134 us (13%)
  Pallas kernels  123 us (12%)
  other arithmetic  76.9 us (7%)
    ppermute x76, waiting for transfers between devices, swap_dp(): return lax.ppermute(v, 'dp', [(i, i ^ bit) for i in range(8)])  217 us
    ppermute x45, waiting for transfers between devices, swap_z(): return lax.ppermute(v, 'ctx', [(i, i ^ mask) for i in range(4)])  197 us
    ppermute x76, starting transfers between devices, swap_dp(): return lax.ppermute(v, 'dp', [(i, i ^ bit) for i in range(8)])  86.7 us
    ppermute x45, starting transfers between devices, swap_z(): return lax.ppermute(v, 'ctx', [(i, i ^ mask) for i in range(4)])  69.5 us
    pallas_call x1, Pallas kernels, attend_back(): pl.pallas_call(functools.partial(attend_back_kernel, heads), out_shape=(j...  65.1 us
    unnamed x270, local copies, waits for them, and re-layouts  55.5 us
    dot_general x4, matrix products, right_tdot(): lax.dot_general(left, right, (((1,), (1,)), ((), ())), preferred_element_...  49.7 us
    dot_general x4, matrix products, left_tdot(): lax.dot_general(left, right, (((0,), (0,)), ((), ())), preferred_element_...  43.4 us
  transfers between devices with their start and end apart: 121, of which 42 were waited for; matrix products, arithmetic and copies ran while one was open for 22% of the time, Pallas kernels for 12%

profile of v1, /device:TPU:0, one launch (start us, length us, event | category | flops | bytes accessed | tf_op | source)
XLA Modules:
  0.0 1052.8 jit_solution(2451430506863885496)
XLA Ops:
  92.5 14.2 %collective-permute-done.17.refs_2_ = bf16[512,1280]{1,0:T(8,128)(2,1)} collective-permute-done((bf16[512,1280]{1,0:T(8,128)(2,1)S(1)}, bf16[512,1280]{1,0:T(8,128)(2,1)}, u32[]{:S(2)}, u32[]{:S(2)}) %collective-permute-start.17) | collective-permute-done | bytes 1310752 | tf_op jit(solution)/shard_map/ppermute | solution.py:274
  119.0 39.0 %collective-permute-done.57.refs_2_ = bf16[160,1280]{1,0:T(8,128)(2,1)} collective-permute-done((bf16[160,1280]{1,0:T(8,128)(2,1)}, bf16[160,1280]{1,0:T(8,128)(2,1)}, u32[]{:S(2)}, u32[]{:S(2)}) %collective-permute-start.57) | collective-permute-done | bytes 409632 | tf_op jit(solution)/shard_map/ppermute | solution.py:274
  162.0 14.3 %collective-permute-done.18.refs_3_ = bf16[512,1280]{1,0:T(8,128)(2,1)} collective-permute-done((bf16[512,1280]{1,0:T(8,128)(2,1)}, bf16[512,1280]{1,0:T(8,128)(2,1)}, u32[]{:S(2)}, u32[]{:S(2)}) %collective-permute-start.18) | collective-permute-done | bytes 1310752 | tf_op jit(solution)/shard_map/ppermute | solution.py:274
  186.3 11.6 %collective-permute-done.56.refs_1_ = bf16[160,1280]{1,0:T(8,128)(2,1)} collective-permute-done((bf16[160,1280]{1,0:T(8,128)(2,1)}, bf16[160,1280]{1,0:T(8,128)(2,1)}, u32[]{:S(2)}, u32[]{:S(2)}) %collective-permute-start.56) | collective-permute-done | bytes 409632 | tf_op jit(solution)/shard_map/ppermute | solution.py:274
  207.7 34.4 %attend.1 = (f32[2048,320]{1,0:T(8,128)}, bf16[2048,320]{1,0:T(8,128)(2,1)}, bf16[5,2048,128]{2,1,0:T(8,128)(2,1)}, bf16[5,2048,128]{2,1,0:T(8,128)(2,1)}, bf16[5,2048,128]{2,1,0:T(8,128)(2,1)}) custom-call(s32[1]{0:T(128)} %copy.144.length_ref, f32[2048,960]{1,0:T(8,128)} %fusion.77.qkv_ref, f32[1,320]{1,0:T(1,128)} %fusion.57.gain_ref), custom_call_target="tpu_custom_call" | custom-call | flops 10737418240 | bytes 25165824 | tf_op jit(solution)/shard_map/attend/pallas_call | solution.py:141
  248.8 13.1 %collective-permute-done.36.refs_1_ = bf16[512,320]{1,0:T(8,128)(2,1)S(1)} collective-permute-done((bf16[512,320]{1,0:T(8,128)(2,1)S(1)}, bf16[512,320]{1,0:T(8,128)(2,1)S(1)}, u32[]{:S(2)}, u32[]{:S(2)}) %collective-permute-start.36) | collective-permute-done | bytes 327712 | tf_op jit(solution)/shard_map/ppermute | solution.py:274
  261.8 11.8 %collective-permute-done.37.refs_2_ = bf16[512,320]{1,0:T(8,128)(2,1)S(1)} collective-permute-done((bf16[512,320]{1,0:T(8,128)(2,1)S(1)}, bf16[512,320]{1,0:T(8,128)(2,1)S(1)}, u32[]{:S(2)}, u32[]{:S(2)}) %collective-permute-start.37) | collective-permute-done | bytes 327712 | tf_op jit(solution)/shard_map/ppermute | solution.py:274
  332.3 10.3 collective-permute-done.45.refs_5_
  342.6 17.6 %collective-permute-done.46.refs_6_ = bf16[2,40,5120]{2,1,0:T(8,128)(2,1)S(1)} collective-permute-done((bf16[2,40,5120]{2,1,0:T(8,128)(2,1)}, bf16[2,40,5120]{2,1,0:T(8,128)(2,1)S(1)}, u32[]{:S(2)}, u32[]{:S(2)}) %collective-permute-start.46) | collective-permute-done | bytes 819232 | tf_op jit(solution)/shard_map/ppermute | solution.py:270
  363.7 14.0 %collective-permute-done.52.refs_12_ = bf16[2,40,5120]{2,1,0:T(8,128)(2,1)S(1)} collective-permute-done((bf16[2,40,5120]{2,1,0:T(8,128)(2,1)}, bf16[2,40,5120]{2,1,0:T(8,128)(2,1)S(1)}, u32[]{:S(2)}, u32[]{:S(2)}) %collective-permute-start.52) | collective-permute-done | bytes 819232 | tf_op jit(solution)/shard_map/ppermute | solution.py:270
  379.2 16.2 %collective-permute-done.47.refs_7_ = bf16[2,40,5120]{2,1,0:T(8,128)(2,1)} collective-permute-done((bf16[2,40,5120]{2,1,0:T(8,128)(2,1)S(1)}, bf16[2,40,5120]{2,1,0:T(8,128)(2,1)}, u32[]{:S(2)}, u32[]{:S(2)}) %collective-permute-start.47) | collective-permute-done | bytes 819232 | tf_op jit(solution)/shard_map/ppermute | solution.py:270
  422.9 21.6 %fusion.17 = f32[1024,5120]{1,0:T(8,128)} fusion(bf16[1280,5120]{1,0:T(8,128)(2,1)} %bitcast.367, bf16[512,1280]{1,0:T(8,128)(2,1)} %collective-permute-done.39, bf16[512,1280]{1,0:T(8,128)(2,1)} %multiply_convert_fusion.6), kind=kOutput, calls=%fused_computation.72 | convolution fusion | flops 13427015680 | bytes 36700160 | tf_op jit(solution)/shard_map/dot_general | solution.py:27
  497.2 20.8 %multiply_reduce_fusion.1 = (f32[2560]{0:T(1024)S(1)}, f32[2560]{0:T(1024)S(1)}, f32[1024,2560]{1,0:T(8,128)}, bf16[1024,2560]{1,0:T(8,128)(2,1)}) fusion(f32[1024,5120]{1,0:T(8,128)} %fusion.17, f32[2560]{0:T(1024)S(1)} %mul.290, f32[2560]{0:T(1024)S(1)} %mul.287, bf16[2560,1280]{1,0:T(8,128)(2,1)} %bitcast.349, ...), kind=kOutput, calls=%fused_computation.4 | convolution fusion | flops 6765931520 | bytes 45916160 | tf_op jit(solution)/shard_map/dot_general | solution.py:37
  525.7 20.9 %fusion.1 = f32[1024,1280]{1,0:T(8,128)} fusion(bf16[1280,5120]{1,0:T(8,128)(2,1)} %bitcast.368, bf16[1024,2560]{1,0:T(8,128)(2,1)} %multiply_convert_fusion, bf16[1024,2560]{1,0:T(8,128)(2,1)} %get-tuple-element.46), kind=kOutput, calls=%fused_computation.15 | convolution fusion | flops 13442744320 | bytes 28835840 | tf_op jit(solution)/shard_map/dot_general | solution.py:37
  546.6 21.2 %convolution_convert_fusion = bf16[1280,5120]{1,0:T(8,128)(2,1)} fusion(bf16[1024,2560]{1,0:T(8,128)(2,1)} %multiply_convert_fusion, bf16[1024,2560]{1,0:T(8,128)(2,1)} %get-tuple-element.46, bf16[512,1280]{1,0:T(8,128)(2,1)} %collective-permute-done.39, bf16[512,1280]{1,0:T(8,128)(2,1)} %multiply_convert_fusion.6), kind=kOutput, calls=%fused_computation | convolution fusion | flops 13454540800 | bytes 26214400 | tf_op jit(solution)/shard_map/dot_general | solution.py:31
  591.0 75.2 %collective-permute-done.112 = bf16[4,80,1280]{2,1,0:T(8,128)(2,1)S(1)} collective-permute-done((bf16[4,80,1280]{2,1,0:T(8,128)(2,1)S(1)}, bf16[4,80,1280]{2,1,0:T(8,128)(2,1)S(1)}, u32[]{:S(2)}, u32[]{:S(2)}) %collective-permute-start.112) | collective-permute-done | bytes 819232 | tf_op jit(solution)/shard_map/ppermute | solution.py:270
  713.9 21.9 %collective-permute-done.120 = bf16[80,1280]{1,0:T(8,128)(2,1)S(1)} collective-permute-done((bf16[80,1280]{1,0:T(8,128)(2,1)S(1)}, bf16[80,1280]{1,0:T(8,128)(2,1)S(1)}, u32[]{:S(2)}, u32[]{:S(2)}) %collective-permute-start.120) | collective-permute-done | bytes 204832 | tf_op jit(solution)/shard_map/ppermute | solution.py:274
  750.5 65.1 %attend_back.1 = (bf16[2048,960]{1,0:T(8,128)(2,1)}, f32[1,320]{1,0:T(1,128)}) custom-call(s32[1]{0:T(128)} %copy.144.length_ref, f32[2048,960]{1,0:T(8,128)} %fusion.77.qkv_ref, f32[1,320]{1,0:T(1,128)} %fusion.57.gain_ref, f32[2048,320]{1,0:T(8,128)} %get-tuple-element.23.mixed_ref, bf16[2048,320]{1,0:T(8,128)(2,1)} %bitcast.358, ...), custom_call_target="tpu_custom_call" | custom-call | flops 26843545600 | bytes 25165824 | tf_op jit(solution)/shard_map/attend_back/pallas_call | solution.py:249
  817.3 10.6 %convolution_convert_fusion.4 = bf16[1280,960]{0,1:T(8,128)(2,1)} fusion(bf16[2048,1280]{1,0:T(8,128)(2,1)} %bitcast.355, bf16[2048,960]{1,0:T(8,128)(2,1)} %get-tuple-element.28), kind=kOutput, calls=%fused_computation.22 | convolution fusion | flops 5034393600 | bytes 11632640 | tf_op jit(solution)/shard_map/dot_general | solution.py:31
  890.9 21.2 %collective-permute-done.87 = bf16[2,80,960]{2,1,0:T(8,128)(2,1)S(1)} collective-permute-done((bf16[2,80,960]{2,1,0:T(8,128)(2,1)S(1)}, bf16[2,80,960]{2,1,0:T(8,128)(2,1)S(1)}, u32[]{:S(2)}, u32[]{:S(2)}) %collective-permute-start.87) | collective-permute-done | bytes 307232 | tf_op jit(solution)/shard_map/ppermute | solution.py:270
  942.5 16.3 %collective-permute-done.101 = bf16[4,40,5120]{2,1,0:T(8,128)(2,1)} collective-permute-done((bf16[4,40,5120]{2,1,0:T(8,128)(2,1)}, bf16[4,40,5120]{2,1,0:T(8,128)(2,1)}, u32[]{:S(2)}, u32[]{:S(2)}) %collective-permute-start.101) | collective-permute-done | bytes 1638432 | tf_op jit(solution)/shard_map/ppermute | solution.py:270
  966.1 24.4 %collective-permute-start.96 = (bf16[4,40,1280]{2,1,0:T(8,128)(2,1)S(1)}, bf16[4,40,1280]{2,1,0:T(8,128)(2,1)S(1)}, u32[]{:S(2)}, u32[]{:S(2)}) collective-permute-start(bf16[4,40,1280]{2,1,0:T(8,128)(2,1)S(1)} %dynamic-slice_bitcast_fusion.16), channel_id=1, source_target_pairs={{0,16},{4,20},{8,24},{12,28},{16,0},{20,4},{24,8},{28,12},{1,17},{... | collective-permute-start | bytes 1228808 | tf_op jit(solution)/shard_map/ppermute | solution.py:270
  1004.0 13.2 %collective-permute-done.98 = bf16[40,1280]{1,0:T(8,128)(2,1)S(1)} collective-permute-done((bf16[40,1280]{1,0:T(8,128)(2,1)S(1)}, bf16[40,1280]{1,0:T(8,128)(2,1)S(1)}, u32[]{:S(2)}, u32[]{:S(2)}) %collective-permute-start.98) | collective-permute-done | bytes 102432 | tf_op jit(solution)/shard_map/ppermute | solution.py:274
  1018.0 13.5 %collective-permute-done.109 = bf16[40,5120]{1,0:T(8,128)(2,1)S(1)} collective-permute-done((bf16[40,5120]{1,0:T(8,128)(2,1)S(1)}, bf16[40,5120]{1,0:T(8,128)(2,1)S(1)}, u32[]{:S(2)}, u32[]{:S(2)}) %collective-permute-start.109) | collective-permute-done | bytes 409632 | tf_op jit(solution)/shard_map/ppermute | solution.py:274
  (696 shorter events, 503.8 us)
Async XLA Ops:
  50.5 56.1 %collective-permute-start.17 = (bf16[512,1280]{1,0:T(8,128)(2,1)S(1)}, bf16[512,1280]{1,0:T(8,128)(2,1)}, u32[]{:S(2)}, u32[]{:S(2)}) collective-permute-start(bf16[512,1280]{1,0:T(8,128)(2,1)S(1)} %bitcast.345), channel_id=1, source_target_pairs={{0,2},{1,3},{2,0},{3,1},{4,6},{5,7},{6,4},{7,5},{8,10},{9,11},{10,... | collective-permute-start | bytes 3932168 | tf_op jit(solution)/shard_map/ppermute | solution.py:274
  88.3 70.3 %collective-permute-start.16 = (bf16[512,1280]{1,0:T(8,128)(2,1)S(1)}, bf16[512,1280]{1,0:T(8,128)(2,1)}, u32[]{:S(2)}, u32[]{:S(2)}) collective-permute-start(bf16[512,1280]{1,0:T(8,128)(2,1)S(1)} %bitcast.346), channel_id=1, source_target_pairs={{0,1},{1,0},{2,3},{3,2},{4,5},{5,4},{6,7},{7,6},{8,9},{9,8},{10,11... | collective-permute-start | bytes 3932168 | tf_op jit(solution)/shard_map/ppermute | solution.py:274
  106.6 69.7 %collective-permute-start.18 = (bf16[512,1280]{1,0:T(8,128)(2,1)}, bf16[512,1280]{1,0:T(8,128)(2,1)}, u32[]{:S(2)}, u32[]{:S(2)}) collective-permute-start(bf16[512,1280]{1,0:T(8,128)(2,1)} %collective-permute-done.17.refs_2_), channel_id=1, source_target_pairs={{0,1},{1,0},{2,3},{3,2},{4,5},{5,4},{6,7},{7,6},{8,9},{9,8},{10,11... | collective-permute-start | bytes 3932168 | tf_op jit(solution)/shard_map/ppermute | solution.py:274
  107.6 50.4 %collective-permute-start.57 = (bf16[160,1280]{1,0:T(8,128)(2,1)}, bf16[160,1280]{1,0:T(8,128)(2,1)}, u32[]{:S(2)}, u32[]{:S(2)}) collective-permute-start(bf16[160,1280]{1,0:T(8,128)(2,1)} %refs_0_.1), channel_id=1, source_target_pairs={{0,2},{1,3},{2,0},{3,1},{4,6},{5,7},{6,4},{7,5},{8,10},{9,11},{10,... | collective-permute-start | bytes 1228808 | tf_op jit(solution)/shard_map/ppermute | solution.py:274
  109.0 88.9 %collective-permute-start.56 = (bf16[160,1280]{1,0:T(8,128)(2,1)}, bf16[160,1280]{1,0:T(8,128)(2,1)}, u32[]{:S(2)}, u32[]{:S(2)}) collective-permute-start(bf16[160,1280]{1,0:T(8,128)(2,1)} %refs_0_.1), channel_id=1, source_target_pairs={{0,1},{1,0},{2,3},{3,2},{4,5},{5,4},{6,7},{7,6},{8,9},{9,8},{10,11... | collective-permute-start | bytes 1228808 | tf_op jit(solution)/shard_map/ppermute | solution.py:274
  112.3 86.6 %collective-permute-start.59 = (bf16[160,1280]{1,0:T(8,128)(2,1)}, bf16[160,1280]{1,0:T(8,128)(2,1)}, u32[]{:S(2)}, u32[]{:S(2)}) collective-permute-start(bf16[160,1280]{1,0:T(8,128)(2,1)} %refs_0_.1), channel_id=1, source_target_pairs={{0,8},{4,12},{8,0},{12,4},{16,24},{20,28},{24,16},{28,20},{1,9},{5... | collective-permute-start | bytes 1228808 | tf_op jit(solution)/shard_map/ppermute | solution.py:270
  158.6 125.4 %collective-permute-start.42 = (bf16[2,40,5120]{2,1,0:T(8,128)(2,1)}, bf16[2,40,5120]{2,1,0:T(8,128)(2,1)}, u32[]{:S(2)}, u32[]{:S(2)}) collective-permute-start(bf16[2,40,5120]{2,1,0:T(8,128)(2,1)} %maximum_select_fusion.2.refs_0_), channel_id=1, source_target_pairs={{0,2},{1,3},{2,0},{3,1},{4,6},{5,7},{6,4},{7,5},{8,10},{9,11},{10,... | collective-permute-start | bytes 2457608 | tf_op jit(solution)/shard_map/ppermute | solution.py:274
  197.8 45.8 %collective-permute-start.61 = (bf16[160,1280]{1,0:T(8,128)(2,1)}, bf16[160,1280]{1,0:T(8,128)(2,1)S(1)}, u32[]{:S(2)}, u32[]{:S(2)}) collective-permute-start(bf16[160,1280]{1,0:T(8,128)(2,1)} %collective-permute-done.57.refs_2_), channel_id=1, source_target_pairs={{0,8},{4,12},{8,0},{12,4},{16,24},{20,28},{24,16},{28,20},{1,9},{5... | collective-permute-start | bytes 1228808 | tf_op jit(solution)/shard_map/ppermute | solution.py:270
  199.0 46.9 %collective-permute-start.65 = (bf16[160,1280]{1,0:T(8,128)(2,1)}, bf16[160,1280]{1,0:T(8,128)(2,1)S(1)}, u32[]{:S(2)}, u32[]{:S(2)}) collective-permute-start(bf16[160,1280]{1,0:T(8,128)(2,1)} %collective-permute-done.57.refs_2_), channel_id=1, source_target_pairs={{0,16},{4,20},{8,24},{12,28},{16,0},{20,4},{24,8},{28,12},{1,17},{... | collective-permute-start | bytes 1228808 | tf_op jit(solution)/shard_map/ppermute | solution.py:270
  325.6 52.1 %collective-permute-start.52 = (bf16[2,40,5120]{2,1,0:T(8,128)(2,1)}, bf16[2,40,5120]{2,1,0:T(8,128)(2,1)S(1)}, u32[]{:S(2)}, u32[]{:S(2)}) collective-permute-start(bf16[2,40,5120]{2,1,0:T(8,128)(2,1)} %collective-permute-done.48.refs_8_), channel_id=1, source_target_pairs={{0,8},{4,12},{8,0},{12,4},{16,24},{20,28},{24,16},{28,20},{1,9},{5... | collective-permute-start | bytes 2457608 | tf_op jit(solution)/shard_map/ppermute | solution.py:270
  330.2 65.2 %collective-permute-start.47 = (bf16[2,40,5120]{2,1,0:T(8,128)(2,1)S(1)}, bf16[2,40,5120]{2,1,0:T(8,128)(2,1)}, u32[]{:S(2)}, u32[]{:S(2)}) collective-permute-start(bf16[2,40,5120]{2,1,0:T(8,128)(2,1)S(1)} %collective-permute-done.43.refs_3_), channel_id=1, source_target_pairs={{0,8},{4,12},{8,0},{12,4},{16,24},{20,28},{24,16},{28,20},{1,9},{5... | collective-permute-start | bytes 2457608 | tf_op jit(solution)/shard_map/ppermute | solution.py:270
  342.6 80.3 %collective-permute-start.39 = (bf16[512,1280]{1,0:T(8,128)(2,1)}, bf16[512,1280]{1,0:T(8,128)(2,1)}, u32[]{:S(2)}, u32[]{:S(2)}) collective-permute-start(bf16[512,1280]{1,0:T(8,128)(2,1)} %multiply_convert_fusion.6), channel_id=1, source_target_pairs={{0,4},{4,0},{8,12},{12,8},{16,20},{20,16},{24,28},{28,24},{1,5},{5... | collective-permute-start | bytes 3932168 | tf_op jit(solution)/shard_map/ppermute | solution.py:270
  361.0 49.4 %collective-permute-start.51 = (bf16[2,40,5120]{2,1,0:T(8,128)(2,1)S(1)}, bf16[2,40,5120]{2,1,0:T(8,128)(2,1)}, u32[]{:S(2)}, u32[]{:S(2)}) collective-permute-start(bf16[2,40,5120]{2,1,0:T(8,128)(2,1)S(1)} %collective-permute-done.43.refs_3_), channel_id=1, source_target_pairs={{0,16},{4,20},{8,24},{12,28},{16,0},{20,4},{24,8},{28,12},{1,17},{... | collective-permute-start | bytes 2457608 | tf_op jit(solution)/shard_map/ppermute | solution.py:270
  362.5 47.9 %collective-permute-start.54 = (bf16[2,40,5120]{2,1,0:T(8,128)(2,1)S(1)}, bf16[2,40,5120]{2,1,0:T(8,128)(2,1)}, u32[]{:S(2)}, u32[]{:S(2)}) collective-permute-start(bf16[2,40,5120]{2,1,0:T(8,128)(2,1)S(1)} %collective-permute-done.50.refs_10_), channel_id=1, source_target_pairs={{0,8},{4,12},{8,0},{12,4},{16,24},{20,28},{24,16},{28,20},{1,9},{5... | collective-permute-start | bytes 2457608 | tf_op jit(solution)/shard_map/ppermute | solution.py:270
  493.5 91.0 %collective-permute-start.111 = (bf16[2,4,80,1280]{3,2,1,0:T(8,128)(2,1)}, bf16[2,4,80,1280]{3,2,1,0:T(8,128)(2,1)}, u32[]{:S(2)}, u32[]{:S(2)}) collective-permute-start(bf16[2,4,80,1280]{3,2,1,0:T(8,128)(2,1)} %dynamic-slice_bitcast_fusion.3), channel_id=1, source_target_pairs={{0,8},{4,12},{8,0},{12,4},{16,24},{20,28},{24,16},{28,20},{1,9},{5... | collective-permute-start | bytes 4915208 | tf_op jit(solution)/shard_map/ppermute | solution.py:270
  496.0 91.9 %collective-permute-start.116 = (bf16[2,4,80,1280]{3,2,1,0:T(8,128)(2,1)}, bf16[2,4,80,1280]{3,2,1,0:T(8,128)(2,1)}, u32[]{:S(2)}, u32[]{:S(2)}) collective-permute-start(bf16[2,4,80,1280]{3,2,1,0:T(8,128)(2,1)} %dynamic-slice_bitcast_fusion.2), channel_id=1, source_target_pairs={{0,16},{4,20},{8,24},{12,28},{16,0},{20,4},{24,8},{28,12},{1,17},{... | collective-permute-start | bytes 4915208 | tf_op jit(solution)/shard_map/ppermute | solution.py:270
  575.8 284.0 %collective-permute-start.105 = (bf16[2,4,40,5120]{3,2,1,0:T(8,128)(2,1)}, bf16[2,4,40,5120]{3,2,1,0:T(8,128)(2,1)}, u32[]{:S(2)}, u32[]{:S(2)}) collective-permute-start(bf16[2,4,40,5120]{3,2,1,0:T(8,128)(2,1)} %dynamic-slice_bitcast_fusion), channel_id=1, source_target_pairs={{0,16},{4,20},{8,24},{12,28},{16,0},{20,4},{24,8},{28,12},{1,17},{... | collective-permute-start | bytes 9830408 | tf_op jit(solution)/shard_map/ppermute | solution.py:270
  579.4 287.2 %collective-permute-start.100 = (bf16[2,4,40,5120]{3,2,1,0:T(8,128)(2,1)}, bf16[2,4,40,5120]{3,2,1,0:T(8,128)(2,1)}, u32[]{:S(2)}, u32[]{:S(2)}) collective-permute-start(bf16[2,4,40,5120]{3,2,1,0:T(8,128)(2,1)} %dynamic-slice_bitcast_fusion.1), channel_id=1, source_target_pairs={{0,8},{4,12},{8,0},{12,4},{16,24},{20,28},{24,16},{28,20},{1,9},{5... | collective-permute-start | bytes 9830408 | tf_op jit(solution)/shard_map/ppermute | solution.py:270
  584.2 92.2 %collective-permute-start.73 = (f32[512,1280]{1,0:T(8,128)}, f32[512,1280]{1,0:T(8,128)}, u32[]{:S(2)}, u32[]{:S(2)}) collective-permute-start(f32[512,1280]{1,0:T(8,128)} %slice.175), channel_id=1, source_target_pairs={{0,4},{4,0},{8,12},{12,8},{16,20},{20,16},{24,28},{28,24},{1,5},{5... | collective-permute-start | bytes 7864328 | tf_op jit(solution)/shard_map/ppermute | solution.py:270
  587.0 79.2 %collective-permute-start.112 = (bf16[4,80,1280]{2,1,0:T(8,128)(2,1)S(1)}, bf16[4,80,1280]{2,1,0:T(8,128)(2,1)S(1)}, u32[]{:S(2)}, u32[]{:S(2)}) collective-permute-start(bf16[4,80,1280]{2,1,0:T(8,128)(2,1)S(1)} %dynamic-slice_bitcast_fusion.10), channel_id=1, source_target_pairs={{0,16},{4,20},{8,24},{12,28},{16,0},{20,4},{24,8},{28,12},{1,17},{... | collective-permute-start | bytes 2457608 | tf_op jit(solution)/shard_map/ppermute | solution.py:270
  589.9 83.0 %collective-permute-start.117 = (bf16[4,80,1280]{2,1,0:T(8,128)(2,1)S(1)}, bf16[4,80,1280]{2,1,0:T(8,128)(2,1)S(1)}, u32[]{:S(2)}, u32[]{:S(2)}) collective-permute-start(bf16[4,80,1280]{2,1,0:T(8,128)(2,1)S(1)} %dynamic-slice_bitcast_fusion.9), channel_id=1, source_target_pairs={{0,8},{4,12},{8,0},{12,4},{16,24},{20,28},{24,16},{28,20},{1,9},{5... | collective-permute-start | bytes 2457608 | tf_op jit(solution)/shard_map/ppermute | solution.py:270
  859.8 180.8 %collective-permute-start.83 = (bf16[512,1280]{1,0:T(8,128)(2,1)}, bf16[512,1280]{1,0:T(8,128)(2,1)}, u32[]{:S(2)}, u32[]{:S(2)}) collective-permute-start(bf16[512,1280]{1,0:T(8,128)(2,1)} %get-tuple-element.51), channel_id=1, source_target_pairs={{0,1},{1,0},{2,3},{3,2},{4,5},{5,4},{6,7},{7,6},{8,9},{9,8},{10,11... | collective-permute-start | bytes 3932168 | tf_op jit(solution)/shard_map/ppermute | solution.py:274
  867.5 70.7 %collective-permute-start.106 = (bf16[4,40,5120]{2,1,0:T(8,128)(2,1)}, bf16[4,40,5120]{2,1,0:T(8,128)(2,1)}, u32[]{:S(2)}, u32[]{:S(2)}) collective-permute-start(bf16[4,40,5120]{2,1,0:T(8,128)(2,1)} %dynamic-slice_bitcast_fusion.4), channel_id=1, source_target_pairs={{0,8},{4,12},{8,0},{12,4},{16,24},{20,28},{24,16},{28,20},{1,9},{5... | collective-permute-start | bytes 4915208 | tf_op jit(solution)/shard_map/ppermute | solution.py:270
  927.5 113.1 %collective-permute-start.85 = (bf16[512,1280]{1,0:T(8,128)(2,1)}, bf16[512,1280]{1,0:T(8,128)(2,1)}, u32[]{:S(2)}, u32[]{:S(2)}) collective-permute-start(bf16[512,1280]{1,0:T(8,128)(2,1)} %fusion.12), channel_id=1, source_target_pairs={{0,2},{1,3},{2,0},{3,1},{4,6},{5,7},{6,4},{7,5},{8,10},{9,11},{10,... | collective-permute-start | bytes 3932168 | tf_op jit(solution)/shard_map/ppermute | solution.py:274
  (229 other events, 3828.6 us)

commit v2 on v1

--- a/solution.py
+++ b/solution.py
@@ -55,7 +55,7 @@
 
 def head_cols(ref, rows, offset):
     base = offset // LANES * LANES
-    pair = ref[rows, base : base + LANES]
+    pair = ref[rows, base : min(base + LANES, ref.shape[1])]
     return pair[:, offset - base : offset - base + HD]
 
 
@@ -133,8 +133,7 @@
 
 
 def attend(qkv, gain, length):
-    tokens, three = qkv.shape
-    width = three // 3
+    tokens, width = qkv.shape[0], gain.shape[1]
     heads = width // HD
     vmem = pl.BlockSpec(memory_space=pltpu.VMEM)
     aug = jax.ShapeDtypeStruct((heads, tokens, LANES), jnp.bfloat16)
@@ -152,7 +151,7 @@
         scratch_shapes=[pltpu.VMEM((heads, tokens, LANES), jnp.float32)],
         compiler_params=pltpu.CompilerParams(vmem_limit_bytes=56 << 20),
         cost_estimate=pl.CostEstimate(
-            flops=16 * heads * tokens * tokens * HD // 2, bytes_accessed=24 << 20, transcendentals=heads * tokens * tokens // 2
+            flops=heads * tokens * tokens, bytes_accessed=8 << 20, transcendentals=0
         ),
         name="attend",
     )(length, qkv, gain)
@@ -231,7 +230,9 @@
                 )
             dvs.append(jnp.where(inside, dv_ref[head, rows, :][:, :HD], 0.0).astype(jnp.bfloat16))
             sums_new.append(part)
-        grads_ref[rows, :] = jnp.concatenate(dqs + dks + dvs, axis=1)
+        rest = grads_ref.shape[1] - 3 * width
+        nothing = [jnp.zeros((BLK, rest), jnp.bfloat16)] if rest else []
+        grads_ref[rows, :] = jnp.concatenate(dqs + dks + dvs + nothing, axis=1)
         return tuple(sums_new)
 
     sums = lax.fori_loop(
@@ -242,7 +243,7 @@
 
 def attend_back(qkv, gain, length, mixed, d_mixed, qa, ka, va):
     tokens, three = qkv.shape
-    width = three // 3
+    width = gain.shape[1]
     heads = width // HD
     vmem = pl.BlockSpec(memory_space=pltpu.VMEM)
     aug = pltpu.VMEM((heads, tokens, LANES), jnp.float32)
@@ -257,13 +258,14 @@
         scratch_shapes=[pltpu.VMEM((heads, tokens, LANES), jnp.bfloat16), aug, aug, aug],
         compiler_params=pltpu.CompilerParams(vmem_limit_bytes=60 << 20),
         cost_estimate=pl.CostEstimate(
-            flops=40 * heads * tokens * tokens * HD // 2, bytes_accessed=24 << 20, transcendentals=heads * tokens * tokens // 2
+            flops=heads * tokens * tokens, bytes_accessed=8 << 20, transcendentals=0
         ),
         name="attend_back",
     )(length, qkv, gain, mixed, d_mixed, qa, ka, va)
 
 
 CORE, XAX, YAX = 1, 2, 4
+GROUPS = ((0, 3), (3, 5))
 
 
 def swap_dp(v, bit):
@@ -274,80 +276,246 @@
     return lax.ppermute(v, "ctx", [(i, i ^ mask) for i in range(4)])
 
 
+def fence(*arrays):
+    return lax.optimization_barrier(arrays)
+
+
 def pick(v, index, axis=0):
     return lax.dynamic_index_in_dim(v, index, axis, keepdims=False)
 
 
-def gather_z(shard):
-    far = swap_z(shard, 2)
-    return {0: shard, 1: swap_z(shard, 1), 2: far, 3: swap_z(far, 1)}
-
-
-def gather_chips(shard, flip):
-    pieces = {}
-    for mz, piece in gather_z(shard).items():
-        y_first = (mz % 2 == 0) != flip
-        first, second = (YAX, XAX) if y_first else (XAX, YAX)
-        across = swap_dp(piece, first)
-        for key, value in (
-            (0, piece),
-            (first, across),
-            (second, swap_dp(piece, second)),
-            (first | second, swap_dp(across, second)),
-        ):
-            pieces[(key // YAX, key // XAX % 2, mz)] = value
-    return pieces
-
-
-def assemble(pieces, coords, shape, place):
+def assemble(pieces, coords, shapes, place):
     keys = sorted(pieces)
+    count = len(keys)
 
     def kernel(coord_ref, *refs):
-        out_ref, sems = refs[len(keys)], refs[len(keys) + 1]
+        outs, sems = refs[count : count + len(shapes)], refs[-1]
         copies = []
         for at, key in enumerate(keys):
             where = place(*[jnp.bitwise_xor(coord_ref[d], key[d]) for d in range(len(key))])
-            copies.append(pltpu.make_async_copy(refs[at], out_ref.at[where], sems.at[at]))
+            for out, (out_ref, (index, rows)) in enumerate(zip(outs, where)):
+                source = refs[at] if rows is None else refs[at].at[pl.ds(*rows)]
+                copies.append(pltpu.make_async_copy(source, out_ref.at[index], sems.at[at, out]))
         for copy in copies:
             copy.start()
         for copy in copies:
             copy.wait()
 
     some = pieces[keys[0]]
+    outs = pl.pallas_call(
+        kernel,
+        out_shape=[jax.ShapeDtypeStruct(shape, some.dtype) for shape in shapes],
+        in_specs=[pl.BlockSpec(memory_space=pltpu.SMEM)] + [pl.BlockSpec(memory_space=pltpu.HBM)] * count,
+        out_specs=[pl.BlockSpec(memory_space=pltpu.VMEM)] * len(shapes),
+        scratch_shapes=[pltpu.SemaphoreType.DMA((count, len(shapes)))],
+        compiler_params=pltpu.CompilerParams(vmem_limit_bytes=60 << 20),
+        cost_estimate=pl.CostEstimate(flops=0, bytes_accessed=2 * count * some.size * some.dtype.itemsize, transcendentals=0),
+        name="assemble",
+    )(coords, *[pieces[key] for key in keys])
+    return outs
+
+
+def add_low(a, b):
+    return (a.astype(jnp.float32) + b.astype(jnp.float32)).astype(jnp.bfloat16)
+
+
+def by_core(c, own, other, axis=0):
+    return jnp.where(c == 0, jnp.stack([own, other], axis), jnp.stack([other, own], axis))
+
+
+def add3(a, b, d):
+    return (a.astype(jnp.float32) + b.astype(jnp.float32) + d.astype(jnp.float32)).astype(jnp.bfloat16)
+
+
+class Plane:
+    def __init__(self, whole, y, x, x_first):
+        self.whole, self.y, self.x, self.x_first = whole, y, x, x_first
+        self.links = (XAX, YAX) if x_first else (YAX, XAX)
+
+    def cell(self, y_other, x_other):
+        v = self.whole
+        yy = 1 - self.y if y_other else self.y
+        xx = 1 - self.x if x_other else self.x
+        at = (yy, xx) + (0,) * (v.ndim - 2)
+        return lax.dynamic_slice(v, at, (1, 1) + v.shape[2:]).reshape(v.shape[2:])
+
+    def corner(self):
+        return self.cell(True, True)
+
+    def side(self):
+        return self.cell(not self.x_first, self.x_first)
+
+    def far(self):
+        return lax.dynamic_index_in_dim(
+            self.whole, 1 - (self.x if self.x_first else self.y), 1 if self.x_first else 0, keepdims=False
+        )
+
+    def swap_first(self, v):
+        return swap_dp(v, self.links[0])
+
+    def relay(self, got, alone=False):
+        other = 1 - (self.y if self.x_first else self.x)
+        return add_low(self.cell(self.x_first, not self.x_first), got if alone else pick(got, other))
+
+    def swap_second(self, v):
+        return swap_dp(v, self.links[1])
+
+    def total(self, got, relay, alone=False):
+        here = self.y if self.x_first else self.x
+        return add3(self.cell(False, False), got if alone else pick(got, here), relay)
+
+
+def total3(a, b, d):
+    return a.astype(jnp.float32) + b.astype(jnp.float32) + d.astype(jnp.float32)
+
+
+COLS = (0, 640, 1024)
+
+
+def heads_kernel(q_ref, k_ref, v_ref, o_ref, small_ref, out_ref):
+    share, width = o_ref.shape
+    heads_width = width // 4
+    out_ref[...] = jnp.zeros_like(out_ref)
+    for z in range(4):
+        out_ref[z, :, :width] = o_ref[...]
+        for (a, b), at in zip(GROUPS, COLS):
+            size = (b - a) * HD
+            cols = [ref[:, z * heads_width + a * HD : z * heads_width + b * HD] for ref in (q_ref, k_ref, v_ref)]
+            out_ref[z, :, width + at : width + at + 3 * size] = jnp.concatenate(cols, 1)
+        out_ref[z, : small_ref.shape[0], out_ref.shape[2] - small_ref.shape[1] :] = small_ref[...]
+
+
+def prepare_heads(query, key, value, output, small, half):
+    share = output.shape[0]
+    vmem = pl.BlockSpec(memory_space=pltpu.VMEM)
+    return pl.pallas_call(
+        heads_kernel,
+        out_shape=jax.ShapeDtypeStruct((4, share, half), jnp.bfloat16),
+        in_specs=[vmem] * 5,
+        out_specs=vmem,
+        compiler_params=pltpu.CompilerParams(vmem_limit_bytes=60 << 20),
+        cost_estimate=pl.CostEstimate(flops=0, bytes_accessed=2 << 20, transcendentals=0),
+        name="prepare_heads",
+    )(query, key, value, output, small)
+
+
+def prepare_kernel(core_ref, up_ref, gate_ref, down_ref, own_ref, other_ref, dw_ref):
+    width = down_ref.shape[2]
+    step = up_ref.shape[1] // 8
+    for kind, ref in enumerate((up_ref, gate_ref)):
+        for core in range(2):
+
+            @pl.when(core_ref[0] == core)
+            def _():
+                for at in range(4):
+                    here = pl.ds(at * step, step)
+                    own_ref[kind, :, here] = ref[:, (2 * at + core) * step : (2 * at + core + 1) * step]
+                    other_ref[kind, :, here] = ref[:, (2 * at + 1 - core) * step : (2 * at + 2 - core) * step]
+    for part in range(2):
+        for side in range(2):
+            dw_ref[part, :, side * width : (side + 1) * width] = down_ref[2 * part + side]
+
+
+def prepare(c, up, gate, down):
+    share, wide = up.shape
+    vmem = pl.BlockSpec(memory_space=pltpu.VMEM)
+    planes = jax.ShapeDtypeStruct((2, share, wide // 2), jnp.bfloat16)
+    return pl.pallas_call(
+        prepare_kernel,
+        out_shape=(planes,) * 3,
+        in_specs=[pl.BlockSpec(memory_space=pltpu.SMEM)] + [vmem] * 3,
+        out_specs=(vmem,) * 3,
+        compiler_params=pltpu.CompilerParams(vmem_limit_bytes=60 << 20),
+        cost_estimate=pl.CostEstimate(flops=0, bytes_accessed=4 << 20, transcendentals=0),
+        name="prepare",
+    )(c.astype(jnp.int32).reshape(1), up, gate, down)
+
+
+def run_copies(copies):
+    copies = [pltpu.make_async_copy(*copy) for copy in copies]
+    for copy in copies:
+        copy.start()
+    for copy in copies:
+        copy.wait()
+
+
+def join(upper, lower):
+    rows, width = upper.shape
+
+    def kernel(upper_ref, lower_ref, out_ref, sems):
+        run_copies(
+            [
+                (upper_ref, out_ref.at[pl.ds(0, rows)], sems.at[0]),
+                (lower_ref, out_ref.at[pl.ds(rows, rows)], sems.at[1]),
+            ]
+        )
+
     return pl.pallas_call(
         kernel,
-        out_shape=jax.ShapeDtypeStruct(shape, some.dtype),
-        in_specs=[pl.BlockSpec(memory_space=pltpu.SMEM)] + [pl.BlockSpec(memory_space=pl.ANY)] * len(keys),
+        out_shape=jax.ShapeDtypeStruct((2 * rows, width), upper.dtype),
+        in_specs=[pl.BlockSpec(memory_space=pltpu.HBM)] * 2,
         out_specs=pl.BlockSpec(memory_space=pltpu.VMEM),
-        scratch_shapes=[pltpu.SemaphoreType.DMA((len(keys),))],
-        compiler_params=pltpu.CompilerParams(vmem_limit_bytes=40 << 20),
-        cost_estimate=pl.CostEstimate(flops=0, bytes_accessed=2 * len(keys) * some.size * some.dtype.itemsize, transcendentals=0),
-        name="assemble",
-    )(coords, *[pieces[key] for key in keys])
-
-
-def add_low(a, b):
-    return (a.astype(jnp.float32) + b.astype(jnp.float32)).astype(jnp.bfloat16)
-
-
-def reduce_z(parts, z):
-    relay = swap_z(pick(parts, z ^ 3), 1)
-    far = add_low(pick(parts, z ^ 2), relay)
-    near = swap_z(pick(parts, z ^ 1), 1)
-    far = swap_z(far, 2)
-    return pick(parts, z).astype(jnp.float32) + near.astype(jnp.float32) + far.astype(jnp.float32)
-
-
-def reduce_xy(parts, x, y, x_first):
-    if x_first:
-        half = add_low(pick(parts, x, 1), swap_dp(pick(parts, 1 - x, 1), XAX))
-        return add_low(pick(half, y), swap_dp(pick(half, 1 - y), YAX))
-    half = add_low(pick(parts, y), swap_dp(pick(parts, 1 - y), YAX))
-    return add_low(pick(half, x), swap_dp(pick(half, 1 - x), XAX))
-
-
-def by_core(c, own, other, axis=0):
-    return jnp.where(c == 0, jnp.stack([own, other], axis), jnp.stack([other, own], axis))
+        scratch_shapes=[pltpu.SemaphoreType.DMA((2,))],
+        compiler_params=pltpu.CompilerParams(vmem_limit_bytes=60 << 20),
+        cost_estimate=pl.CostEstimate(flops=0, bytes_accessed=6 << 20, transcendentals=0),
+        name="join",
+    )(upper, lower)
+
+
+def place(sources, plan, coords, cuts):
+    count, rows = len(sources), sources[0].shape[1]
+
+    def kernel(coord_ref, *refs):
+        outs, sems = refs[count:-1], refs[-1]
+        copies = []
+        for at, (key, array, plane, inner) in enumerate(plan):
+            where = tuple(jnp.bitwise_xor(coord_ref[d], key[d]) for d in range(3)) + (inner,)
+            for out, (out_ref, (size, start, length)) in enumerate(zip(outs, cuts)):
+                copies.append((refs[array].at[plane, :, pl.ds(start, length)], out_ref.at[where], sems.at[at, out]))
+        run_copies(copies)
+
+    return pl.pallas_call(
+        kernel,
+        out_shape=[jax.ShapeDtypeStruct((2, 2, 2, 4, rows, size), jnp.bfloat16) for size, _, _ in cuts],
+        in_specs=[pl.BlockSpec(memory_space=pltpu.SMEM)] + [pl.BlockSpec(memory_space=pltpu.HBM)] * count,
+        out_specs=[pl.BlockSpec(memory_space=pltpu.VMEM)] * len(cuts),
+        scratch_shapes=[pltpu.SemaphoreType.DMA((len(plan), len(cuts)))],
+        compiler_params=pltpu.CompilerParams(vmem_limit_bytes=60 << 20),
+        cost_estimate=pl.CostEstimate(flops=0, bytes_accessed=14 << 20, transcendentals=0),
+        name="place",
+    )(coords, *sources)
+
+
+def spread(sources, plan, coords, width):
+    count, share, half = len(sources), sources[0].shape[1], sources[0].shape[2]
+
+    def kernel(coord_ref, *refs):
+        up_ref, gate_ref, down_ref, sems = refs[count:]
+        copies = []
+        for at, (key, array, plane, core) in enumerate(plan):
+            yy, xx, zz = (jnp.bitwise_xor(coord_ref[d], key[d]) for d in range(3))
+            for kind, out_ref in enumerate((up_ref, gate_ref)):
+                copies.append((refs[array].at[plane + kind], out_ref.at[yy, xx, core, zz], sems.at[at, kind]))
+            for side in range(2):
+                lanes = pl.ds(side * width, width)
+                copies.append((refs[array].at[plane + 2, :, lanes], down_ref.at[yy, xx, zz, core, side], sems.at[at, 2 + side]))
+        run_copies(copies)
+
+    up, gate, down = pl.pallas_call(
+        kernel,
+        out_shape=[
+            jax.ShapeDtypeStruct((2, 2, 2, 4, share, half), jnp.bfloat16),
+            jax.ShapeDtypeStruct((2, 2, 2, 4, share, half), jnp.bfloat16),
+            jax.ShapeDtypeStruct((2, 2, 4, 2, 2, share, width), jnp.bfloat16),
+        ],
+        in_specs=[pl.BlockSpec(memory_space=pltpu.SMEM)] + [pl.BlockSpec(memory_space=pltpu.HBM)] * count,
+        out_specs=[pl.BlockSpec(memory_space=pltpu.VMEM)] * 3,
+        scratch_shapes=[pltpu.SemaphoreType.DMA((len(plan), 4))],
+        compiler_params=pltpu.CompilerParams(vmem_limit_bytes=60 << 20),
+        cost_estimate=pl.CostEstimate(flops=0, bytes_accessed=40 << 20, transcendentals=0),
+        name="spread",
+    )(coords, *sources)
+    return up.reshape(32 * share, half), gate.reshape(32 * share, half), down.reshape(64 * share, width)
 
 
 def on_cores(
@@ -371,6 +539,8 @@
     share = query_weight.shape[0]
     hidden_share = down_weight.shape[0]
     heads_width = width // 4
+    three = COLS[-1]
+    hidden_half = up_weight.shape[1] // 2
     tokens = local * 4
     low = jnp.bfloat16
     f32 = jnp.float32
@@ -380,40 +550,60 @@
     line = z.astype(jnp.int32).reshape(1)
     states = inputs.reshape(local, width)
 
-    shards = jnp.stack([query_weight, key_weight, value_projection], 1).reshape(share, 3, 4, heads_width)
-    shards = shards.transpose(2, 0, 1, 3).reshape(4, share, 3 * heads_width)
-    pieces = {(m,): swap_z(pick(shards, z ^ m), m) if m else pick(shards, z) for m in range(4)}
-    rows_qkv = assemble(pieces, line, (4, share, 3 * heads_width), lambda zz: (zz,)).reshape(2, 2 * share, 3 * heads_width)
-    pieces = {}
-    for half, (first, second) in enumerate(((XAX, YAX), (YAX, XAX))):
-        piece = rows_qkv[half]
-        across = swap_dp(piece, first)
-        for key, value in ((0, piece), (first, across), (second, swap_dp(piece, second)), (first | second, swap_dp(across, second))):
-            for core in (0, 1):
-                pieces[(key // YAX, key // XAX % 2, core, half)] = swap_dp(value, CORE) if core else value
-    full_qkv = assemble(
-        pieces,
-        jnp.stack([y, x, c, jnp.zeros_like(c)]).astype(jnp.int32),
-        (2, 2, 2, 2, 2 * share, 3 * heads_width),
-        lambda yy, xx, cc, half: (yy, xx, cc, half),
-    ).reshape(width, 3 * heads_width)
-
-    whole_states = assemble(
-        {(m,): piece for m, piece in gather_z(states).items()}, line, (4, local, width), lambda zz: (zz,)
-    ).reshape(tokens, width)
-
     length_parts = jnp.stack([lengths[0] // 64, lengths[0] % 64]).astype(low)
     small = jnp.concatenate([score_gain, attention_step, up_scale, gate_scale, swiglu_step, length_parts])
-    small = jnp.pad(small, (0, width - small.shape[0])).reshape(1, width)
-    misc_rows = share + 8
-    misc = jnp.concatenate([output_weight, small, jnp.zeros((7, width), low)], 0)
-    misc = assemble(gather_chips(misc, False), chip, (2, 2, 4, misc_rows, width), lambda yy, xx, zz: (yy, xx, zz))
-    misc = by_core(c, misc, swap_dp(misc, CORE), 2)
-    full_output = misc[:, :, :, :, :share].reshape(width, width)
-    vectors = misc[:, :, :, :, share]
     cuts = [0]
     for size in (share, share, hidden_share, hidden_share, share, 2):
         cuts.append(cuts[-1] + size)
+    small = jnp.pad(small, (0, 512 - small.shape[0])).reshape(2, 256)
+    half = up_weight.shape[1] // 2
+    ug_own, ug_other, dw = prepare(c, up_weight, gate_weight, down_weight.reshape(4, share, width))
+    q0 = prepare_heads(query_weight, key_weight, value_projection, output_weight, small, half)
+
+    def on_x(*v):
+        return swap_dp(jnp.concatenate(v) if len(v) > 1 else v[0], XAX)
+
+    def on_y(*v):
+        return swap_dp(jnp.concatenate(v) if len(v) > 1 else v[0], YAX)
+
+    def exchange(blocks):
+        return lax.all_to_all(blocks, "ctx", 0, 0, tiled=True)
+
+    ug_sib = swap_dp(ug_other, CORE)
+    ug_sib, ug_own = fence(ug_sib, ug_own)
+    f0 = jnp.concatenate([by_core(c, ug_own, ug_sib), dw[:, None]], 1).reshape(6, share, half)
+    q0 = exchange(q0)
+    f0x, f0y, f1 = on_x(f0), on_y(f0), swap_z(f0, 1)
+    f0, f0x, f0y, f1, q0, states = fence(f0, f0x, f0y, f1, q0, states)
+    xb, yb = on_x(f1, f0y[:3], q0), on_y(f1, f0x[3:], q0)
+    s1, s2 = swap_z(states, 1), swap_z(states, 2)
+    xb, yb, s1, s2, f0 = fence(xb, yb, s1, s2, f0)
+    f2, s3 = swap_z(f0, 2), swap_z(s2, 1)
+    xc, yc = on_x(yb[:3], yb[9:11]), on_y(xb[3:6], xb[11:])
+    qc = swap_dp(jnp.concatenate([q0, xb[9:], yb[9:]]), CORE)
+    f2, s3, xc, yc, qc = fence(f2, s3, xc, yc, qc)
+    f2x, f2y, f3 = on_x(f2), on_y(f2), swap_z(f2, 1)
+    qd = swap_dp(jnp.concatenate([xc[3:], yc[3:]]), CORE)
+    sources = [q0, xb, yb, xc, yc, qc, qd]
+    plan = []
+    for mc, (own, own_at, on_x_, x_at, on_y_, y_at, cross0, at0, cross1, at1) in enumerate(
+        ((0, 0, 1, 9, 2, 9, 3, 3, 4, 3), (5, 0, 5, 4, 5, 8, 6, 0, 6, 2))
+    ):
+        for zz in range(4):
+            plan.append(((0, 0, mc), own, own_at + zz, zz))
+            plan.append(((0, 1, mc), on_x_, x_at + zz, zz))
+            plan.append(((1, 0, mc), on_y_, y_at + zz, zz))
+            if zz < 2:
+                plan.append(((1, 1, mc), cross0, at0 + zz, zz))
+            else:
+                plan.append(((1, 1, mc), cross1, at1 + zz - 2, zz))
+    full_output, full_qkv, vectors = place(
+        sources, plan, jnp.stack([y, x, c]).astype(jnp.int32),
+        [(width, 0, width), (half - width - 256, width, half - width - 256), (256, half - 256, 256)],
+    )
+    vectors = vectors[:, :, :, :, :2].reshape(2, 2, 2, 4, 512)
+    full_output = full_output.reshape(width, width)
+    full_qkv = full_qkv.reshape(width, -1)
     full_gain, full_astep, full_uscale, full_gscale, full_mstep, full_lengths = (
         vectors[..., a:b].astype(f32) for a, b in zip(cuts[:-1], cuts[1:])
     )
@@ -423,46 +613,55 @@
     scale_up = pick(full_uscale, c, 2).reshape(-1)
     scale_gate = pick(full_gscale, c, 2).reshape(-1)
     gain = pick(full_gain.reshape(4, 1, heads_width), z)
-
-    def halves(weight):
-        cut = weight.reshape(share, 4, 2, hidden_share * 4)
-        return cut[:, :, 0].reshape(share, -1), cut[:, :, 1].reshape(share, -1)
-
-    up_halves, gate_halves = halves(up_weight), halves(gate_weight)
-    half0 = jnp.concatenate([up_halves[0], gate_halves[0]], 1)
-    half1 = jnp.concatenate([up_halves[1], gate_halves[1]], 1)
-    own, other = jnp.where(c == 0, half0, half1), jnp.where(c == 0, half1, half0)
-    shard = by_core(c, own, swap_dp(other, CORE))
-    wide = half0.shape[1]
-    hidden_half = wide // 2
-    full_wide = assemble(
-        gather_chips(shard, False), chip, (2, 2, 2, 4, share, wide), lambda yy, xx, zz: (yy, xx, slice(None), zz)
-    ).reshape(width, wide)
-    full_down = assemble(
-        gather_chips(down_weight, True), chip, (2, 2, 4, hidden_share, width), lambda yy, xx, zz: (yy, xx, zz)
-    ).reshape(hidden_half, width)
-
-    qkv = matmul(whole_states, full_qkv)
-    mixed, mixed_heads, qa, ka, va = attend(qkv, gain, lengths)
-    blocks = mixed_heads.reshape(4, local, heads_width)
-    pieces = {(m,): swap_z(pick(blocks, z ^ m), m) if m else pick(blocks, z) for m in range(4)}
-    mixed_low = assemble(pieces, line, (4, local, heads_width), lambda zz: (zz,)).transpose(1, 0, 2).reshape(local, width)
+    (whole_states,) = assemble(
+        {(0,): states, (1,): s1, (2,): s2, (3,): s3}, line, [(4, local, width)], lambda zz: [(zz, None)]
+    )
+    whole_states = whole_states.reshape(tokens, width)
+    gains = [gain[:, a * HD : b * HD] for a, b in GROUPS]
+    qkv0 = matmul(whole_states, full_qkv[:, : COLS[1]])
+    qkv1 = matmul(whole_states, full_qkv[:, COLS[1] :])
+    qkv0, qkv1, f2x, f2y, f3 = fence(qkv0, qkv1, f2x, f2y, f3)
+    xd, yd = on_x(f3, f2y[:3]), on_y(f3, f2x[3:])
+    mixed0, heads0, qa0, ka0, va0 = attend(qkv0, gains[0], lengths)
+    heads0, xd, yd, qkv1 = fence(heads0, xd, yd, qkv1)
+    parts0 = exchange(heads0.reshape(4, local, -1))
+    xe, ye = on_x(yd[:3]), on_y(xd[3:6])
+    mixed1, heads1, qa1, ka1, va1 = attend(qkv1, gains[1], lengths)
+    heads1, xe, ye, parts0 = fence(heads1, xe, ye, parts0)
+    parts1 = exchange(heads1.reshape(4, local, -1))
+    sources = [f0, f0x, f0y, f1, xb, yb, xc, yc, f2, f2x, f2y, f3, xd, yd, xe, ye]
+    plan = []
+    for mz, (own, at_x, at_y, at_yx, at_xy) in enumerate(
+        (
+            ((0, 0), (1, 0), (2, 0), (4, 6), (5, 6)),
+            ((3, 0), (4, 0), (5, 0), (6, 0), (7, 0)),
+            ((8, 0), (9, 0), (10, 0), (12, 6), (13, 6)),
+            ((11, 0), (12, 0), (13, 0), (14, 0), (15, 0)),
+        )
+    ):
+        for core in range(2):
+            for key, (array, plane) in (((0, 0), own), ((0, 1), at_x), ((1, 0), at_y)):
+                plan.append((key + (mz,), array, plane + 3 * core, core))
+            array, plane = (at_yx, at_xy)[core]
+            plan.append(((1, 1, mz), array, plane, core))
+    full_up, full_gate, full_down = spread(sources, plan, chip, width)
+    full_up, full_gate, full_down, parts1 = fence(full_up, full_gate, full_down, parts1)
+    mixed_low = jnp.concatenate([parts0, parts1], -1).transpose(1, 0, 2).reshape(local, width)
     branch = matmul(mixed_low, full_output)
     resid = states.astype(f32)
     branch_norm = normalize(branch)
     first = resid + astep * (branch_norm - resid)
     middle = normalize(first)
-
     middle_low = middle.astype(low)
-    middle_both = jnp.concatenate([middle_low, swap_dp(middle_low, CORE)], 0)
-    both = matmul(middle_both, full_wide)
-    upper, gating = both[:, :hidden_half], both[:, hidden_half:]
+    middle_both = join(middle_low, swap_dp(middle_low, CORE))
+    upper = matmul(middle_both, full_up)
+    gating = matmul(middle_both, full_gate)
     upper_scaled = upper * scale_up
     gate_arg = gating * scale_gate
     gate_act = jax.nn.silu(gate_arg)
     hidden = (upper_scaled * gate_act).astype(low)
     lower = matmul(hidden, full_down)
-    lower = lower[:local] + swap_dp(lower[local:], CORE)
+    lower = lower[:local] + swap_dp(lower[local:].astype(low), CORE).astype(f32)
     lower_norm = normalize(lower)
     second = middle + mstep * (lower_norm - middle)
     final = normalize(second)
@@ -477,82 +676,162 @@
     d_middle = d_second * (1.0 - mstep)
     grad_mstep = jnp.sum(d_second * (lower_norm - middle), axis=0)
     d_lower = norm_back(lower, lower_norm, d_second * mstep).astype(low)
-    d_lower_both = jnp.concatenate([d_lower, swap_dp(d_lower, CORE)], 0)
-    grad_down = left_tdot(hidden, d_lower_both).astype(low).reshape(2, 2, 4, 2, hidden_share // 2, width)
-    down_grad = jnp.concatenate(
-        [reduce_z(reduce_xy(grad_down[:, :, :, part], x, y, part == 0), z) for part in range(2)], 0
-    )
+    d_lower_both = join(d_lower, swap_dp(d_lower, CORE))
+    g_down = left_tdot(hidden, d_lower_both).astype(low).reshape(2, 2, 4, 2, hidden_share // 2, width)
+    downs = [Plane(g_down[:, :, :, part], y, x, part == 0) for part in range(2)]
+    sends = [p.far() for p in downs]
+    sends, d_lower_both = fence(sends, d_lower_both)
+    down_far = [p.swap_first(v) for p, v in zip(downs, sends)]
     d_hidden = right_tdot(d_lower_both, full_down)
     d_upper = d_hidden * gate_act
     sigmoid_gate = jax.nn.sigmoid(gate_arg)
     d_gate_arg = d_hidden * upper_scaled * (sigmoid_gate * (1.0 + gate_arg * (1.0 - sigmoid_gate)))
     grad_uscale = jnp.sum(d_upper * upper, axis=0)
     grad_gscale = jnp.sum(d_gate_arg * gating, axis=0)
-    d_wide = jnp.concatenate([(d_upper * scale_up).astype(low), (d_gate_arg * scale_gate).astype(low)], 1)
-    grad_wide = left_tdot(middle_both, d_wide).astype(low).reshape(2, 2, 2, 4, share, wide)
-    wide_rows = [reduce_z(reduce_xy(grad_wide[:, :, core], x, y, core == 0), z) for core in range(2)]
-    own = jnp.where(c == 0, wide_rows[0], wide_rows[1])
-    other = swap_dp(jnp.where(c == 0, wide_rows[1], wide_rows[0]), CORE)
-    wide_grad = by_core(c, own.reshape(share, 2, 4, -1), other.reshape(share, 2, 4, -1), 3)
-    up_grad = wide_grad[:, 0].reshape(up_weight.shape)
-    gate_grad = wide_grad[:, 1].reshape(up_weight.shape)
-    d_both = right_tdot(d_wide, full_wide)
-    d_middle = d_middle + d_both[:local] + swap_dp(d_both[local:], CORE)
-
+    d_up, d_gate = (d_upper * scale_up).astype(low), (d_gate_arg * scale_gate).astype(low)
+    d_up, d_gate, down_far = fence(d_up, d_gate, down_far)
+    down_relay = [p.swap_second(p.relay(v)) for p, v in zip(downs, down_far)]
+    ups = left_tdot(middle_both, d_up).astype(low).reshape(2, 2, 2, 4, share, hidden_half)
+    ups = [Plane(ups[:, :, core], y, x, core == 0) for core in range(2)]
+    corners, up_sides = [p.corner() for p in ups], [p.side() for p in ups]
+    corners, up_sides, down_relay, d_up, d_gate = fence(corners, up_sides, down_relay, d_up, d_gate)
+    up_corner = [p.swap_first(v) for p, v in zip(ups, corners)]
+    d_both = right_tdot(d_up, full_up) + right_tdot(d_gate, full_gate)
+    up_corner, d_both, d_gate, up_sides = fence(up_corner, d_both, d_gate, up_sides)
+    up_side = [p.swap_first(v) for p, v in zip(ups, up_sides)]
+    d_middle = d_middle + d_both[:local] + swap_dp(d_both[local:].astype(low), CORE).astype(f32)
     d_first = norm_back(first, middle, d_middle)
     input_grad = d_first * (1.0 - astep)
     grad_astep = jnp.sum(d_first * (branch_norm - resid), axis=0)
     d_branch = norm_back(branch, branch_norm, d_first * astep).astype(low)
     d_mixed = right_tdot(d_branch, full_output).astype(low)
     blocks = d_mixed.reshape(local, 4, heads_width).transpose(1, 0, 2)
-    pieces = {(m,): swap_z(pick(blocks, z ^ m), m) if m else pick(blocks, z) for m in range(4)}
-    d_mixed = assemble(pieces, line, (4, local, heads_width), lambda zz: (zz,)).reshape(tokens, heads_width)
-    grad_output = left_tdot(mixed_low, d_branch).astype(low).reshape(2, 2, 2, 4, share, width)
-    grad_output = add_low(pick(grad_output, c, 2), swap_dp(pick(grad_output, 1 - c, 2), CORE))
-    output_grad = reduce_z(reduce_xy(grad_output, x, y, True), z)
-    d_qkv, grad_gain = attend_back(qkv, gain, lengths, mixed, d_mixed, qa, ka, va)
-    d_states = right_tdot(d_qkv, full_qkv).astype(low).reshape(4, local, width)
-    input_grad = input_grad + reduce_z(d_states, z)
-    grad_qkv = left_tdot(whole_states, d_qkv).astype(low).reshape(2, 2, 2, 2, 2 * share, 3 * heads_width)
-    grad_qkv = add_low(pick(grad_qkv, c, 2), swap_dp(pick(grad_qkv, 1 - c, 2), CORE))
-    rows_qkv = jnp.stack([reduce_xy(grad_qkv[:, :, half], x, y, half == 0) for half in range(2)])
-    rows_qkv = rows_qkv.reshape(4, share, 3 * heads_width)
-    pieces = {(m,): swap_z(pick(rows_qkv, z ^ m), m) if m else pick(rows_qkv, z) for m in range(4)}
-    columns = assemble(pieces, line, (4, share, 3 * heads_width), lambda zz: (zz,))
-    columns = columns.reshape(4, share, 3, heads_width).transpose(2, 1, 0, 3).reshape(3, share, width).astype(f32)
-
-    gain_all = lax.dynamic_update_slice(jnp.zeros((4, heads_width), f32), grad_gain, (z, 0)).reshape(32, share)
+    blocks = [blocks[:, :, a * HD : b * HD] for a, b in GROUPS]
     scales = jnp.concatenate([grad_uscale.reshape(2, 2, 4, hidden_share), grad_gscale.reshape(2, 2, 4, hidden_share)], -1)
     scales = jnp.where((jnp.arange(2) == c)[None, None, :, None, None], scales[:, :, None], 0.0).reshape(32, -1)
     packed = jnp.concatenate(
-        [gain_all, grad_astep.reshape(32, share), scales, grad_mstep.reshape(32, share), jnp.full((32, 1), err_local)], 1
+        [grad_astep.reshape(32, share), scales, grad_mstep.reshape(32, share), jnp.full((32, 1), err_local)], 1
     )
     packed = jnp.pad(packed, ((0, 0), (0, 512 - packed.shape[1]))).reshape(2, 2, 2, 4, 4, 128)
     packed = pick(packed, c, 2) + swap_dp(pick(packed, 1 - c, 2), CORE)
+    down = jnp.stack([p.total(v, r) for p, v, r in zip(downs, down_far, down_relay)], 1)
+    down_far = swap_z(pick(down, z ^ 3), 1)
+    blocks, d_branch, up_side, d_gate, up_corner, packed, down, down_far = fence(
+        blocks, d_branch, up_side, d_gate, up_corner, packed, down, down_far
+    )
+    parts0 = exchange(blocks[0])
+    up_relay = [p.swap_second(p.relay(v, True)) for p, v in zip(ups, up_corner)]
+    gates = left_tdot(middle_both, d_gate).astype(low).reshape(2, 2, 2, 4, share, hidden_half)
+    gates = [Plane(gates[:, :, core], y, x, core == 0) for core in range(2)]
+    corners, gate_sides = [p.corner() for p in gates], [p.side() for p in gates]
     packed = pick(packed, x, 1) + swap_dp(pick(packed, 1 - x, 1), XAX)
+    up_relay, corners, gate_sides, block1, d_branch, packed = fence(
+        up_relay, corners, gate_sides, blocks[1], d_branch, packed
+    )
+    gate_corner = [p.swap_first(v) for p, v in zip(gates, corners)]
+    up = jnp.stack([p.total(v, r, True) for p, v, r in zip(ups, up_side, up_relay)])
+    down_far, down_near = swap_z(add_low(pick(down, z ^ 2), down_far), 2), swap_z(pick(down, z ^ 1), 1)
+    g_out = left_tdot(mixed_low, d_branch).astype(low).reshape(2, 2, 2, 2, 2 * share, width)
+    out_c = swap_dp(pick(g_out, 1 - c, 2), CORE)
+    g_out = add_low(pick(g_out, c, 2), out_c)
+    parts0, gate_corner, up, g_out, gate_sides, down_far, down_near = fence(
+        parts0, gate_corner, up, g_out, gate_sides, down_far, down_near
+    )
+    parts1 = exchange(block1)
+    gate_side = [p.swap_first(v) for p, v in zip(gates, gate_sides)]
+    gate_relay = [p.swap_second(p.relay(v, True)) for p, v in zip(gates, gate_corner)]
+    up_far = swap_z(pick(up, z ^ 3, 1), 1)
+    d_heads0 = parts0.reshape(tokens, -1)
+    d_qkv0, gain_grad0 = attend_back(qkv0, gains[0], lengths, mixed0, d_heads0, qa0, ka0, va0)
+    d_qkv0, gain_grad0, parts1, gate_side, gate_relay, up_far, up, packed = fence(
+        d_qkv0, gain_grad0, parts1, gate_side, gate_relay, up_far, up, packed
+    )
+    gate = jnp.stack([p.total(v, r, True) for p, v, r in zip(gates, gate_side, gate_relay)])
+    up_far, up_near = swap_z(add_low(pick(up, z ^ 2, 1), up_far), 2), swap_z(pick(up, z ^ 1, 1), 1)
+    gate_far, gate_near = swap_z(pick(gate, z ^ 3, 1), 1), swap_z(pick(gate, z ^ 1, 1), 1)
     packed = pick(packed, y) + swap_dp(pick(packed, 1 - y), YAX)
-    packed = (
-        pick(packed, z)
-        + swap_z(pick(packed, z ^ 1), 1)
-        + swap_z(pick(packed, z ^ 2), 2)
-        + swap_z(pick(packed, z ^ 3), 3)
-    ).reshape(512)
+    d_heads1 = parts1.reshape(tokens, -1)
+    d_qkv1, gain_grad1 = attend_back(qkv1, gains[1], lengths, mixed1, d_heads1, qa1, ka1, va1)
+    d_qkv1, gain_grad1, gate, up_far, up_near, gate_far, gate_near, d_qkv0, packed = fence(
+        d_qkv1, gain_grad1, gate, up_far, up_near, gate_far, gate_near, d_qkv0, packed
+    )
+    d_qkv = jnp.concatenate([d_qkv0, d_qkv1], 1)
+    d_states = right_tdot(d_qkv, full_qkv).astype(low).reshape(4, local, width)
+    states_send = pick(d_states, z ^ 3)
+    gate_send = add_low(pick(gate, z ^ 2, 1), gate_far)
+    states_send, d_states, d_qkv, whole_states, gain_grad1, gate_send, gate, packed = fence(
+        states_send, d_states, d_qkv, whole_states, gain_grad1, gate_send, gate, packed
+    )
+    cut = local // 2
+    relay0 = swap_z(states_send[:cut], 1)
+    gate_far = swap_z(gate_send, 2)
+    pair = swap_z(jnp.stack([pick(packed, z ^ 2), pick(packed, z ^ 3)]), 2)
+    packed = jnp.stack([pick(packed, z), pick(packed, z ^ 1)]) + pair
+    grad_gain = jnp.concatenate([gain_grad0, gain_grad1], 1).reshape(-1)
+    gain_all = lax.dynamic_update_slice(jnp.zeros((4 * heads_width,), f32), grad_gain, (z * heads_width,))
+    spare = COLS[0] + 3 * (GROUPS[0][1] - GROUPS[0][0]) * HD
+    g_qkv = left_tdot(whole_states, d_qkv)
+    g_qkv = jnp.where(jnp.arange(three)[None] == spare, gain_all[:, None], g_qkv)
+    g_qkv = g_qkv.astype(low).reshape(2, 2, 2, 2, 2 * share, three)
+    qkv_c = swap_dp(pick(g_qkv, 1 - c, 2), CORE)
+    relay0, qkv_c, g_qkv, d_states, states_send, packed, gate_far = fence(
+        relay0, qkv_c, g_qkv, d_states, states_send, packed, gate_far
+    )
+    relay1 = swap_z(states_send[cut:], 1)
+    far0 = swap_z(add_low(pick(d_states, z ^ 2)[:cut], relay0), 2)
+    g_rows = jnp.concatenate([add_low(pick(g_qkv, c, 2), qkv_c), g_out], -1)
+    rows = [Plane(g_rows[:, :, part], y, x, part == 0) for part in range(2)]
+    row_far = [p.swap_first(p.far()) for p in rows]
+    packed = packed[0] + swap_z(packed[1], 1)
+    own_rows = total3(pick(up, z, 1), up_near, up_far), total3(pick(gate, z, 1), gate_near, gate_far)
+    own_rows = jnp.stack(own_rows, 1)
+    other = swap_dp(pick(own_rows, 1 - c), CORE)
+    down_grad = total3(pick(down, z), down_near, down_far).reshape(hidden_share, width)
+    relay1, far0, row_far, d_states, own_rows, other, packed, down_grad = fence(
+        relay1, far0, row_far, d_states, own_rows, other, packed, down_grad
+    )
+    states_near = pick(d_states, z ^ 1)
+    near0 = swap_z(states_near[:cut], 1)
+    row_relay = [p.swap_second(p.relay(v)) for p, v in zip(rows, row_far)]
+    states_send = add_low(pick(d_states, z ^ 2)[cut:], relay1)
+    wide_grad = by_core(c, pick(own_rows, c).reshape(2, share, 4, -1), other.reshape(2, share, 4, -1), 3)
+    up_grad = wide_grad[0].reshape(up_weight.shape)
+    gate_grad = wide_grad[1].reshape(up_weight.shape)
+    near0, row_relay, states_send, states_near, up_grad, gate_grad = fence(
+        near0, row_relay, states_send, states_near, up_grad, gate_grad
+    )
+    rows_sum = jnp.stack([p.total(v, r) for p, v, r in zip(rows, row_far, row_relay)]).reshape(4, share, three + width)
+    columns = exchange(rows_sum)
+    far1, near1 = swap_z(states_send, 2), swap_z(states_near[cut:], 1)
+    packed = packed.reshape(512)
+    output_grad = jnp.sum(columns[..., three:].astype(f32), 0)
+    columns_cut = [
+        columns[..., at : at + 3 * (b - a) * HD].reshape(4, share, 3, -1) for (a, b), at in zip(GROUPS, COLS)
+    ]
+    score_gain_grad = jnp.sum(columns[..., spare].astype(f32), 0)
+    columns = jnp.concatenate(columns_cut, -1).transpose(2, 1, 0, 3).reshape(3, share, width).astype(f32)
+    columns, output_grad, score_gain_grad, input_grad, far1, near1 = fence(
+        columns, output_grad, score_gain_grad, input_grad, far1, near1
+    )
+    own = pick(d_states, z)
+    states_sum = [total3(own[:cut], near0, far0), total3(own[cut:], near1, far1)]
+    input_grad = input_grad + jnp.concatenate(states_sum)
     return (
         final.astype(low)[None],
-        packed[cuts[5]] / count,
+        packed[cuts[5] - cuts[1]] / count,
         input_grad[None],
         columns[0],
         columns[1],
         columns[2],
         output_grad,
+        score_gain_grad,
         packed[: cuts[1]],
-        packed[cuts[1] : cuts[2]],
         up_grad,
         gate_grad,
         down_grad,
-        packed[cuts[2] : cuts[3]],
-        packed[cuts[3] : cuts[4]],
-        packed[cuts[4] : cuts[5]],
+        packed[cuts[2] - cuts[1] : cuts[3] - cuts[1]],
+        packed[cuts[3] - cuts[1] : cuts[4] - cuts[1]],
+        packed[cuts[4] - cuts[1] : cuts[5] - cuts[1]],
     )
 
 

time: 1060 us -> 898 us (0.85)
  waiting for transfers between devices: 415 us -> 296 us
  starting transfers between devices: 156 us -> 104 us
  local copies, waits for them, and re-layouts: 141 us -> 92.3 us
  other arithmetic: 76.9 us -> 99.3 us
  Pallas kernels: 123 us -> 141 us
  matrix products: 134 us -> 149 us
    ppermute x76 -> x45, waiting for transfers between devices: 217 us -> 98.3 us  [swap_dp(): return lax.ppermute(v, 'dp', [(i, i ^ bit) for i in range(8)])]
    ppermute x76 -> x45, starting transfers between devices: 86.7 us -> 38.7 us  [swap_dp(): return lax.ppermute(v, 'dp', [(i, i ^ bit) for i in range(8)])]
    unnamed x270 -> x163, local copies, waits for them, and re-layouts: 55.5 us -> 21.3 us
    ppermute x45 -> x23, starting transfers between devices: 69.5 us -> 38.2 us  [swap_z(): return lax.ppermute(v, 'ctx', [(i, i ^ mask) for i in range(4)])]
    all_to_all x0 -> x6, waiting for transfers between devices: none -> 28.3 us  [exchange(): return lax.all_to_all(blocks, 'ctx', 0, 0, tiled=True)]
    ppermute x45 -> x23, waiting for transfers between devices: 197 us -> 170 us  [swap_z(): return lax.ppermute(v, 'ctx', [(i, i ^ mask) for i in range(4)])]
    all_to_all x0 -> x6, starting transfers between devices: none -> 26.9 us  [exchange(): return lax.all_to_all(blocks, 'ctx', 0, 0, tiled=True)]
    another operation x4 -> x17, other arithmetic: 0.2 us -> 19.8 us  [the longest x3 5.18 us: on_cores(): jnp.stack([p.total(v, r, True) for p, v, r in zip(gates, gate_side, gate_...]
  transfers between devices with their start and end apart: 121 -> 74, of which waited for: 42 -> 36; matrix products, arithmetic and copies ran while one was open for 22% -> 19% of each run, Pallas kernels for 12% -> 15%
where the time goes in v2:
time: 898 us; the launch traced here: 888 us
  waiting for transfers between devices  296 us (33%)
  matrix products  149 us (17%)
  Pallas kernels  141 us (16%)
  starting transfers between devices  104 us (12%)
  other arithmetic  99.3 us (11%)
  local copies, waits for them, and re-layouts  92.3 us (10%)
    ppermute x23, waiting for transfers between devices, swap_z(): return lax.ppermute(v, 'ctx', [(i, i ^ mask) for i in range(4)])  170 us
    ppermute x45, waiting for transfers between devices, swap_dp(): return lax.ppermute(v, 'dp', [(i, i ^ bit) for i in range(8)])  98.3 us
    pallas_call x2, Pallas kernels, attend_back(): pl.pallas_call(functools.partial(attend_back_kernel, heads), out_shape=(j...  66.5 us
    dot_general x5, matrix products, right_tdot(): lax.dot_general(left, right, (((1,), (1,)), ((), ())), preferred_element_...  53.8 us
    dot_general x6, matrix products, matmul(): return jnp.dot(left, right, preferred_element_type=jnp.float32)  52.7 us
    dot_general x5, matrix products, left_tdot(): lax.dot_general(left, right, (((0,), (0,)), ((), ())), preferred_element_...  42.5 us
    ppermute x45, starting transfers between devices, swap_dp(): return lax.ppermute(v, 'dp', [(i, i ^ bit) for i in range(8)])  38.7 us
    ppermute x23, starting transfers between devices, swap_z(): return lax.ppermute(v, 'ctx', [(i, i ^ mask) for i in range(4)])  38.2 us
  transfers between devices with their start and end apart: 74, of which 36 were waited for; matrix products, arithmetic and copies ran while one was open for 19% of the time, Pallas kernels for 15%

profile of v2, /device:TPU:0, one launch (start us, length us, event | category | flops | bytes accessed | tf_op | source)
XLA Modules:
  0.0 888.1 jit_solution(213618122977106870)
XLA Ops:
  21.6 16.1 %all-to-all-done.refs_0_ = bf16[4,40,2560]{2,1,0:T(8,128)(2,1)S(1)} async-done(((bf16[4,40,2560]{2,1,0:T(8,128)(2,1)}), bf16[4,40,2560]{2,1,0:T(8,128)(2,1)S(1)}, u32[]{:S(2)}, u32[]{:S(2)}) %all-to-all-start) | async-done | bytes 819232 | tf_op jit(solution)/shard_map/all_to_all | solution.py:570
  47.0 11.7 %collective-permute-done.3.refs_3_ = bf16[6,40,2560]{2,1,0:T(8,128)(2,1)S(1)} collective-permute-done((bf16[6,40,2560]{2,1,0:T(8,128)(2,1)S(1)}, bf16[6,40,2560]{2,1,0:T(8,128)(2,1)S(1)}, u32[]{:S(2)}, u32[]{:S(2)}) %collective-permute-start.3) | collective-permute-done | bytes 1228832 | tf_op jit(solution)/shard_map/ppermute | solution.py:276
  69.0 54.6 %collective-permute-done.6.refs_1_ = bf16[512,1280]{1,0:T(8,128)(2,1)S(1)} collective-permute-done((bf16[512,1280]{1,0:T(8,128)(2,1)S(1)}, bf16[512,1280]{1,0:T(8,128)(2,1)S(1)}, u32[]{:S(2)}, u32[]{:S(2)}) %collective-permute-start.6) | collective-permute-done | bytes 1310752 | tf_op jit(solution)/shard_map/ppermute | solution.py:276
  132.7 17.8 %collective-permute-done.11.refs_4_.refs_7_ = bf16[5,40,2560]{2,1,0:T(8,128)(2,1)S(1)} collective-permute-done((bf16[5,40,2560]{2,1,0:T(8,128)(2,1)S(1)}, bf16[5,40,2560]{2,1,0:T(8,128)(2,1)S(1)}, u32[]{:S(2)}, u32[]{:S(2)}) %collective-permute-start.11) | collective-permute-done | bytes 1024032 | tf_op jit(solution)/shard_map/ppermute | solution.py:272
  154.6 27.7 %collective-permute-done.8.refs_8_ = bf16[6,40,2560]{2,1,0:T(8,128)(2,1)S(1)} collective-permute-done((bf16[6,40,2560]{2,1,0:T(8,128)(2,1)S(1)}, bf16[6,40,2560]{2,1,0:T(8,128)(2,1)S(1)}, u32[]{:S(2)}, u32[]{:S(2)}) %collective-permute-start.8) | collective-permute-done | bytes 1228832 | tf_op jit(solution)/shard_map/ppermute | solution.py:276
  225.9 21.6 %attend.2 = (f32[2048,192]{1,0:T(8,128)}, bf16[2048,192]{1,0:T(8,128)(2,1)}, bf16[3,2048,128]{2,1,0:T(8,128)(2,1)}, bf16[3,2048,128]{2,1,0:T(8,128)(2,1)}, bf16[3,2048,128]{2,1,0:T(8,128)(2,1)}) custom-call(s32[1]{0:T(128)} %copy.83.length_ref, f32[2048,640]{1,0:T(8,128)} %fusion.5.qkv_ref, f32[1,192]{1,0:T(1,128)} %slice.269.gain_ref), custom_call_target="tpu_custom_call" | custom-call | flops 12582912 | bytes 8388608 | tf_op jit(solution)/shard_map/attend/pallas_call | solution.py:140
  247.5 16.4 %collective-permute-done.17.refs_12_ = bf16[9,40,2560]{2,1,0:T(8,128)(2,1)S(1)} collective-permute-done((bf16[9,40,2560]{2,1,0:T(8,128)(2,1)}, bf16[9,40,2560]{2,1,0:T(8,128)(2,1)S(1)}, u32[]{:S(2)}, u32[]{:S(2)}) %collective-permute-start.17) | collective-permute-done | bytes 1843232 | tf_op jit(solution)/shard_map/ppermute | solution.py:272
  274.3 14.4 %attend.3 = (f32[2048,128]{1,0:T(8,128)}, bf16[2048,128]{1,0:T(8,128)(2,1)}, bf16[2,2048,128]{2,1,0:T(8,128)(2,1)}, bf16[2,2048,128]{2,1,0:T(8,128)(2,1)}, bf16[2,2048,128]{2,1,0:T(8,128)(2,1)}) custom-call(s32[1]{0:T(128)} %copy.83.length_ref, f32[2048,384]{1,0:T(8,128)} %fusion.31.qkv_ref, f32[1,128]{1,0:T(1,128)} %slice.270.gain_ref), custom_call_target="tpu_custom_call" | custom-call | flops 8388608 | bytes 8388608 | tf_op jit(solution)/shard_map/attend/pallas_call | solution.py:140
  297.3 15.2 %spread.1 = (bf16[2,2,2,4,40,2560]{5,4,3,2,1,0:T(8,128)(2,1)}, bf16[2,2,2,4,40,2560]{5,4,3,2,1,0:T(8,128)(2,1)}, bf16[2,2,4,2,2,40,1280]{6,5,4,3,2,1,0:T(8,128)(2,1)}) custom-call(s32[3]{0:T(128)} %pad_add_fusion.2.coord_ref, bf16[6,40,2560]{2,1,0:T(8,128)(2,1)} %bitcast.353, bf16[6,40,2560]{2,1,0:T(8,128)(2,1)} %collective-permute-done.1.refs_1_, ...), custom_call_target="tpu_custom_call" | custom-call | bytes 41943040 | tf_op jit(solution)/shard_map/spread/pallas_call | solution.py:504
  326.6 12.9 %fusion.87 = f32[1024,2560]{1,0:T(8,128)} fusion(bf16[1024,1280]{1,0:T(8,128)(2,1)} %join.2, bf16[1280,2560]{1,0:T(8,128)(2,1)} %bitcast.374), kind=kOutput, calls=%fused_computation.268 | convolution fusion | flops 6710886400 | bytes 19660800 | tf_op jit(solution)/shard_map/dot_general | solution.py:27
  339.5 15.0 %multiply_convert_fusion.2 = (bf16[1024,2560]{1,0:T(8,128)(2,1)S(1)}, f32[1024,2560]{1,0:T(8,128)}) fusion(f32[2560]{0:T(1024)S(1)} %mul.290, f32[1024,2560]{1,0:T(8,128)} %fusion.87, f32[2560]{0:T(1024)S(1)} %mul.293, bf16[1024,1280]{1,0:T(8,128)(2,1)S(1)} %copy-done.35, bf16[1280,2560]{1,0:T(8,128)(2,1)} %bitcast.372), kind=kOutput, calls=%fused_computation.8 | convolution fusion | flops 6731857920 | bytes 35409920 | tf_op jit(solution)/shard_map/dot_general | solution.py:27
  391.2 10.0 %convolution_convert_fusion.2 = bf16[2560,1280]{1,0:T(8,128)(2,1)S(1)} fusion(bf16[1024,2560]{1,0:T(8,128)(2,1)} %copy-done.74, bf16[1024,1280]{1,0:T(8,128)(2,1)} %join.3), kind=kOutput, calls=%fused_computation.2 | convolution fusion | flops 6714163200 | bytes 14417920 | tf_op jit(solution)/shard_map/dot_general | solution.py:31
  409.4 21.9 %multiply_reduce_fusion.1 = (f32[2560]{0:T(1024)S(1)}, f32[2560]{0:T(1024)S(1)}, f32[1024,2560]{1,0:T(8,128)}, bf16[1024,2560]{1,0:T(8,128)(2,1)}) fusion(f32[1024,2560]{1,0:T(8,128)} %get-tuple-element.405, f32[1024,2560]{1,0:T(8,128)} %fusion.87, f32[2560]{0:T(1024)S(1)} %mul.293, f32[2560]{0:T(1024)S(1)} %mul.290, bf16[1024,1280]{1,0:T(8,128)(2,1)} %join.3, ...), kind=kOutput, calls=%fused_computation.4 | convolution fusion | flops 6760688640 | bytes 45916160 | tf_op jit(solution)/shard_map/dot_general | solution.py:37
  452.0 10.1 %convolution_convert_fusion.1 = bf16[1280,2560]{1,0:T(8,128)(2,1)S(1)} fusion(bf16[1024,1280]{1,0:T(8,128)(2,1)S(1)} %copy-done.36, bf16[1024,2560]{1,0:T(8,128)(2,1)} %get-tuple-element.236), kind=kOutput, calls=%fused_computation.1 | convolution fusion | flops 6714163200 | bytes 14417920 | tf_op jit(solution)/shard_map/dot_general | solution.py:31
  469.7 12.3 %fusion.89 = f32[1024,1280]{1,0:T(8,128)} fusion(bf16[1024,2560]{1,0:T(8,128)(2,1)} %multiply_convert_fusion, bf16[1280,2560]{1,0:T(8,128)(2,1)} %bitcast.375), kind=kOutput, calls=%fused_computation.270 | convolution fusion | flops 6710886400 | bytes 17039360 | tf_op jit(solution)/shard_map/dot_general | solution.py:37
  484.6 11.8 %convolution_add_fusion = f32[1024,1280]{1,0:T(8,128)S(1)} fusion(f32[1024,1280]{1,0:T(8,128)} %fusion.89, bf16[1024,2560]{1,0:T(8,128)(2,1)} %get-tuple-element.236, bf16[1280,2560]{1,0:T(8,128)(2,1)} %bitcast.373), kind=kOutput, calls=%fused_computation.14 | convolution fusion | flops 6712197120 | bytes 22282240 | tf_op jit(solution)/shard_map/dot_general | solution.py:37
  535.2 9.7 %convolution_convert_fusion = bf16[1280,2560]{1,0:T(8,128)(2,1)S(1)} fusion(bf16[1024,1280]{1,0:T(8,128)(2,1)S(1)} %copy-done.37, bf16[1024,2560]{1,0:T(8,128)(2,1)} %multiply_convert_fusion), kind=kOutput, calls=%fused_computation | convolution fusion | flops 6714163200 | bytes 14417920 | tf_op jit(solution)/shard_map/dot_general | solution.py:31
  582.5 14.7 %collective-permute-done.38 = bf16[4,40,2560]{2,1,0:T(8,128)(2,1)} collective-permute-done((bf16[4,40,2560]{2,1,0:T(8,128)(2,1)}, bf16[4,40,2560]{2,1,0:T(8,128)(2,1)}, u32[]{:S(2)}, u32[]{:S(2)}) %collective-permute-start.38) | collective-permute-done | bytes 819232 | tf_op jit(solution)/shard_map/ppermute | solution.py:272
  616.4 39.5 %attend_back.2 = (bf16[2048,640]{1,0:T(8,128)(2,1)}, f32[1,192]{1,0:T(1,128)}) custom-call(s32[1]{0:T(128)} %copy.83.length_ref, f32[2048,640]{1,0:T(8,128)} %fusion.5.qkv_ref, f32[1,192]{1,0:T(1,128)} %slice.269.gain_ref, f32[2048,192]{1,0:T(8,128)} %get-tuple-element.226.mixed_ref, bf16[2048,192]{1,0:T(8,128)(2,1)} %bitcast.354, ...), custom_call_target="tpu_custom_call" | custom-call | flops 12582912 | bytes 8388608 | tf_op jit(solution)/shard_map/attend_back/pallas_call | solution.py:250
  673.1 27.0 %attend_back.3 = (bf16[2048,384]{1,0:T(8,128)(2,1)}, f32[1,128]{1,0:T(1,128)}) custom-call(s32[1]{0:T(128)} %copy.83.length_ref, f32[2048,384]{1,0:T(8,128)} %fusion.31.qkv_ref, f32[1,128]{1,0:T(1,128)} %slice.270.gain_ref, f32[2048,128]{1,0:T(8,128)} %get-tuple-element.225.mixed_ref, bf16[2048,128]{1,0:T(8,128)(2,1)} %bitcast.359, ...), custom_call_target="tpu_custom_call" | custom-call | flops 8388608 | bytes 8388608 | tf_op jit(solution)/shard_map/attend_back/pallas_call | solution.py:250
  734.6 19.8 %collective-permute-done.56 = bf16[2,40,2560]{2,1,0:T(8,128)(2,1)S(1)} collective-permute-done((bf16[2,40,2560]{2,1,0:T(8,128)(2,1)}, bf16[2,40,2560]{2,1,0:T(8,128)(2,1)S(1)}, u32[]{:S(2)}, u32[]{:S(2)}) %collective-permute-start.56) | collective-permute-done | bytes 409632 | tf_op jit(solution)/shard_map/ppermute | solution.py:276
  769.3 26.7 %collective-permute-done.58 = bf16[256,1280]{1,0:T(8,128)(2,1)S(1)} collective-permute-done((bf16[256,1280]{1,0:T(8,128)(2,1)S(1)}, bf16[256,1280]{1,0:T(8,128)(2,1)S(1)}, u32[]{:S(2)}, u32[]{:S(2)}) %collective-permute-start.58) | collective-permute-done | bytes 655392 | tf_op jit(solution)/shard_map/ppermute | solution.py:276
  842.8 11.2 %all-to-all-done.5 = bf16[4,40,2304]{2,1,0:T(8,128)(2,1)S(1)} async-done(((bf16[4,40,2304]{2,1,0:T(8,128)(2,1)}), bf16[4,40,2304]{2,1,0:T(8,128)(2,1)S(1)}, u32[]{:S(2)}, u32[]{:S(2)}) %all-to-all-start.5) | async-done | bytes 737312 | tf_op jit(solution)/shard_map/all_to_all | solution.py:570
  857.0 16.4 %collective-permute-done.67 = bf16[256,1280]{1,0:T(8,128)(2,1)} collective-permute-done((bf16[256,1280]{1,0:T(8,128)(2,1)S(1)}, bf16[256,1280]{1,0:T(8,128)(2,1)}, u32[]{:S(2)}, u32[]{:S(2)}) %collective-permute-start.67) | collective-permute-done | bytes 655392 | tf_op jit(solution)/shard_map/ppermute | solution.py:276
  (503 shorter events, 427.0 us)
Async XLA Ops:
  19.6 39.1 %collective-permute-start.3 = (bf16[6,40,2560]{2,1,0:T(8,128)(2,1)S(1)}, bf16[6,40,2560]{2,1,0:T(8,128)(2,1)S(1)}, u32[]{:S(2)}, u32[]{:S(2)}) collective-permute-start(bf16[6,40,2560]{2,1,0:T(8,128)(2,1)S(1)} %bitcast.351), channel_id=1, source_target_pairs={{0,1},{1,0},{2,3},{3,2},{4,5},{5,4},{6,7},{7,6},{8,9},{9,8},{10,11... | collective-permute-start | bytes 3686408 | tf_op jit(solution)/shard_map/ppermute | solution.py:276
  63.0 60.6 %collective-permute-start.4 = (bf16[13,40,2560]{2,1,0:T(8,128)(2,1)S(1)}, bf16[13,40,2560]{2,1,0:T(8,128)(2,1)S(1)}, u32[]{:S(2)}, u32[]{:S(2)}) collective-permute-start(bf16[13,40,2560]{2,1,0:T(8,128)(2,1)S(1)} %get-tuple-element.379), channel_id=1, source_target_pairs={{0,8},{4,12},{8,0},{12,4},{16,24},{20,28},{24,16},{28,20},{1,9},{5... | collective-permute-start | bytes 7987208 | tf_op jit(solution)/shard_map/ppermute | solution.py:272
  64.6 59.1 %collective-permute-start.5 = (bf16[13,40,2560]{2,1,0:T(8,128)(2,1)S(1)}, bf16[13,40,2560]{2,1,0:T(8,128)(2,1)S(1)}, u32[]{:S(2)}, u32[]{:S(2)}) collective-permute-start(bf16[13,40,2560]{2,1,0:T(8,128)(2,1)S(1)} %get-tuple-element.378), channel_id=1, source_target_pairs={{0,16},{4,20},{8,24},{12,28},{16,0},{20,4},{24,8},{28,12},{1,17},{... | collective-permute-start | bytes 7987208 | tf_op jit(solution)/shard_map/ppermute | solution.py:272
  66.1 57.5 %collective-permute-start.6 = (bf16[512,1280]{1,0:T(8,128)(2,1)S(1)}, bf16[512,1280]{1,0:T(8,128)(2,1)S(1)}, u32[]{:S(2)}, u32[]{:S(2)}) collective-permute-start(bf16[512,1280]{1,0:T(8,128)(2,1)S(1)} %bitcast.329), channel_id=1, source_target_pairs={{0,1},{1,0},{2,3},{3,2},{4,5},{5,4},{6,7},{7,6},{8,9},{9,8},{10,11... | collective-permute-start | bytes 3932168 | tf_op jit(solution)/shard_map/ppermute | solution.py:276
  66.4 57.2 %collective-permute-start.7 = (bf16[512,1280]{1,0:T(8,128)(2,1)S(1)}, bf16[512,1280]{1,0:T(8,128)(2,1)S(1)}, u32[]{:S(2)}, u32[]{:S(2)}) collective-permute-start(bf16[512,1280]{1,0:T(8,128)(2,1)S(1)} %bitcast.330), channel_id=1, source_target_pairs={{0,2},{1,3},{2,0},{3,1},{4,6},{5,7},{6,4},{7,5},{8,10},{9,11},{10,... | collective-permute-start | bytes 3932168 | tf_op jit(solution)/shard_map/ppermute | solution.py:276
  125.1 58.2 %collective-permute-start.12 = (bf16[12,40,2560]{2,1,0:T(8,128)(2,1)S(1)}, bf16[12,40,2560]{2,1,0:T(8,128)(2,1)}, u32[]{:S(2)}, u32[]{:S(2)}) collective-permute-start(bf16[12,40,2560]{2,1,0:T(8,128)(2,1)S(1)} %pad_maximum_fusion.4), channel_id=1, source_target_pairs={{0,4},{4,0},{8,12},{12,8},{16,20},{20,16},{24,28},{28,24},{1,5},{5... | collective-permute-start | bytes 7372808 | tf_op jit(solution)/shard_map/ppermute | solution.py:272
  127.3 56.0 %collective-permute-start.9 = (bf16[512,1280]{1,0:T(8,128)(2,1)S(1)}, bf16[512,1280]{1,0:T(8,128)(2,1)S(1)}, u32[]{:S(2)}, u32[]{:S(2)}) collective-permute-start(bf16[512,1280]{1,0:T(8,128)(2,1)S(1)} %collective-permute-done.7.refs_2_), channel_id=1, source_target_pairs={{0,1},{1,0},{2,3},{3,2},{4,5},{5,4},{6,7},{7,6},{8,9},{9,8},{10,11... | collective-permute-start | bytes 3932168 | tf_op jit(solution)/shard_map/ppermute | solution.py:276
  129.3 53.0 %collective-permute-start.8 = (bf16[6,40,2560]{2,1,0:T(8,128)(2,1)S(1)}, bf16[6,40,2560]{2,1,0:T(8,128)(2,1)S(1)}, u32[]{:S(2)}, u32[]{:S(2)}) collective-permute-start(bf16[6,40,2560]{2,1,0:T(8,128)(2,1)S(1)} %bitcast.352), channel_id=1, source_target_pairs={{0,2},{1,3},{2,0},{3,1},{4,6},{5,7},{6,4},{7,5},{8,10},{9,11},{10,... | collective-permute-start | bytes 3686408 | tf_op jit(solution)/shard_map/ppermute | solution.py:276
  222.1 41.7 %collective-permute-start.17 = (bf16[9,40,2560]{2,1,0:T(8,128)(2,1)}, bf16[9,40,2560]{2,1,0:T(8,128)(2,1)S(1)}, u32[]{:S(2)}, u32[]{:S(2)}) collective-permute-start(bf16[9,40,2560]{2,1,0:T(8,128)(2,1)} %get-tuple-element.385), channel_id=1, source_target_pairs={{0,8},{4,12},{8,0},{12,4},{16,24},{20,28},{24,16},{28,20},{1,9},{5... | collective-permute-start | bytes 5529608 | tf_op jit(solution)/shard_map/ppermute | solution.py:272
  223.6 41.5 %collective-permute-start.18 = (bf16[9,40,2560]{2,1,0:T(8,128)(2,1)}, bf16[9,40,2560]{2,1,0:T(8,128)(2,1)}, u32[]{:S(2)}, u32[]{:S(2)}) collective-permute-start(bf16[9,40,2560]{2,1,0:T(8,128)(2,1)} %get-tuple-element.384), channel_id=1, source_target_pairs={{0,16},{4,20},{8,24},{12,28},{16,0},{20,4},{24,8},{28,12},{1,17},{... | collective-permute-start | bytes 5529608 | tf_op jit(solution)/shard_map/ppermute | solution.py:272
  406.9 38.2 %collective-permute-start.24 = (bf16[2,4,80,1280]{3,2,1,0:T(8,128)(2,1)}, bf16[2,4,80,1280]{3,2,1,0:T(8,128)(2,1)}, u32[]{:S(2)}, u32[]{:S(2)}) collective-permute-start(bf16[2,4,80,1280]{3,2,1,0:T(8,128)(2,1)} %dynamic-slice_bitcast_fusion.2), channel_id=1, source_target_pairs={{0,8},{4,12},{8,0},{12,4},{16,24},{20,28},{24,16},{28,20},{1,9},{5... | collective-permute-start | bytes 4915208 | tf_op jit(solution)/shard_map/ppermute | solution.py:272
  408.1 37.9 %collective-permute-start.25 = (bf16[2,4,80,1280]{3,2,1,0:T(8,128)(2,1)}, bf16[2,4,80,1280]{3,2,1,0:T(8,128)(2,1)}, u32[]{:S(2)}, u32[]{:S(2)}) collective-permute-start(bf16[2,4,80,1280]{3,2,1,0:T(8,128)(2,1)} %dynamic-slice_bitcast_fusion.1), channel_id=1, source_target_pairs={{0,16},{4,20},{8,24},{12,28},{16,0},{20,4},{24,8},{28,12},{1,17},{... | collective-permute-start | bytes 4915208 | tf_op jit(solution)/shard_map/ppermute | solution.py:272
  531.9 50.7 %collective-permute-start.41 = (bf16[2,80,1280]{2,1,0:T(8,128)(2,1)}, bf16[2,80,1280]{2,1,0:T(8,128)(2,1)}, u32[]{:S(2)}, u32[]{:S(2)}) collective-permute-start(bf16[2,80,1280]{2,1,0:T(8,128)(2,1)} %fusion.48), channel_id=1, source_target_pairs={{0,2},{1,3},{2,0},{3,1},{4,6},{5,7},{6,4},{7,5},{8,10},{9,11},{10,... | collective-permute-start | bytes 1228808 | tf_op jit(solution)/shard_map/ppermute | solution.py:276
  600.3 55.6 %collective-permute-start.46 = (bf16[4,40,2560]{2,1,0:T(8,128)(2,1)}, bf16[4,40,2560]{2,1,0:T(8,128)(2,1)}, u32[]{:S(2)}, u32[]{:S(2)}) collective-permute-start(bf16[4,40,2560]{2,1,0:T(8,128)(2,1)} %fusion.11), channel_id=1, source_target_pairs={{0,8},{4,12},{8,0},{12,4},{16,24},{20,28},{24,16},{28,20},{1,9},{5... | collective-permute-start | bytes 2457608 | tf_op jit(solution)/shard_map/ppermute | solution.py:272
  603.9 52.0 %collective-permute-start.45 = (bf16[4,40,2560]{2,1,0:T(8,128)(2,1)}, bf16[4,40,2560]{2,1,0:T(8,128)(2,1)}, u32[]{:S(2)}, u32[]{:S(2)}) collective-permute-start(bf16[4,40,2560]{2,1,0:T(8,128)(2,1)} %fusion.12), channel_id=1, source_target_pairs={{0,16},{4,20},{8,24},{12,28},{16,0},{20,4},{24,8},{28,12},{1,17},{... | collective-permute-start | bytes 2457608 | tf_op jit(solution)/shard_map/ppermute | solution.py:272
  605.2 50.7 %collective-permute-start.43 = (bf16[4,40,2560]{2,1,0:T(8,128)(2,1)}, bf16[4,40,2560]{2,1,0:T(8,128)(2,1)}, u32[]{:S(2)}, u32[]{:S(2)}) collective-permute-start(bf16[4,40,2560]{2,1,0:T(8,128)(2,1)} %get-tuple-element.273), channel_id=1, source_target_pairs={{0,8},{4,12},{8,0},{12,4},{16,24},{20,28},{24,16},{28,20},{1,9},{5... | collective-permute-start | bytes 2457608 | tf_op jit(solution)/shard_map/ppermute | solution.py:272
  606.1 49.9 %collective-permute-start.44 = (bf16[4,40,2560]{2,1,0:T(8,128)(2,1)}, bf16[4,40,2560]{2,1,0:T(8,128)(2,1)}, u32[]{:S(2)}, u32[]{:S(2)}) collective-permute-start(bf16[4,40,2560]{2,1,0:T(8,128)(2,1)} %get-tuple-element.274), channel_id=1, source_target_pairs={{0,16},{4,20},{8,24},{12,28},{16,0},{20,4},{24,8},{28,12},{1,17},{... | collective-permute-start | bytes 2457608 | tf_op jit(solution)/shard_map/ppermute | solution.py:272
  606.8 49.1 %all-to-all-start.4 = ((bf16[4,512,128]{1,2,0:T(8,128)(2,1)}), bf16[4,512,128]{1,2,0:T(8,128)(2,1)}, u32[]{:S(2)}, u32[]{:S(2)}) async-start(bf16[4,512,128]{1,2,0:T(8,128)(2,1)} %slice.283), calls=%async_computation.4 | async-start | bytes 1048576 | tf_op jit(solution)/shard_map/all_to_all | solution.py:570
  612.2 43.8 %collective-permute-start.47 = (bf16[2,40,2560]{2,1,0:T(8,128)(2,1)}, bf16[2,40,2560]{2,1,0:T(8,128)(2,1)}, u32[]{:S(2)}, u32[]{:S(2)}) collective-permute-start(bf16[2,40,2560]{2,1,0:T(8,128)(2,1)} %dynamic-slice_bitcast_fusion.21), channel_id=1, source_target_pairs={{0,1},{1,0},{2,3},{3,2},{4,5},{5,4},{6,7},{7,6},{8,9},{9,8},{10,11... | collective-permute-start | bytes 1228808 | tf_op jit(solution)/shard_map/ppermute | solution.py:276
  656.0 44.1 %collective-permute-start.52 = (f32[4,4,128]{2,1,0:T(4,128)S(1)}, f32[4,4,128]{2,1,0:T(4,128)S(1)}, u32[]{:S(2)}, u32[]{:S(2)}) collective-permute-start(f32[4,4,128]{2,1,0:T(4,128)S(1)} %fusion.76), channel_id=1, source_target_pairs={{0,16},{4,20},{8,24},{12,28},{16,0},{20,4},{24,8},{28,12},{1,17},{... | collective-permute-start | bytes 24584 | tf_op jit(solution)/shard_map/ppermute | solution.py:272
  662.2 37.9 %collective-permute-start.50 = (bf16[2,40,2560]{2,1,0:T(8,128)(2,1)}, bf16[2,40,2560]{2,1,0:T(8,128)(2,1)}, u32[]{:S(2)}, u32[]{:S(2)}) collective-permute-start(bf16[2,40,2560]{2,1,0:T(8,128)(2,1)} %get-tuple-element.383), channel_id=1, source_target_pairs={{0,1},{1,0},{2,3},{3,2},{4,5},{5,4},{6,7},{7,6},{8,9},{9,8},{10,11... | collective-permute-start | bytes 1228808 | tf_op jit(solution)/shard_map/ppermute | solution.py:276
  662.2 37.9 %collective-permute-start.51 = (bf16[2,40,2560]{2,1,0:T(8,128)(2,1)}, bf16[2,40,2560]{2,1,0:T(8,128)(2,1)}, u32[]{:S(2)}, u32[]{:S(2)}) collective-permute-start(bf16[2,40,2560]{2,1,0:T(8,128)(2,1)} %get-tuple-element.382), channel_id=1, source_target_pairs={{0,1},{1,0},{2,3},{3,2},{4,5},{5,4},{6,7},{7,6},{8,9},{9,8},{10,11... | collective-permute-start | bytes 1228808 | tf_op jit(solution)/shard_map/ppermute | solution.py:276
  835.2 38.2 %collective-permute-start.67 = (bf16[256,1280]{1,0:T(8,128)(2,1)S(1)}, bf16[256,1280]{1,0:T(8,128)(2,1)}, u32[]{:S(2)}, u32[]{:S(2)}) collective-permute-start(bf16[256,1280]{1,0:T(8,128)(2,1)S(1)} %slice.255), channel_id=1, source_target_pairs={{0,1},{1,0},{2,3},{3,2},{4,5},{5,4},{6,7},{7,6},{8,9},{9,8},{10,11... | collective-permute-start | bytes 1966088 | tf_op jit(solution)/shard_map/ppermute | solution.py:276
  837.3 43.8 %collective-permute-start.66 = (bf16[256,1280]{1,0:T(8,128)(2,1)S(1)}, bf16[256,1280]{1,0:T(8,128)(2,1)}, u32[]{:S(2)}, u32[]{:S(2)}) collective-permute-start(bf16[256,1280]{1,0:T(8,128)(2,1)S(1)} %copy-done.59), channel_id=1, source_target_pairs={{0,2},{1,3},{2,0},{3,1},{4,6},{5,7},{6,4},{7,5},{8,10},{9,11},{10,... | collective-permute-start | bytes 1966088 | tf_op jit(solution)/shard_map/ppermute | solution.py:276
  (131 other events, 1767.2 us)

commit v3 on v2

--- a/solution.py
+++ b/solution.py
@@ -53,10 +53,16 @@
 LANES = 128
 
 
-def head_cols(ref, rows, offset):
-    base = offset // LANES * LANES
-    pair = ref[rows, base : min(base + LANES, ref.shape[1])]
-    return pair[:, offset - base : offset - base + HD]
+def same_head(size, value):
+    rows = lax.broadcasted_iota(jnp.int32, (size, size), 0) // HD
+    cols = lax.broadcasted_iota(jnp.int32, (size, size), 1) // HD
+    return jnp.where(rows == cols, value, 0.0).astype(jnp.bfloat16)
+
+
+def over_heads(v, matrix):
+    hi = v.astype(jnp.bfloat16)
+    low = (v - hi.astype(jnp.float32)).astype(jnp.bfloat16)
+    return jnp.dot(hi, matrix, preferred_element_type=jnp.float32) + jnp.dot(low, matrix, preferred_element_type=jnp.float32)
 
 
 def split3(v):
@@ -73,43 +79,44 @@
     length = length_ref[0]
     lane = lax.broadcasted_iota(jnp.int32, (BLK, HD), 1)
 
+    mean = same_head(2 * width, 1.0 / HD)
+    gains = jnp.concatenate([gain_ref[...], gain_ref[...]], axis=1)
+
     def prepare(block, carry):
         start = pl.multiple_of(block * BLK, BLK)
         rows = pl.ds(start, BLK)
         inside = (lax.broadcasted_iota(jnp.int32, (BLK, 1), 0) + start < length).astype(jnp.float32)
         ones = jnp.where(lane < 3, inside, 0.0).astype(jnp.bfloat16)
         nothing = jnp.zeros((BLK, HD), jnp.bfloat16)
+        raw = qkv_ref[rows, : 2 * width]
+        scaled = gains * (raw * lax.rsqrt(over_heads(raw * raw, mean) + eps))
+        qs = scaled[:, :width].astype(jnp.bfloat16) * jnp.bfloat16(HD**-0.5)
+        ks = (scaled[:, width:] * inside).astype(jnp.bfloat16)
+        vs = (qkv_ref[rows, 2 * width : 3 * width] * inside).astype(jnp.bfloat16)
         for head in range(heads):
-            gain = gain_ref[:, head * HD : (head + 1) * HD]
-            q = head_cols(qkv_ref, rows, head * HD)
-            k = head_cols(qkv_ref, rows, width + head * HD)
-            v = head_cols(qkv_ref, rows, 2 * width + head * HD)
-            qn = q * lax.rsqrt(jnp.mean(q * q, axis=-1, keepdims=True) + eps)
-            kn = k * lax.rsqrt(jnp.mean(k * k, axis=-1, keepdims=True) + eps)
-            qs = (gain * qn).astype(jnp.bfloat16) * jnp.bfloat16(HD**-0.5)
-            ks = (gain * kn * inside).astype(jnp.bfloat16)
-            vs = (v * inside).astype(jnp.bfloat16)
-            qa_ref[head, rows, :] = jnp.concatenate([qs, nothing], axis=1)
-            ka_ref[head, rows, :] = jnp.concatenate([ks, ones], axis=1)
-            va_ref[head, rows, :] = jnp.concatenate([vs, ones], axis=1)
+            cols = slice(head * HD, (head + 1) * HD)
+            qa_ref[head, rows, :] = jnp.concatenate([qs[:, cols], nothing], axis=1)
+            ka_ref[head, rows, :] = jnp.concatenate([ks[:, cols], ones], axis=1)
+            va_ref[head, rows, :] = jnp.concatenate([vs[:, cols], ones], axis=1)
         return carry
 
     lax.fori_loop(0, tokens // BLK, prepare, 0)
-    causal = lax.broadcasted_iota(jnp.int32, (BLK, BLK), 1) <= lax.broadcasted_iota(jnp.int32, (BLK, BLK), 0)
+    part = BLK // 2
+    place = lax.broadcasted_iota(jnp.int32, (BLK, part), 0) - lax.broadcasted_iota(jnp.int32, (BLK, part), 1)
 
     def per_head(head, carry):
         for qi in range(tokens // BLK):
             rows = pl.ds(qi * BLK, BLK)
             q = qa_ref[head, rows, :]
             acc = jnp.zeros((BLK, LANES), jnp.float32)
-            for ki in range(qi + 1):
-                keys = pl.ds(ki * BLK, BLK)
+            for ki in range(2 * (qi + 1)):
+                keys = pl.ds(ki * part, part)
                 scores = lax.dot_general(
                     q, ka_ref[head, keys, :], (((1,), (1,)), ((), ())), preferred_element_type=jnp.float32
                 )
                 weights = jnp.exp(scores)
-                if ki == qi:
-                    weights = jnp.where(causal, weights, 0.0)
+                if ki >= 2 * qi:
+                    weights = jnp.where(place >= (ki - 2 * qi) * part, weights, 0.0)
                 acc = acc + jnp.dot(
                     weights.astype(jnp.bfloat16), va_ref[head, keys, :], preferred_element_type=jnp.float32
                 )
@@ -159,22 +166,26 @@
 
 def attend_back_kernel(
     heads, length_ref, qkv_ref, gain_ref, mixed_ref, cot_ref, qa_ref, ka_ref, va_ref,
-    grads_ref, gain_grad_ref, doa_ref, dq_ref, dk_ref, dv_ref,
+    grads_ref, gain_grad_ref, doa_ref, dq_ref, dk_ref, dv_ref, raw_ref, sem,
 ):
     tokens = qkv_ref.shape[0]
     width = heads * HD
     length = length_ref[0]
     lane = lax.broadcasted_iota(jnp.int32, (BLK, HD), 1)
+    raw_copy = pltpu.make_async_copy(qkv_ref.at[:, pl.ds(0, 2 * width)], raw_ref, sem)
+    raw_copy.start()
+    minus = same_head(width, -1.0)
 
     def prepare(block, carry):
         rows = pl.ds(pl.multiple_of(block * BLK, BLK), BLK)
+        d_mixed = cot_ref[rows, :]
+        hi, mid, low = split3(over_heads(d_mixed.astype(jnp.float32) * mixed_ref[rows, :], minus))
         for head in range(heads):
-            d_mixed = head_cols(cot_ref, rows, head * HD)
-            mixed = head_cols(mixed_ref, rows, head * HD)
-            delta = jnp.sum(d_mixed.astype(jnp.float32) * mixed, axis=-1, keepdims=True)
-            hi, mid, low = split3(-delta)
-            extra = jnp.where(lane == 0, hi, jnp.where(lane == 1, mid, jnp.where(lane == 2, low, jnp.zeros_like(low))))
-            doa_ref[head, rows, :] = jnp.concatenate([d_mixed, extra], axis=1)
+            cols = slice(head * HD, (head + 1) * HD)
+            extra = jnp.where(
+                lane == 0, hi[:, cols], jnp.where(lane == 1, mid[:, cols], jnp.where(lane == 2, low[:, cols], jnp.zeros_like(low[:, cols])))
+            )
+            doa_ref[head, rows, :] = jnp.concatenate([d_mixed[:, cols], extra], axis=1)
         return carry
 
     lax.fori_loop(0, tokens // BLK, prepare, 0)
@@ -210,35 +221,32 @@
 
     lax.fori_loop(0, heads, per_head, 0)
 
+    raw_copy.wait()
+    mean = same_head(2 * width, 1.0 / HD)
+    gains = jnp.concatenate([gain_ref[...], gain_ref[...]], axis=1)
+    scale = jnp.where(lax.broadcasted_iota(jnp.int32, (1, 2 * width), 1) < width, HD**-0.5, 1.0)
+
     def finish(block, sums):
         start = pl.multiple_of(block * BLK, BLK)
         rows = pl.ds(start, BLK)
         inside = lax.broadcasted_iota(jnp.int32, (BLK, 1), 0) + start < length
-        dqs, dks, dvs, sums_new = [], [], [], []
-        for head in range(heads):
-            gain = gain_ref[:, head * HD : (head + 1) * HD]
-            part = sums[head]
-            for offset, ref, outs, scale in ((0, dq_ref, dqs, HD**-0.5), (width, dk_ref, dks, 1.0)):
-                raw = head_cols(qkv_ref, rows, offset + head * HD)
-                factor = lax.rsqrt(jnp.mean(raw * raw, axis=-1, keepdims=True) + eps)
-                normed = raw * factor
-                grad = ref[head, rows, :][:, :HD] * scale
-                part = part + jnp.sum(grad * normed, axis=0, keepdims=True)
-                scaled = grad * gain
-                outs.append(
-                    (factor * (scaled - normed * jnp.mean(scaled * normed, axis=-1, keepdims=True))).astype(jnp.bfloat16)
-                )
-            dvs.append(jnp.where(inside, dv_ref[head, rows, :][:, :HD], 0.0).astype(jnp.bfloat16))
-            sums_new.append(part)
+        grad = jnp.concatenate([ref[head, rows, :][:, :HD] for ref in (dq_ref, dk_ref) for head in range(heads)], axis=1)
+        grad = grad * scale
+        raw = raw_ref[rows, :]
+        factor = lax.rsqrt(over_heads(raw * raw, mean) + eps)
+        normed = raw * factor
+        scaled = grad * gains
+        back = factor * (scaled - normed * over_heads(scaled * normed, mean))
+        grads_ref[rows, : 2 * width] = back.astype(jnp.bfloat16)
+        dv = jnp.concatenate([dv_ref[head, rows, :][:, :HD] for head in range(heads)], axis=1)
+        grads_ref[rows, 2 * width : 3 * width] = jnp.where(inside, dv, 0.0).astype(jnp.bfloat16)
         rest = grads_ref.shape[1] - 3 * width
-        nothing = [jnp.zeros((BLK, rest), jnp.bfloat16)] if rest else []
-        grads_ref[rows, :] = jnp.concatenate(dqs + dks + dvs + nothing, axis=1)
-        return tuple(sums_new)
-
-    sums = lax.fori_loop(
-        0, tokens // BLK, finish, tuple(jnp.zeros((1, HD), jnp.float32) for _ in range(heads))
-    )
-    gain_grad_ref[...] = jnp.concatenate(sums, axis=1)
+        if rest:
+            grads_ref[rows, 3 * width :] = jnp.zeros((BLK, rest), jnp.bfloat16)
+        return sums + jnp.sum(grad * normed, axis=0, keepdims=True)
+
+    sums = lax.fori_loop(0, tokens // BLK, finish, jnp.zeros((1, 2 * width), jnp.float32))
+    gain_grad_ref[...] = sums[:, :width] + sums[:, width:]
 
 
 def attend_back(qkv, gain, length, mixed, d_mixed, qa, ka, va):
@@ -253,9 +261,16 @@
             jax.ShapeDtypeStruct((tokens, three), jnp.bfloat16),
             jax.ShapeDtypeStruct((1, width), jnp.float32),
         ),
-        in_specs=[pl.BlockSpec(memory_space=pltpu.SMEM)] + [vmem] * 7,
+        in_specs=[pl.BlockSpec(memory_space=pltpu.SMEM), pl.BlockSpec(memory_space=pltpu.HBM)] + [vmem] * 6,
         out_specs=(vmem,) * 2,
-        scratch_shapes=[pltpu.VMEM((heads, tokens, LANES), jnp.bfloat16), aug, aug, aug],
+        scratch_shapes=[
+            pltpu.VMEM((heads, tokens, LANES), jnp.bfloat16),
+            aug,
+            aug,
+            aug,
+            pltpu.VMEM((tokens, 2 * width), jnp.float32),
+            pltpu.SemaphoreType.DMA,
+        ],
         compiler_params=pltpu.CompilerParams(vmem_limit_bytes=60 << 20),
         cost_estimate=pl.CostEstimate(
             flops=heads * tokens * tokens, bytes_accessed=8 << 20, transcendentals=0
@@ -284,37 +299,6 @@
     return lax.dynamic_index_in_dim(v, index, axis, keepdims=False)
 
 
-def assemble(pieces, coords, shapes, place):
-    keys = sorted(pieces)
-    count = len(keys)
-
-    def kernel(coord_ref, *refs):
-        outs, sems = refs[count : count + len(shapes)], refs[-1]
-        copies = []
-        for at, key in enumerate(keys):
-            where = place(*[jnp.bitwise_xor(coord_ref[d], key[d]) for d in range(len(key))])
-            for out, (out_ref, (index, rows)) in enumerate(zip(outs, where)):
-                source = refs[at] if rows is None else refs[at].at[pl.ds(*rows)]
-                copies.append(pltpu.make_async_copy(source, out_ref.at[index], sems.at[at, out]))
-        for copy in copies:
-            copy.start()
-        for copy in copies:
-            copy.wait()
-
-    some = pieces[keys[0]]
-    outs = pl.pallas_call(
-        kernel,
-        out_shape=[jax.ShapeDtypeStruct(shape, some.dtype) for shape in shapes],
-        in_specs=[pl.BlockSpec(memory_space=pltpu.SMEM)] + [pl.BlockSpec(memory_space=pltpu.HBM)] * count,
-        out_specs=[pl.BlockSpec(memory_space=pltpu.VMEM)] * len(shapes),
-        scratch_shapes=[pltpu.SemaphoreType.DMA((count, len(shapes)))],
-        compiler_params=pltpu.CompilerParams(vmem_limit_bytes=60 << 20),
-        cost_estimate=pl.CostEstimate(flops=0, bytes_accessed=2 * count * some.size * some.dtype.itemsize, transcendentals=0),
-        name="assemble",
-    )(coords, *[pieces[key] for key in keys])
-    return outs
-
-
 def add_low(a, b):
     return (a.astype(jnp.float32) + b.astype(jnp.float32)).astype(jnp.bfloat16)
 
@@ -327,42 +311,23 @@
     return (a.astype(jnp.float32) + b.astype(jnp.float32) + d.astype(jnp.float32)).astype(jnp.bfloat16)
 
 
-class Plane:
-    def __init__(self, whole, y, x, x_first):
-        self.whole, self.y, self.x, self.x_first = whole, y, x, x_first
+class Cells:
+    def __init__(self, parts, x_first):
+        self.corner, self.side, self.relay, self.keep = parts
         self.links = (XAX, YAX) if x_first else (YAX, XAX)
 
-    def cell(self, y_other, x_other):
-        v = self.whole
-        yy = 1 - self.y if y_other else self.y
-        xx = 1 - self.x if x_other else self.x
-        at = (yy, xx) + (0,) * (v.ndim - 2)
-        return lax.dynamic_slice(v, at, (1, 1) + v.shape[2:]).reshape(v.shape[2:])
-
-    def corner(self):
-        return self.cell(True, True)
-
-    def side(self):
-        return self.cell(not self.x_first, self.x_first)
-
-    def far(self):
-        return lax.dynamic_index_in_dim(
-            self.whole, 1 - (self.x if self.x_first else self.y), 1 if self.x_first else 0, keepdims=False
-        )
-
-    def swap_first(self, v):
+    def first(self, v):
         return swap_dp(v, self.links[0])
 
-    def relay(self, got, alone=False):
-        other = 1 - (self.y if self.x_first else self.x)
-        return add_low(self.cell(self.x_first, not self.x_first), got if alone else pick(got, other))
-
-    def swap_second(self, v):
-        return swap_dp(v, self.links[1])
-
-    def total(self, got, relay, alone=False):
-        here = self.y if self.x_first else self.x
-        return add3(self.cell(False, False), got if alone else pick(got, here), relay)
+    def second(self, corner):
+        return swap_dp(add_low(self.relay, corner), self.links[1])
+
+    def total(self, side, relay):
+        return add3(self.keep, side, relay)
+
+
+def cells(parts):
+    return [Cells(parts[:4], True), Cells(parts[4:], False)]
 
 
 def total3(a, b, d):
@@ -437,29 +402,6 @@
         copy.start()
     for copy in copies:
         copy.wait()
-
-
-def join(upper, lower):
-    rows, width = upper.shape
-
-    def kernel(upper_ref, lower_ref, out_ref, sems):
-        run_copies(
-            [
-                (upper_ref, out_ref.at[pl.ds(0, rows)], sems.at[0]),
-                (lower_ref, out_ref.at[pl.ds(rows, rows)], sems.at[1]),
-            ]
-        )
-
-    return pl.pallas_call(
-        kernel,
-        out_shape=jax.ShapeDtypeStruct((2 * rows, width), upper.dtype),
-        in_specs=[pl.BlockSpec(memory_space=pltpu.HBM)] * 2,
-        out_specs=pl.BlockSpec(memory_space=pltpu.VMEM),
-        scratch_shapes=[pltpu.SemaphoreType.DMA((2,))],
-        compiler_params=pltpu.CompilerParams(vmem_limit_bytes=60 << 20),
-        cost_estimate=pl.CostEstimate(flops=0, bytes_accessed=6 << 20, transcendentals=0),
-        name="join",
-    )(upper, lower)
 
 
 def place(sources, plan, coords, cuts):
@@ -515,7 +457,439 @@
         cost_estimate=pl.CostEstimate(flops=0, bytes_accessed=40 << 20, transcendentals=0),
         name="spread",
     )(coords, *sources)
+    return up, gate, down
+
+
+def spread_last(weights, parts, key, coords):
+    _, share, half = parts[0].shape
+    width = weights[2].shape[-1]
+
+    def kernel(coord_ref, *refs):
+        held_ref, in_sems, out_sems = refs[8:]
+        yy, xx, zz = (jnp.bitwise_xor(coord_ref[d], key[d]) for d in range(3))
+        run_copies([(refs[core], held_ref.at[core], in_sems.at[core]) for core in range(2)])
+        up_ref, gate_ref, down_ref = refs[5:8]
+        copies = []
+        for core in range(2):
+            for kind, ref in enumerate((up_ref, gate_ref)):
+                copies.append((held_ref.at[core, kind], ref.at[yy, xx, core, zz], out_sems.at[core, kind]))
+            for side in range(2):
+                lanes = pl.ds(side * width, width)
+                copies.append((held_ref.at[core, 2, :, lanes], down_ref.at[yy, xx, zz, core, side], out_sems.at[core, 2 + side]))
+        run_copies(copies)
+
+    hbm = pl.BlockSpec(memory_space=pltpu.HBM)
+    up, gate, down = pl.pallas_call(
+        kernel,
+        out_shape=[jax.ShapeDtypeStruct(v.shape, v.dtype) for v in weights],
+        in_specs=[pl.BlockSpec(memory_space=pltpu.SMEM)] + [hbm] * 5,
+        out_specs=[hbm] * 3,
+        scratch_shapes=[
+            pltpu.VMEM((2, 3, share, half), jnp.bfloat16),
+            pltpu.SemaphoreType.DMA((2,)),
+            pltpu.SemaphoreType.DMA((2, 4)),
+        ],
+        input_output_aliases={3: 0, 4: 1, 5: 2},
+        compiler_params=pltpu.CompilerParams(vmem_limit_bytes=BIG),
+        cost_estimate=small_cost(),
+        name="spread_last",
+    )(coords, *parts, *weights)
     return up.reshape(32 * share, half), gate.reshape(32 * share, half), down.reshape(64 * share, width)
+
+BIG = 60 << 20
+TILE = 512
+
+
+def small_cost(bytes_accessed=1 << 20):
+    return pl.CostEstimate(flops=0, bytes_accessed=bytes_accessed, transcendentals=0)
+
+
+def dot(a, b, on_a=1, on_b=0):
+    return lax.dot_general(a, b, (((on_a,), (on_b,)), ((), ())), preferred_element_type=jnp.float32)
+
+
+def ff_forward(own, other, up, gate, down, scale_up, scale_gate):
+    rows, width = own.shape
+    hidden = up.shape[1]
+    steps = hidden // TILE
+
+    def kernel(own_ref, other_ref, up_ref, gate_ref, down_ref, su_ref, sg_ref,
+               upper_ref, gating_ref, hidden_ref, lower_ref, lower_other_ref, turned_ref, both_ref, acc_ref):
+        step = pl.program_id(0)
+
+        @pl.when(step == 0)
+        def _():
+            both_ref[:rows] = own_ref[...]
+            both_ref[rows:] = other_ref[...]
+
+        both = both_ref[...]
+        upper = dot(both, up_ref[...])
+        gating = dot(both, gate_ref[...])
+        upper_ref[...] = upper
+        gating_ref[...] = gating
+        gate_arg = gating * sg_ref[...]
+        hid = ((upper * su_ref[...]) * (gate_arg / (1.0 + jnp.exp(-gate_arg)))).astype(jnp.bfloat16)
+        hidden_ref[...] = hid
+        part = dot(hid, down_ref[...])
+
+        @pl.when(step == 0)
+        def _():
+            acc_ref[...] = part
+
+        @pl.when(step > 0)
+        def _():
+            acc_ref[...] += part
+
+        @pl.when(step == steps - 1)
+        def _():
+            lower_ref[...] = acc_ref[:rows]
+            lower_other_ref[...] = acc_ref[rows:].astype(jnp.bfloat16)
+
+        @pl.when(step == 1)
+        def _():
+            turned_ref[...] = both_ref[...].T
+
+    f32, low = jnp.float32, jnp.bfloat16
+    return pl.pallas_call(
+        kernel,
+        out_shape=(
+            jax.ShapeDtypeStruct((2 * rows, hidden), f32),
+            jax.ShapeDtypeStruct((2 * rows, hidden), f32),
+            jax.ShapeDtypeStruct((2 * rows, hidden), low),
+            jax.ShapeDtypeStruct((rows, width), f32),
+            jax.ShapeDtypeStruct((rows, width), low),
+            jax.ShapeDtypeStruct((width, 2 * rows), low),
+        ),
+        grid=(steps,),
+        in_specs=[
+            pl.BlockSpec((rows, width), lambda i: (0, 0)),
+            pl.BlockSpec((rows, width), lambda i: (0, 0)),
+            pl.BlockSpec((width, TILE), lambda i: (0, i)),
+            pl.BlockSpec((width, TILE), lambda i: (0, i)),
+            pl.BlockSpec((TILE, width), lambda i: (i, 0)),
+            pl.BlockSpec((1, TILE), lambda i: (0, i)),
+            pl.BlockSpec((1, TILE), lambda i: (0, i)),
+        ],
+        out_specs=(
+            pl.BlockSpec((2 * rows, TILE), lambda i: (0, i)),
+            pl.BlockSpec((2 * rows, TILE), lambda i: (0, i)),
+            pl.BlockSpec((2 * rows, TILE), lambda i: (0, i)),
+            pl.BlockSpec((rows, width), lambda i: (0, 0)),
+            pl.BlockSpec((rows, width), lambda i: (0, 0)),
+            pl.BlockSpec((width, 2 * rows), lambda i: (0, 0)),
+        ),
+        scratch_shapes=[pltpu.VMEM((2 * rows, width), low), pltpu.VMEM((2 * rows, width), f32)],
+        compiler_params=pltpu.CompilerParams(vmem_limit_bytes=BIG),
+        cost_estimate=small_cost(),
+        name="ff_forward",
+    )(own, other, up, gate, down, scale_up, scale_gate)
+
+
+def down_back(coords, hidden, own, other):
+    rows, width = own.shape
+    cell = hidden.shape[1] // 4
+    unit = width // 2
+
+    def kernel(coord_ref, hidden_ref, own_ref, other_ref, corner0, side0, relay0, keep0, corner1, side1, relay1, keep1):
+        step = pl.program_id(0)
+        part = dot(hidden_ref[:rows], own_ref[...], 0, 0) + dot(hidden_ref[rows:], other_ref[...], 0, 0)
+        part = part.astype(jnp.bfloat16)
+        for at, refs in enumerate(((corner0, corner1), (relay0, side1), (side0, relay1), (keep0, keep1))):
+
+            @pl.when(step == at)
+            def _():
+                refs[0][...] = part[:, :unit]
+                refs[1][...] = part[:, unit:]
+
+    one = jax.ShapeDtypeStruct((cell, unit), jnp.bfloat16)
+    whole = pl.BlockSpec((rows, width), lambda i, coord_ref: (0, 0))
+    one_spec = pl.BlockSpec((cell, unit), lambda i, coord_ref: (0, 0))
+    return pl.pallas_call(
+        kernel,
+        out_shape=(one,) * 8,
+        grid_spec=pltpu.PrefetchScalarGridSpec(
+            num_scalar_prefetch=1,
+            grid=(4,),
+            in_specs=[
+                pl.BlockSpec((2 * rows, cell), lambda i, coord_ref: (0, jnp.bitwise_xor(2 * coord_ref[0] + coord_ref[1], 3 - i))),
+                whole,
+                whole,
+            ],
+            out_specs=(one_spec,) * 8,
+        ),
+        compiler_params=pltpu.CompilerParams(vmem_limit_bytes=BIG),
+        cost_estimate=small_cost(),
+        name="down_back",
+    )(coords, hidden, own, other)
+
+
+def hidden_back(own, other, down, upper, gating, scale_up, scale_gate):
+    rows, width = own.shape
+    hidden = down.shape[0]
+
+    def kernel(own_ref, other_ref, down_ref, upper_ref, gating_ref, su_ref, sg_ref, d_up_ref, d_gate_ref, us_ref, gs_ref):
+        for part, ref in enumerate((own_ref, other_ref)):
+            at = pl.ds(part * rows, rows)
+            d_hidden = dot(ref[...], down_ref[...], 1, 1)
+            upper, gating = upper_ref[at, :], gating_ref[at, :]
+            su, sg = su_ref[...], sg_ref[...]
+            gate_arg = gating * sg
+            sig = 1.0 / (1.0 + jnp.exp(-gate_arg))
+            d_upper = d_hidden * (gate_arg * sig)
+            d_gate_arg = d_hidden * (upper * su) * (sig * (1.0 + gate_arg * (1.0 - sig)))
+            us = jnp.sum(d_upper * upper, axis=0, keepdims=True)
+            gs = jnp.sum(d_gate_arg * gating, axis=0, keepdims=True)
+            us_ref[...] = us if part == 0 else us_ref[...] + us
+            gs_ref[...] = gs if part == 0 else gs_ref[...] + gs
+            d_up_ref[at, :] = (d_upper * su).astype(jnp.bfloat16)
+            d_gate_ref[at, :] = (d_gate_arg * sg).astype(jnp.bfloat16)
+
+    tall = lambda: pl.BlockSpec((2 * rows, TILE), lambda i: (0, i))
+    flat = lambda: pl.BlockSpec((1, TILE), lambda i: (0, i))
+    return pl.pallas_call(
+        kernel,
+        out_shape=(
+            jax.ShapeDtypeStruct((2 * rows, hidden), jnp.bfloat16),
+            jax.ShapeDtypeStruct((2 * rows, hidden), jnp.bfloat16),
+            jax.ShapeDtypeStruct((1, hidden), jnp.float32),
+            jax.ShapeDtypeStruct((1, hidden), jnp.float32),
+        ),
+        grid=(hidden // TILE,),
+        in_specs=[
+            pl.BlockSpec((rows, width), lambda i: (0, 0)),
+            pl.BlockSpec((rows, width), lambda i: (0, 0)),
+            pl.BlockSpec((TILE, width), lambda i: (i, 0)),
+            tall(), tall(), flat(), flat(),
+        ],
+        out_specs=(tall(), tall(), flat(), flat()),
+        compiler_params=pltpu.CompilerParams(vmem_limit_bytes=BIG),
+        cost_estimate=small_cost(),
+        name="hidden_back",
+    )(own, other, down, upper, gating, scale_up, scale_gate)
+
+
+def wide_back(coords, turned, d_wide):
+    width, tokens = turned.shape
+    hidden = d_wide.shape[1]
+    part = width // 8
+
+    def kernel(coord_ref, turned_ref, d_ref, corner0, side0, relay0, keep0, corner1, side1, relay1, keep1, order_ref):
+        @pl.when(pl.program_id(0) == 0)
+        def _():
+            for at in range(4):
+                start = jnp.bitwise_xor(2 * coord_ref[0] + coord_ref[1], at) * (2 * part)
+                order_ref[pl.ds(at * 2 * part, 2 * part), :] = turned_ref[pl.ds(pl.multiple_of(start, 2 * part), 2 * part), :]
+
+        out = dot(order_ref[...], d_ref[...]).astype(jnp.bfloat16)
+        for at, ref in enumerate((keep0, keep1, side0, relay1, relay0, side1, corner0, corner1)):
+            ref[...] = out[at * part : (at + 1) * part]
+
+    tile = 512
+    one = jax.ShapeDtypeStruct((part, hidden), jnp.bfloat16)
+    one_spec = pl.BlockSpec((part, tile), lambda i: (0, i))
+    return pl.pallas_call(
+        kernel,
+        out_shape=(one,) * 8,
+        grid=(hidden // tile,),
+        in_specs=[
+            pl.BlockSpec(memory_space=pltpu.SMEM),
+            pl.BlockSpec((width, tokens), lambda i: (0, 0)),
+            pl.BlockSpec((tokens, tile), lambda i: (0, i)),
+        ],
+        out_specs=(one_spec,) * 8,
+        scratch_shapes=[pltpu.VMEM((width, tokens), jnp.bfloat16)],
+        compiler_params=pltpu.CompilerParams(vmem_limit_bytes=BIG),
+        cost_estimate=small_cost(),
+        name="wide_back",
+    )(coords, turned, d_wide)
+
+
+def states_back(line, d_qkv0, d_qkv1, weights, local, masks):
+    width = weights.shape[0]
+    low = jnp.bfloat16
+
+    def kernel(line_ref, d0_ref, d1_ref, w_ref, *out_refs):
+        step = pl.program_id(0)
+        split = d0_ref.shape[1]
+        part = dot(d0_ref[...], w_ref[:, :split], 1, 1) + dot(d1_ref[...], w_ref[:, split:], 1, 1)
+        for at, ref in enumerate(out_refs):
+
+            @pl.when(step == at)
+            def _():
+                ref[...] = part.astype(low)
+
+    def block(i, line_ref):
+        mask = masks[-1]
+        for at in range(len(masks) - 1):
+            mask = jnp.where(i == at, masks[at], mask)
+        return (jnp.bitwise_xor(line_ref[0], mask), 0)
+
+    return pl.pallas_call(
+        kernel,
+        out_shape=[jax.ShapeDtypeStruct((local, width), low) for _ in masks],
+        grid_spec=pltpu.PrefetchScalarGridSpec(
+            num_scalar_prefetch=1,
+            grid=(len(masks),),
+            in_specs=[
+                pl.BlockSpec((local, d_qkv0.shape[1]), block),
+                pl.BlockSpec((local, d_qkv1.shape[1]), block),
+                pl.BlockSpec(weights.shape, lambda i, line_ref: (0, 0)),
+            ],
+            out_specs=[pl.BlockSpec((local, width), lambda i, line_ref: (0, 0)) for _ in masks],
+        ),
+        compiler_params=pltpu.CompilerParams(vmem_limit_bytes=BIG),
+        cost_estimate=small_cost(),
+        name="states_back",
+    )(line, d_qkv0, d_qkv1, weights)
+
+
+def project(line, states, weights):
+    local, width = states[0].shape
+    split = COLS[1]
+    rest = weights.shape[1] - split
+
+    def kernel(line_ref, *refs):
+        w_ref, out0_ref, out1_ref = refs[4:]
+        step = pl.program_id(0)
+        for at in range(4):
+
+            @pl.when(step == at)
+            def _():
+                out = dot(refs[at][...], w_ref[...])
+                out0_ref[...] = out[:, :split]
+                out1_ref[...] = out[:, split:]
+
+    spot = lambda i, line_ref: (jnp.bitwise_xor(line_ref[0], i), 0)
+    fixed = lambda i, line_ref: (0, 0)
+    return pl.pallas_call(
+        kernel,
+        out_shape=[jax.ShapeDtypeStruct((4 * local, n), jnp.float32) for n in (split, rest)],
+        grid_spec=pltpu.PrefetchScalarGridSpec(
+            num_scalar_prefetch=1,
+            grid=(4,),
+            in_specs=[pl.BlockSpec((local, width), fixed)] * 4 + [pl.BlockSpec(weights.shape, fixed)],
+            out_specs=[pl.BlockSpec((local, n), spot) for n in (split, rest)],
+        ),
+        compiler_params=pltpu.CompilerParams(vmem_limit_bytes=BIG),
+        cost_estimate=small_cost(),
+        name="project",
+    )(line, *states, weights)
+
+
+def rows_back(coords, states, d_qkv0, d_qkv1, gain_grad, spare):
+    chunk, width = states[0].shape
+    cell = width // 8
+    split, three = d_qkv0.shape[1], d_qkv0.shape[1] + d_qkv1.shape[1]
+    tokens = 4 * chunk
+    steps = 4
+    low = jnp.bfloat16
+
+    def kernel(coord_ref, *refs):
+        d0_ref, d1_ref, gain_ref, keep_ref, send_ref, acc0_ref, acc1_ref = refs[4:]
+        step = pl.program_id(0)
+
+        for at in range(4):
+
+            @pl.when(step == at)
+            def _():
+                for d_ref, acc_ref in ((d0_ref, acc0_ref), (d1_ref, acc1_ref)):
+                    part = dot(refs[at][...], d_ref[...], 0, 0)
+                    acc_ref[...] = part if at == 0 else acc_ref[...] + part
+
+        @pl.when(step == steps - 1)
+        def _():
+            here = lax.broadcasted_iota(jnp.int32, (cell, split), 1) == spare
+            for at in range(4):
+                for ref, core in ((keep_ref, coord_ref[2]), (send_ref, 1 - coord_ref[2])):
+                    start = (2 * jnp.bitwise_xor(2 * coord_ref[0] + coord_ref[1], at) + core) * cell
+                    rows = pl.ds(pl.multiple_of(start, cell), cell)
+                    ref[at, :, :split] = jnp.where(here, gain_ref[rows, :], acc0_ref[rows, :]).astype(low)
+                    ref[at, :, split:] = acc1_ref[rows, :].astype(low)
+
+    shape = jax.ShapeDtypeStruct((4, cell, three), low)
+    return pl.pallas_call(
+        kernel,
+        out_shape=(shape, shape),
+        grid_spec=pltpu.PrefetchScalarGridSpec(
+            num_scalar_prefetch=1,
+            grid=(steps,),
+            in_specs=[pl.BlockSpec((chunk, width), lambda i, coord_ref: (0, 0))] * 4
+            + [
+                pl.BlockSpec((chunk, split), lambda i, coord_ref: (jnp.bitwise_xor(coord_ref[3], i), 0)),
+                pl.BlockSpec((chunk, three - split), lambda i, coord_ref: (jnp.bitwise_xor(coord_ref[3], i), 0)),
+                pl.BlockSpec((width, 1), lambda i, coord_ref: (0, 0)),
+            ],
+            out_specs=(pl.BlockSpec((4, cell, three), lambda i, coord_ref: (0, 0, 0)),) * 2,
+            scratch_shapes=[pltpu.VMEM((width, split), jnp.float32), pltpu.VMEM((width, three - split), jnp.float32)],
+        ),
+        compiler_params=pltpu.CompilerParams(vmem_limit_bytes=BIG),
+        cost_estimate=pl.CostEstimate(flops=2 * tokens * width * three, bytes_accessed=16 << 20, transcendentals=0),
+        name="rows_back",
+    )(coords, *states, d_qkv0, d_qkv1, gain_grad)
+
+
+def interleave(c, own, other):
+    _, share, half = own.shape
+    step = half // 4
+
+    def kernel(core_ref, own_ref, other_ref, up_ref, gate_ref):
+        for core in range(2):
+
+            @pl.when(core_ref[0] == core)
+            def _():
+                for kind, ref in enumerate((up_ref, gate_ref)):
+                    for at in range(4):
+                        here = pl.ds(at * step, step)
+                        ref[:, (2 * at + core) * step : (2 * at + core + 1) * step] = own_ref[kind, :, here]
+                        ref[:, (2 * at + 1 - core) * step : (2 * at + 2 - core) * step] = other_ref[kind, :, here]
+
+    vmem = pl.BlockSpec(memory_space=pltpu.VMEM)
+    return pl.pallas_call(
+        kernel,
+        out_shape=(jax.ShapeDtypeStruct((share, 2 * half), own.dtype),) * 2,
+        in_specs=[pl.BlockSpec(memory_space=pltpu.SMEM), vmem, vmem],
+        out_specs=(vmem,) * 2,
+        compiler_params=pltpu.CompilerParams(vmem_limit_bytes=BIG),
+        cost_estimate=small_cost(),
+        name="interleave",
+    )(c.astype(jnp.int32).reshape(1), own, other)
+
+
+def middle_back(d_up, d_gate, up, gate):
+    tokens, hidden = d_up.shape
+    width = up.shape[0]
+    rows = tokens // 2
+    steps = hidden // TILE
+
+    def kernel(d_up_ref, d_gate_ref, up_ref, gate_ref, own_ref, other_ref, acc_ref):
+        step = pl.program_id(0)
+        part = dot(d_up_ref[...], up_ref[...], 1, 1) + dot(d_gate_ref[...], gate_ref[...], 1, 1)
+
+        @pl.when(step == 0)
+        def _():
+            acc_ref[...] = part
+
+        @pl.when(step > 0)
+        def _():
+            acc_ref[...] += part
+
+        @pl.when(step == steps - 1)
+        def _():
+            own_ref[...] = acc_ref[:rows]
+            other_ref[...] = acc_ref[rows:].astype(jnp.bfloat16)
+
+    tall = lambda n: pl.BlockSpec((n, TILE), lambda i: (0, i))
+    return pl.pallas_call(
+        kernel,
+        out_shape=(jax.ShapeDtypeStruct((rows, width), jnp.float32), jax.ShapeDtypeStruct((rows, width), jnp.bfloat16)),
+        grid=(steps,),
+        in_specs=[tall(tokens), tall(tokens), tall(width), tall(width)],
+        out_specs=(pl.BlockSpec((rows, width), lambda i: (0, 0)),) * 2,
+        scratch_shapes=[pltpu.VMEM((tokens, width), jnp.float32)],
+        compiler_params=pltpu.CompilerParams(vmem_limit_bytes=BIG),
+        cost_estimate=small_cost(),
+        name="middle_back",
+    )(d_up, d_gate, up, gate)
 
 
 def on_cores(
@@ -578,11 +952,12 @@
     xb, yb = on_x(f1, f0y[:3], q0), on_y(f1, f0x[3:], q0)
     s1, s2 = swap_z(states, 1), swap_z(states, 2)
     xb, yb, s1, s2, f0 = fence(xb, yb, s1, s2, f0)
-    f2, s3 = swap_z(f0, 2), swap_z(s2, 1)
+    f2a, s3 = swap_z(f0[:3], 2), swap_z(s2, 1)
     xc, yc = on_x(yb[:3], yb[9:11]), on_y(xb[3:6], xb[11:])
     qc = swap_dp(jnp.concatenate([q0, xb[9:], yb[9:]]), CORE)
-    f2, s3, xc, yc, qc = fence(f2, s3, xc, yc, qc)
-    f2x, f2y, f3 = on_x(f2), on_y(f2), swap_z(f2, 1)
+    f2a, s3, xc, yc, qc, f0 = fence(f2a, s3, xc, yc, qc, f0)
+    f2b, f3a = swap_z(f0[3:], 2), swap_z(f2a, 1)
+    f2ax, f2ay = on_x(f2a), on_y(f2a)
     qd = swap_dp(jnp.concatenate([xc[3:], yc[3:]]), CORE)
     sources = [q0, xb, yb, xc, yc, qc, qd]
     plan = []
@@ -613,39 +988,41 @@
     scale_up = pick(full_uscale, c, 2).reshape(-1)
     scale_gate = pick(full_gscale, c, 2).reshape(-1)
     gain = pick(full_gain.reshape(4, 1, heads_width), z)
-    (whole_states,) = assemble(
-        {(0,): states, (1,): s1, (2,): s2, (3,): s3}, line, [(4, local, width)], lambda zz: [(zz, None)]
-    )
-    whole_states = whole_states.reshape(tokens, width)
+    pieces = (states, s1, s2, s3)
     gains = [gain[:, a * HD : b * HD] for a, b in GROUPS]
-    qkv0 = matmul(whole_states, full_qkv[:, : COLS[1]])
-    qkv1 = matmul(whole_states, full_qkv[:, COLS[1] :])
-    qkv0, qkv1, f2x, f2y, f3 = fence(qkv0, qkv1, f2x, f2y, f3)
-    xd, yd = on_x(f3, f2y[:3]), on_y(f3, f2x[3:])
+    qkv0, qkv1 = project(line, pieces, full_qkv)
+    qkv0, qkv1, f2b, f2ax, f2ay, f3a = fence(qkv0, qkv1, f2b, f2ax, f2ay, f3a)
+    f3b = swap_z(f2b, 1)
+    f2bx, f2by, f3ax, f3ay = on_x(f2b), on_y(f2b), on_x(f3a), on_y(f3a)
     mixed0, heads0, qa0, ka0, va0 = attend(qkv0, gains[0], lengths)
-    heads0, xd, yd, qkv1 = fence(heads0, xd, yd, qkv1)
+    heads0, f3b, f2bx, f2by, f3ax, f3ay, qkv1 = fence(heads0, f3b, f2bx, f2by, f3ax, f3ay, qkv1)
     parts0 = exchange(heads0.reshape(4, local, -1))
-    xe, ye = on_x(yd[:3]), on_y(xd[3:6])
+    f3bx, f3by, f2ac, f2bc = on_x(f3b), on_y(f3b), on_x(f2ay), on_y(f2bx)
     mixed1, heads1, qa1, ka1, va1 = attend(qkv1, gains[1], lengths)
-    heads1, xe, ye, parts0 = fence(heads1, xe, ye, parts0)
+    heads1, f3bx, f3by, f2ac, f2bc, parts0 = fence(heads1, f3bx, f3by, f2ac, f2bc, parts0)
     parts1 = exchange(heads1.reshape(4, local, -1))
-    sources = [f0, f0x, f0y, f1, xb, yb, xc, yc, f2, f2x, f2y, f3, xd, yd, xe, ye]
-    plan = []
-    for mz, (own, at_x, at_y, at_yx, at_xy) in enumerate(
-        (
-            ((0, 0), (1, 0), (2, 0), (4, 6), (5, 6)),
-            ((3, 0), (4, 0), (5, 0), (6, 0), (7, 0)),
-            ((8, 0), (9, 0), (10, 0), (12, 6), (13, 6)),
-            ((11, 0), (12, 0), (13, 0), (14, 0), (15, 0)),
-        )
-    ):
-        for core in range(2):
-            for key, (array, plane) in (((0, 0), own), ((0, 1), at_x), ((1, 0), at_y)):
-                plan.append((key + (mz,), array, plane + 3 * core, core))
-            array, plane = (at_yx, at_xy)[core]
-            plan.append(((1, 1, mz), array, plane, core))
-    full_up, full_gate, full_down = spread(sources, plan, chip, width)
-    full_up, full_gate, full_down, parts1 = fence(full_up, full_gate, full_down, parts1)
+    f3ac, f3bc = on_x(f3ay), on_y(f3bx)
+    sources = [f0, f0x, f0y, f1, xb, yb, xc, yc]
+    sources += [f2a, f2ax, f2ay, f2ac, f2b, f2bx, f2by, f2bc, f3a, f3ax, f3ay, f3b, f3bx, f3by]
+    chips = ((0, 0), (0, 1), (1, 0), (1, 1))
+    spots = {
+        (0, 0): ((0, 0), (1, 0), (2, 0), (4, 6)),
+        (0, 1): ((0, 3), (1, 3), (2, 3), (5, 6)),
+        (1, 0): ((3, 0), (4, 0), (5, 0), (6, 0)),
+        (1, 1): ((3, 3), (4, 3), (5, 3), (7, 0)),
+        (2, 0): ((8, 0), (9, 0), (10, 0), (11, 0)),
+        (2, 1): ((12, 0), (13, 0), (14, 0), (15, 0)),
+        (3, 0): ((16, 0), (17, 0), (18, 0)),
+        (3, 1): ((19, 0), (20, 0), (21, 0)),
+    }
+    plan = [
+        (key + (mz,), array, plane, core)
+        for (mz, core), arrays in spots.items()
+        for key, (array, plane) in zip(chips, arrays)
+    ]
+    weights = spread(sources, plan, chip, width)
+    weights, f3ac, f3bc, parts1 = fence(weights, f3ac, f3bc, parts1)
+    full_up, full_gate, full_down = spread_last(weights, (f3ac, f3bc), (1, 1, 3), chip)
     mixed_low = jnp.concatenate([parts0, parts1], -1).transpose(1, 0, 2).reshape(local, width)
     branch = matmul(mixed_low, full_output)
     resid = states.astype(f32)
@@ -653,15 +1030,13 @@
     first = resid + astep * (branch_norm - resid)
     middle = normalize(first)
     middle_low = middle.astype(low)
-    middle_both = join(middle_low, swap_dp(middle_low, CORE))
-    upper = matmul(middle_both, full_up)
-    gating = matmul(middle_both, full_gate)
-    upper_scaled = upper * scale_up
-    gate_arg = gating * scale_gate
-    gate_act = jax.nn.silu(gate_arg)
-    hidden = (upper_scaled * gate_act).astype(low)
-    lower = matmul(hidden, full_down)
-    lower = lower[:local] + swap_dp(lower[local:].astype(low), CORE).astype(f32)
+    middle_other = swap_dp(middle_low, CORE)
+
+    flat_up, flat_gate = scale_up.reshape(1, -1), scale_gate.reshape(1, -1)
+    upper, gating, hidden, lower, lower_other, turned = ff_forward(
+        middle_low, middle_other, full_up, full_gate, full_down, flat_up, flat_gate
+    )
+    lower = lower + swap_dp(lower_other, CORE).astype(f32)
     lower_norm = normalize(lower)
     second = middle + mstep * (lower_norm - middle)
     final = normalize(second)
@@ -676,30 +1051,25 @@
     d_middle = d_second * (1.0 - mstep)
     grad_mstep = jnp.sum(d_second * (lower_norm - middle), axis=0)
     d_lower = norm_back(lower, lower_norm, d_second * mstep).astype(low)
-    d_lower_both = join(d_lower, swap_dp(d_lower, CORE))
-    g_down = left_tdot(hidden, d_lower_both).astype(low).reshape(2, 2, 4, 2, hidden_share // 2, width)
-    downs = [Plane(g_down[:, :, :, part], y, x, part == 0) for part in range(2)]
-    sends = [p.far() for p in downs]
-    sends, d_lower_both = fence(sends, d_lower_both)
-    down_far = [p.swap_first(v) for p, v in zip(downs, sends)]
-    d_hidden = right_tdot(d_lower_both, full_down)
-    d_upper = d_hidden * gate_act
-    sigmoid_gate = jax.nn.sigmoid(gate_arg)
-    d_gate_arg = d_hidden * upper_scaled * (sigmoid_gate * (1.0 + gate_arg * (1.0 - sigmoid_gate)))
-    grad_uscale = jnp.sum(d_upper * upper, axis=0)
-    grad_gscale = jnp.sum(d_gate_arg * gating, axis=0)
-    d_up, d_gate = (d_upper * scale_up).astype(low), (d_gate_arg * scale_gate).astype(low)
-    d_up, d_gate, down_far = fence(d_up, d_gate, down_far)
-    down_relay = [p.swap_second(p.relay(v)) for p, v in zip(downs, down_far)]
-    ups = left_tdot(middle_both, d_up).astype(low).reshape(2, 2, 2, 4, share, hidden_half)
-    ups = [Plane(ups[:, :, core], y, x, core == 0) for core in range(2)]
-    corners, up_sides = [p.corner() for p in ups], [p.side() for p in ups]
-    corners, up_sides, down_relay, d_up, d_gate = fence(corners, up_sides, down_relay, d_up, d_gate)
-    up_corner = [p.swap_first(v) for p, v in zip(ups, corners)]
-    d_both = right_tdot(d_up, full_up) + right_tdot(d_gate, full_gate)
-    up_corner, d_both, d_gate, up_sides = fence(up_corner, d_both, d_gate, up_sides)
-    up_side = [p.swap_first(v) for p, v in zip(ups, up_sides)]
-    d_middle = d_middle + d_both[:local] + swap_dp(d_both[local:].astype(low), CORE).astype(f32)
+    d_lower_other = swap_dp(d_lower, CORE)
+    downs = cells(down_back(chip, hidden, d_lower, d_lower_other))
+    downs[0].corner, downs[1].corner, d_lower, d_lower_other = fence(downs[0].corner, downs[1].corner, d_lower, d_lower_other)
+    down_corner = [p.first(p.corner) for p in downs]
+    down_side = [p.first(p.side) for p in downs]
+    d_up, d_gate, grad_uscale, grad_gscale = hidden_back(
+        d_lower, d_lower_other, full_down, upper, gating, flat_up, flat_gate
+    )
+    d_up, d_gate, down_corner, down_side = fence(d_up, d_gate, down_corner, down_side)
+    down_relay = [p.second(v) for p, v in zip(downs, down_corner)]
+    ups = cells(wide_back(chip, turned, d_up))
+    ups[0].corner, ups[1].corner, down_relay, d_up, d_gate = fence(ups[0].corner, ups[1].corner, down_relay, d_up, d_gate)
+    up_corner = [p.first(p.corner) for p in ups]
+    d_both, d_both_other = middle_back(d_up, d_gate, full_up, full_gate)
+    up_corner, d_both, d_both_other, ups[0].side, ups[1].side = fence(
+        up_corner, d_both, d_both_other, ups[0].side, ups[1].side
+    )
+    up_side = [p.first(p.side) for p in ups]
+    d_middle = d_middle + d_both + swap_dp(d_both_other, CORE).astype(f32)
     d_first = norm_back(first, middle, d_middle)
     input_grad = d_first * (1.0 - astep)
     grad_astep = jnp.sum(d_first * (branch_norm - resid), axis=0)
@@ -714,39 +1084,38 @@
     )
     packed = jnp.pad(packed, ((0, 0), (0, 512 - packed.shape[1]))).reshape(2, 2, 2, 4, 4, 128)
     packed = pick(packed, c, 2) + swap_dp(pick(packed, 1 - c, 2), CORE)
-    down = jnp.stack([p.total(v, r) for p, v, r in zip(downs, down_far, down_relay)], 1)
+    down = jnp.concatenate([p.total(v, r) for p, v, r in zip(downs, down_side, down_relay)], 1)
+    down = down.reshape(4, hidden_share, width)
     down_far = swap_z(pick(down, z ^ 3), 1)
     blocks, d_branch, up_side, d_gate, up_corner, packed, down, down_far = fence(
         blocks, d_branch, up_side, d_gate, up_corner, packed, down, down_far
     )
     parts0 = exchange(blocks[0])
-    up_relay = [p.swap_second(p.relay(v, True)) for p, v in zip(ups, up_corner)]
-    gates = left_tdot(middle_both, d_gate).astype(low).reshape(2, 2, 2, 4, share, hidden_half)
-    gates = [Plane(gates[:, :, core], y, x, core == 0) for core in range(2)]
-    corners, gate_sides = [p.corner() for p in gates], [p.side() for p in gates]
+    up_relay = [p.second(v) for p, v in zip(ups, up_corner)]
+    gates = cells(wide_back(chip, turned, d_gate))
     packed = pick(packed, x, 1) + swap_dp(pick(packed, 1 - x, 1), XAX)
-    up_relay, corners, gate_sides, block1, d_branch, packed = fence(
-        up_relay, corners, gate_sides, blocks[1], d_branch, packed
-    )
-    gate_corner = [p.swap_first(v) for p, v in zip(gates, corners)]
-    up = jnp.stack([p.total(v, r, True) for p, v, r in zip(ups, up_side, up_relay)])
+    up_relay, gates[0].corner, gates[1].corner, block1, d_branch, packed = fence(
+        up_relay, gates[0].corner, gates[1].corner, blocks[1], d_branch, packed
+    )
+    gate_corner = [p.first(p.corner) for p in gates]
+    up = jnp.stack([p.total(v, r) for p, v, r in zip(ups, up_side, up_relay)]).reshape(2, 4, share, hidden_half)
     down_far, down_near = swap_z(add_low(pick(down, z ^ 2), down_far), 2), swap_z(pick(down, z ^ 1), 1)
     g_out = left_tdot(mixed_low, d_branch).astype(low).reshape(2, 2, 2, 2, 2 * share, width)
     out_c = swap_dp(pick(g_out, 1 - c, 2), CORE)
     g_out = add_low(pick(g_out, c, 2), out_c)
-    parts0, gate_corner, up, g_out, gate_sides, down_far, down_near = fence(
-        parts0, gate_corner, up, g_out, gate_sides, down_far, down_near
+    parts0, gate_corner, up, g_out, gates[0].side, gates[1].side, down_far, down_near = fence(
+        parts0, gate_corner, up, g_out, gates[0].side, gates[1].side, down_far, down_near
     )
     parts1 = exchange(block1)
-    gate_side = [p.swap_first(v) for p, v in zip(gates, gate_sides)]
-    gate_relay = [p.swap_second(p.relay(v, True)) for p, v in zip(gates, gate_corner)]
+    gate_side = [p.first(p.side) for p in gates]
+    gate_relay = [p.second(v) for p, v in zip(gates, gate_corner)]
     up_far = swap_z(pick(up, z ^ 3, 1), 1)
     d_heads0 = parts0.reshape(tokens, -1)
     d_qkv0, gain_grad0 = attend_back(qkv0, gains[0], lengths, mixed0, d_heads0, qa0, ka0, va0)
     d_qkv0, gain_grad0, parts1, gate_side, gate_relay, up_far, up, packed = fence(
         d_qkv0, gain_grad0, parts1, gate_side, gate_relay, up_far, up, packed
     )
-    gate = jnp.stack([p.total(v, r, True) for p, v, r in zip(gates, gate_side, gate_relay)])
+    gate = jnp.stack([p.total(v, r) for p, v, r in zip(gates, gate_side, gate_relay)]).reshape(2, 4, share, hidden_half)
     up_far, up_near = swap_z(add_low(pick(up, z ^ 2, 1), up_far), 2), swap_z(pick(up, z ^ 1, 1), 1)
     gate_far, gate_near = swap_z(pick(gate, z ^ 3, 1), 1), swap_z(pick(gate, z ^ 1, 1), 1)
     packed = pick(packed, y) + swap_dp(pick(packed, 1 - y), YAX)
@@ -755,54 +1124,42 @@
     d_qkv1, gain_grad1, gate, up_far, up_near, gate_far, gate_near, d_qkv0, packed = fence(
         d_qkv1, gain_grad1, gate, up_far, up_near, gate_far, gate_near, d_qkv0, packed
     )
-    d_qkv = jnp.concatenate([d_qkv0, d_qkv1], 1)
-    d_states = right_tdot(d_qkv, full_qkv).astype(low).reshape(4, local, width)
-    states_send = pick(d_states, z ^ 3)
+    (states_send,) = states_back(line, d_qkv0, d_qkv1, full_qkv, local, (3,))
     gate_send = add_low(pick(gate, z ^ 2, 1), gate_far)
-    states_send, d_states, d_qkv, whole_states, gain_grad1, gate_send, gate, packed = fence(
-        states_send, d_states, d_qkv, whole_states, gain_grad1, gate_send, gate, packed
-    )
-    cut = local // 2
-    relay0 = swap_z(states_send[:cut], 1)
+    states_send, gate_send, gate, packed, d_qkv0, d_qkv1 = fence(states_send, gate_send, gate, packed, d_qkv0, d_qkv1)
+    states_relay = swap_z(states_send, 1)
     gate_far = swap_z(gate_send, 2)
     pair = swap_z(jnp.stack([pick(packed, z ^ 2), pick(packed, z ^ 3)]), 2)
     packed = jnp.stack([pick(packed, z), pick(packed, z ^ 1)]) + pair
+    states_far, states_near, states_own = states_back(line, d_qkv0, d_qkv1, full_qkv, local, (2, 1, 0))
     grad_gain = jnp.concatenate([gain_grad0, gain_grad1], 1).reshape(-1)
     gain_all = lax.dynamic_update_slice(jnp.zeros((4 * heads_width,), f32), grad_gain, (z * heads_width,))
     spare = COLS[0] + 3 * (GROUPS[0][1] - GROUPS[0][0]) * HD
-    g_qkv = left_tdot(whole_states, d_qkv)
-    g_qkv = jnp.where(jnp.arange(three)[None] == spare, gain_all[:, None], g_qkv)
-    g_qkv = g_qkv.astype(low).reshape(2, 2, 2, 2, 2 * share, three)
-    qkv_c = swap_dp(pick(g_qkv, 1 - c, 2), CORE)
-    relay0, qkv_c, g_qkv, d_states, states_send, packed, gate_far = fence(
-        relay0, qkv_c, g_qkv, d_states, states_send, packed, gate_far
-    )
-    relay1 = swap_z(states_send[cut:], 1)
-    far0 = swap_z(add_low(pick(d_states, z ^ 2)[:cut], relay0), 2)
-    g_rows = jnp.concatenate([add_low(pick(g_qkv, c, 2), qkv_c), g_out], -1)
-    rows = [Plane(g_rows[:, :, part], y, x, part == 0) for part in range(2)]
-    row_far = [p.swap_first(p.far()) for p in rows]
+    qkv_keep, qkv_send = rows_back(
+        jnp.stack([y, x, c, z]).astype(jnp.int32), pieces, d_qkv0, d_qkv1, gain_all.reshape(width, 1), spare
+    )
+    states_relay, qkv_send, qkv_keep, states_far, states_near, states_own, packed, gate_far = fence(
+        states_relay, qkv_send, qkv_keep, states_far, states_near, states_own, packed, gate_far
+    )
+    states_far = swap_z(add_low(states_far, states_relay), 2)
+    states_near = swap_z(states_near, 1)
+    qkv_sum = add_low(qkv_keep, swap_dp(qkv_send, CORE))
+    out_sum = [lax.dynamic_slice(g_out, (y ^ (at // 2), x ^ (at % 2), 0, 0, 0), (1, 1) + g_out.shape[2:]) for at in range(4)]
+    out_sum = [v.reshape(2 * 2 * share, width) for v in out_sum]
+    cell = lambda at, unit: jnp.concatenate(
+        [v[2 * share * unit : 2 * share * (unit + 1)] for v in (qkv_sum[at], out_sum[at])], 1
+    )
+    rows = [Cells((cell(3, u), cell(1 + u, u), cell(2 - u, u), cell(0, u)), u == 0) for u in range(2)]
+    row_far = [p.first(jnp.stack([p.side, p.corner])) for p in rows]
     packed = packed[0] + swap_z(packed[1], 1)
     own_rows = total3(pick(up, z, 1), up_near, up_far), total3(pick(gate, z, 1), gate_near, gate_far)
     own_rows = jnp.stack(own_rows, 1)
-    other = swap_dp(pick(own_rows, 1 - c), CORE)
+    own_part, other_part = pick(own_rows, c), swap_dp(pick(own_rows, 1 - c), CORE)
     down_grad = total3(pick(down, z), down_near, down_far).reshape(hidden_share, width)
-    relay1, far0, row_far, d_states, own_rows, other, packed, down_grad = fence(
-        relay1, far0, row_far, d_states, own_rows, other, packed, down_grad
-    )
-    states_near = pick(d_states, z ^ 1)
-    near0 = swap_z(states_near[:cut], 1)
-    row_relay = [p.swap_second(p.relay(v)) for p, v in zip(rows, row_far)]
-    states_send = add_low(pick(d_states, z ^ 2)[cut:], relay1)
-    wide_grad = by_core(c, pick(own_rows, c).reshape(2, share, 4, -1), other.reshape(2, share, 4, -1), 3)
-    up_grad = wide_grad[0].reshape(up_weight.shape)
-    gate_grad = wide_grad[1].reshape(up_weight.shape)
-    near0, row_relay, states_send, states_near, up_grad, gate_grad = fence(
-        near0, row_relay, states_send, states_near, up_grad, gate_grad
-    )
-    rows_sum = jnp.stack([p.total(v, r) for p, v, r in zip(rows, row_far, row_relay)]).reshape(4, share, three + width)
+    row_relay = [p.second(v[1]) for p, v in zip(rows, row_far)]
+    up_grad, gate_grad = interleave(c, own_part, other_part)
+    rows_sum = jnp.stack([p.total(v[0], r) for p, v, r in zip(rows, row_far, row_relay)]).reshape(4, share, three + width)
     columns = exchange(rows_sum)
-    far1, near1 = swap_z(states_send, 2), swap_z(states_near[cut:], 1)
     packed = packed.reshape(512)
     output_grad = jnp.sum(columns[..., three:].astype(f32), 0)
     columns_cut = [
@@ -810,12 +1167,10 @@
     ]
     score_gain_grad = jnp.sum(columns[..., spare].astype(f32), 0)
     columns = jnp.concatenate(columns_cut, -1).transpose(2, 1, 0, 3).reshape(3, share, width).astype(f32)
-    columns, output_grad, score_gain_grad, input_grad, far1, near1 = fence(
-        columns, output_grad, score_gain_grad, input_grad, far1, near1
-    )
-    own = pick(d_states, z)
-    states_sum = [total3(own[:cut], near0, far0), total3(own[cut:], near1, far1)]
-    input_grad = input_grad + jnp.concatenate(states_sum)
+    columns, output_grad, score_gain_grad, input_grad, states_far, states_near, up_grad, gate_grad, down_grad = fence(
+        columns, output_grad, score_gain_grad, input_grad, states_far, states_near, up_grad, gate_grad, down_grad
+    )
+    input_grad = input_grad + total3(states_own, states_near, states_far)
     return (
         final.astype(low)[None],
         packed[cuts[5] - cuts[1]] / count,

time: 898 us -> 797 us (0.89)
  matrix products: 149 us -> 9.83 us
  Pallas kernels: 141 us -> 274 us
  waiting for transfers between devices: 296 us -> 253 us
  local copies, waits for them, and re-layouts: 92.3 us -> 53.8 us
  other arithmetic: 99.3 us -> 80.7 us
    pallas_call x3 -> x12, Pallas kernels: 11.4 us -> 157 us  [the longest x1 34.2 us: ff_forward(): pl.pallas_call(kernel, out_shape=(jax.ShapeDtypeStruct((2 * rows, hidden)...]
    dot_general x5 -> x1, matrix products: 53.8 us -> 1.88 us  [right_tdot(): lax.dot_general(left, right, (((1,), (1,)), ((), ())), preferred_element_...]
    dot_general x6 -> x1, matrix products: 52.7 us -> 4.76 us  [matmul(): return jnp.dot(left, right, preferred_element_type=jnp.float32)]
    dot_general x5 -> x1, matrix products: 42.5 us -> 3.18 us  [left_tdot(): lax.dot_general(left, right, (((0,), (0,)), ((), ())), preferred_element_...]
    ppermute x23 -> x22, waiting for transfers between devices: 170 us -> 141 us  [swap_z(): return lax.ppermute(v, 'ctx', [(i, i ^ mask) for i in range(4)])]
    ppermute x45 -> x53, waiting for transfers between devices: 98.3 us -> 85.1 us  [swap_dp(): return lax.ppermute(v, 'dp', [(i, i ^ bit) for i in range(8)])]
    another operation x12, other arithmetic: 16.5 us -> 4.81 us  [the longest x1 1.33 us: on_cores(): jnp.stack([p.total(v, r) for p, v, r in zip(ups, up_side, up_relay)])]
    unnamed x163 -> x154, local copies, waits for them, and re-layouts: 21.3 us -> 10.1 us
  transfers between devices with their start and end apart: 74 -> 81, of which waited for: 36 -> 33; matrix products, arithmetic and copies ran while one was open for 19% -> 11% of each run, Pallas kernels for 15% -> 28%
where the time goes in v3:
time: 797 us; the launch traced here: 786 us
  Pallas kernels  274 us (34%)
  waiting for transfers between devices  253 us (32%)
  starting transfers between devices  109 us (14%)
  other arithmetic  80.7 us (10%)
  local copies, waits for them, and re-layouts  53.8 us (7%)
  matrix products  9.83 us (1%)
    ppermute x22, waiting for transfers between devices, swap_z(): return lax.ppermute(v, 'ctx', [(i, i ^ mask) for i in range(4)])  141 us
    ppermute x53, waiting for transfers between devices, swap_dp(): return lax.ppermute(v, 'dp', [(i, i ^ bit) for i in range(8)])  85.1 us
    pallas_call x2, Pallas kernels, attend_back(): pl.pallas_call(functools.partial(attend_back_kernel, heads), out_shape=(j...  57.8 us
    ppermute x53, starting transfers between devices, swap_dp(): return lax.ppermute(v, 'dp', [(i, i ^ bit) for i in range(8)])  48.1 us
    pallas_call x1, Pallas kernels, ff_forward(): pl.pallas_call(kernel, out_shape=(jax.ShapeDtypeStruct((2 * rows, hidden)...  34.2 us
    pallas_call x2, Pallas kernels, attend(): pl.pallas_call(functools.partial(attend_kernel, heads), out_shape=(jax.Sh...  32.1 us
    ppermute x22, starting transfers between devices, swap_z(): return lax.ppermute(v, 'ctx', [(i, i ^ mask) for i in range(4)])  31.4 us
    all_to_all x6, starting transfers between devices, exchange(): return lax.all_to_all(blocks, 'ctx', 0, 0, tiled=True)  29.1 us
  transfers between devices with their start and end apart: 81, of which 33 were waited for; matrix products, arithmetic and copies ran while one was open for 11% of the time, Pallas kernels for 28%

profile of v3, /device:TPU:0, one launch (start us, length us, event | category | flops | bytes accessed | tf_op | source)
XLA Modules:
  0.0 786.5 jit_solution(15925962023637084925)
XLA Ops:
  21.6 16.1 %all-to-all-done.refs_0_ = bf16[4,40,2560]{2,1,0:T(8,128)(2,1)S(1)} async-done(((bf16[4,40,2560]{2,1,0:T(8,128)(2,1)}), bf16[4,40,2560]{2,1,0:T(8,128)(2,1)S(1)}, u32[]{:S(2)}, u32[]{:S(2)}) %all-to-all-start) | async-done | bytes 819232 | tf_op jit(solution)/shard_map/all_to_all | solution.py:944
  37.7 8.0 %collective-permute-done.1.refs_1_ = bf16[6,40,2560]{2,1,0:T(8,128)(2,1)} collective-permute-done((bf16[6,40,2560]{2,1,0:T(8,128)(2,1)S(1)}, bf16[6,40,2560]{2,1,0:T(8,128)(2,1)}, u32[]{:S(2)}, u32[]{:S(2)}) %collective-permute-start.1) | collective-permute-done | bytes 1228832 | tf_op jit(solution)/shard_map/ppermute | solution.py:287
  47.0 11.7 %collective-permute-done.3.refs_3_ = bf16[6,40,2560]{2,1,0:T(8,128)(2,1)S(1)} collective-permute-done((bf16[6,40,2560]{2,1,0:T(8,128)(2,1)S(1)}, bf16[6,40,2560]{2,1,0:T(8,128)(2,1)S(1)}, u32[]{:S(2)}, u32[]{:S(2)}) %collective-permute-start.3) | collective-permute-done | bytes 1228832 | tf_op jit(solution)/shard_map/ppermute | solution.py:291
  67.9 54.6 %collective-permute-done.6.refs_1_ = bf16[512,1280]{1,0:T(8,128)(2,1)S(1)} collective-permute-done((bf16[512,1280]{1,0:T(8,128)(2,1)S(1)}, bf16[512,1280]{1,0:T(8,128)(2,1)S(1)}, u32[]{:S(2)}, u32[]{:S(2)}) %collective-permute-start.6) | collective-permute-done | bytes 1310752 | tf_op jit(solution)/shard_map/ppermute | solution.py:291
  131.7 36.3 %collective-permute-done.8.refs_8_ = bf16[3,40,2560]{2,1,0:T(8,128)(2,1)} collective-permute-done((bf16[3,40,2560]{2,1,0:T(8,128)(2,1)S(1)}, bf16[3,40,2560]{2,1,0:T(8,128)(2,1)}, u32[]{:S(2)}, u32[]{:S(2)}) %collective-permute-start.8) | collective-permute-done | bytes 614432 | tf_op jit(solution)/shard_map/ppermute | solution.py:291
  185.4 11.0 %project.1 = (f32[2048,640]{1,0:T(8,128)}, f32[2048,384]{1,0:T(8,128)}) custom-call(s32[1]{0:T(128)} %bitcast.13.line_ref, bf16[512,1280]{1,0:T(8,128)(2,1)} %bitcast.228, bf16[512,1280]{1,0:T(8,128)(2,1)} %copy-done.31, bf16[512,1280]{1,0:T(8,128)(2,1)} %copy-done.32, bf16[512,1280]{1,0:T(8,128)(2,1)} %copy-done.33, bf16[1280,1024]{1,0:T(8,128)(2,1)} %bitcast.225), custom_call_target="tpu_custom_call" | custom-call | bytes 1048576 | tf_op jit(solution)/shard_map/project/pallas_call | solution.py:764
  209.6 19.2 %attend.2 = (f32[2048,192]{1,0:T(8,128)}, bf16[2048,192]{1,0:T(8,128)(2,1)}, bf16[3,2048,128]{2,1,0:T(8,128)(2,1)}, bf16[3,2048,128]{2,1,0:T(8,128)(2,1)}, bf16[3,2048,128]{2,1,0:T(8,128)(2,1)}) custom-call(s32[1]{0:T(128)} %copy.86.length_ref, f32[2048,640]{1,0:T(8,128)} %get-tuple-element.247.qkv_ref, f32[1,192]{1,0:T(1,128)} %slice.313.gain_ref), custom_call_target="tpu_custom_call" | custom-call | flops 12582912 | bytes 8388608 | tf_op jit(solution)/shard_map/attend/pallas_call | solution.py:147
  244.4 12.9 %attend.3 = (f32[2048,128]{1,0:T(8,128)}, bf16[2048,128]{1,0:T(8,128)(2,1)}, bf16[2,2048,128]{2,1,0:T(8,128)(2,1)}, bf16[2,2048,128]{2,1,0:T(8,128)(2,1)}, bf16[2,2048,128]{2,1,0:T(8,128)(2,1)}) custom-call(s32[1]{0:T(128)} %copy.86.length_ref, f32[2048,384]{1,0:T(8,128)} %get-tuple-element.252.qkv_ref, f32[1,128]{1,0:T(1,128)} %slice.314.gain_ref), custom_call_target="tpu_custom_call" | custom-call | flops 8388608 | bytes 8388608 | tf_op jit(solution)/shard_map/attend/pallas_call | solution.py:147
  257.3 8.1 %collective-permute-done.23.refs_20_ = bf16[3,40,2560]{2,1,0:T(8,128)(2,1)S(1)} collective-permute-done((bf16[3,40,2560]{2,1,0:T(8,128)(2,1)S(1)}, bf16[3,40,2560]{2,1,0:T(8,128)(2,1)S(1)}, u32[]{:S(2)}, u32[]{:S(2)}) %collective-permute-start.23) | collective-permute-done | bytes 614432 | tf_op jit(solution)/shard_map/ppermute | solution.py:287
  278.2 14.8 %spread.1 = (bf16[2,2,2,4,40,2560]{5,4,3,2,1,0:T(8,128)(2,1)}, bf16[2,2,2,4,40,2560]{5,4,3,2,1,0:T(8,128)(2,1)}, bf16[2,2,4,2,2,40,1280]{6,5,4,3,2,1,0:T(8,128)(2,1)}) custom-call(s32[3]{0:T(128)} %pad_add_fusion.2.coord_ref, bf16[6,40,2560]{2,1,0:T(8,128)(2,1)} %bitcast.237, bf16[6,40,2560]{2,1,0:T(8,128)(2,1)} %collective-permute-done.1.refs_1_, ...), custom_call_target="tpu_custom_call" | custom-call | bytes 41943040 | tf_op jit(solution)/shard_map/spread/pallas_call | solution.py:446
  305.4 34.2 %ff_forward.1 = (f32[1024,2560]{1,0:T(8,128)}, f32[1024,2560]{1,0:T(8,128)}, bf16[1024,2560]{1,0:T(8,128)(2,1)}, f32[512,1280]{1,0:T(8,128)}, bf16[512,1280]{1,0:T(8,128)(2,1)}, /*index=5*/bf16[1280,1024]{1,0:T(8,128)(2,1)}) custom-call(bf16[512,1280]{1,0:T(8,128)(2,1)} %multiply_convert_fusion.3.own_ref, ...), custom_call_target="tpu_custom_call" | custom-call | bytes 1048576 | tf_op jit(solution)/shard_map/ff_forward/pallas_call | solution.py:553
  361.6 14.0 %down_back.1 = (bf16[640,640]{1,0:T(8,128)(2,1)}, bf16[640,640]{1,0:T(8,128)(2,1)}, bf16[640,640]{1,0:T(8,128)(2,1)}, bf16[640,640]{1,0:T(8,128)(2,1)}, bf16[640...) custom-call(s32[3]{0:T(128)} %pad_add_fusion.2.coord_ref, ...), custom_call_target="tpu_custom_call" | custom-call | bytes 1048576 | tf_op jit(solution)/shard_map/down_back/pallas_call | solution.py:607
  379.7 20.2 %hidden_back.1 = (bf16[1024,2560]{1,0:T(8,128)(2,1)}, bf16[1024,2560]{1,0:T(8,128)(2,1)}, f32[1,2560]{1,0:T(1,128)}, f32[1,2560]{1,0:T(1,128)}) custom-call(bf16[512,1280]{1,0:T(8,128)(2,1)} %copy-done.10, bf16[512,1280]{1,0:T(8,128)(2,1)} %copy-done.23, bf16[2560,1280]{1,0:T(8,128)(2,1)} %bitcast.220, f32[1024,2560]{1,0:T(8,128)} %get-tuple-element.291.upper_ref, ...), custom_call_target="tpu_custom_call" | custom-call | bytes 1048576 | tf_op jit(solution)/shard_map/hidden_back/pallas_call | solution.py:649
  399.9 14.1 %collective-permute-done.34 = bf16[640,640]{1,0:T(8,128)(2,1)} collective-permute-done((bf16[640,640]{1,0:T(8,128)(2,1)}, bf16[640,640]{1,0:T(8,128)(2,1)}, u32[]{:S(2)}, u32[]{:S(2)}) %collective-permute-start.34) | collective-permute-done | bytes 819232 | tf_op jit(solution)/shard_map/ppermute | solution.py:287
  421.0 11.0 %wide_back.2 = (bf16[160,2560]{1,0:T(8,128)(2,1)}, bf16[160,2560]{1,0:T(8,128)(2,1)}, bf16[160,2560]{1,0:T(8,128)(2,1)}, bf16[160,2560]{1,0:T(8,128)(2,1)}, bf16...) custom-call(s32[3]{0:T(128)} %pad_add_fusion.2.coord_ref, ...), custom_call_target="tpu_custom_call" | custom-call | bytes 1048576 | tf_op jit(solution)/shard_map/wide_back/pallas_call | solution.py:690
  445.3 22.0 %middle_back.1 = (f32[512,1280]{1,0:T(8,128)}, bf16[512,1280]{1,0:T(8,128)(2,1)}) custom-call(bf16[1024,2560]{1,0:T(8,128)(2,1)} %get-tuple-element.309.d_ref.d_up_ref, bf16[1024,2560]{1,0:T(8,128)(2,1)} %get-tuple-element.334.d_gate_ref.d_ref, bf16[1280,2560]{1,0:T(8,128)(2,1)} %bitcast.222, bf16[1280,2560]{1,0:T(8,128)(2,1)} %bitcast.224), custom_call_target="tpu_custom_call" | custom-call | bytes 1048576 | tf_op jit(solution)/shard_map/middle_back/pallas_call | solution.py:882
  508.2 11.0 %wide_back.3 = (bf16[160,2560]{1,0:T(8,128)(2,1)}, bf16[160,2560]{1,0:T(8,128)(2,1)}, bf16[160,2560]{1,0:T(8,128)(2,1)}, bf16[160,2560]{1,0:T(8,128)(2,1)}, bf16...) custom-call(s32[3]{0:T(128)} %pad_add_fusion.2.coord_ref, ...), custom_call_target="tpu_custom_call" | custom-call | bytes 1048576 | tf_op jit(solution)/shard_map/wide_back/pallas_call | solution.py:690
  569.8 34.3 %attend_back.2 = (bf16[2048,640]{1,0:T(8,128)(2,1)}, f32[1,192]{1,0:T(1,128)}) custom-call(s32[1]{0:T(128)} %copy.86.length_ref, f32[2048,640]{1,0:T(8,128)} %get-tuple-element.247.qkv_ref, f32[1,192]{1,0:T(1,128)} %slice.313.gain_ref, f32[2048,192]{1,0:T(8,128)} %get-tuple-element.284.mixed_ref, bf16[2048,192]{1,0:T(8,128)(2,1)} %bitcast.250, ...), custom_call_target="tpu_custom_call" | custom-call | flops 12582912 | bytes 8388608 | tf_op jit(solution)/shard_map/attend_back/pallas_call | solution.py:258
  621.7 23.6 %attend_back.3 = (bf16[2048,384]{1,0:T(8,128)(2,1)}, f32[1,128]{1,0:T(1,128)}) custom-call(s32[1]{0:T(128)} %copy.86.length_ref, f32[2048,384]{1,0:T(8,128)} %get-tuple-element.252.qkv_ref, f32[1,128]{1,0:T(1,128)} %slice.314.gain_ref, f32[2048,128]{1,0:T(8,128)} %get-tuple-element.283.mixed_ref, bf16[2048,128]{1,0:T(8,128)(2,1)} %bitcast.255, ...), custom_call_target="tpu_custom_call" | custom-call | flops 8388608 | bytes 8388608 | tf_op jit(solution)/shard_map/attend_back/pallas_call | solution.py:258
  662.3 13.3 %rows_back.1 = (bf16[4,160,1024]{2,1,0:T(8,128)(2,1)}, bf16[4,160,1024]{2,1,0:T(8,128)(2,1)}) custom-call(s32[4]{0:T(128)} %pad_add_fusion.3.coord_ref, bf16[512,1280]{1,0:T(8,128)(2,1)} %bitcast.229, bf16[512,1280]{1,0:T(8,128)(2,1)} %copy-done.31, bf16[512,1280]{1,0:T(8,128)(2,1)} %copy-done.32, bf16[512,1280]{1,0:T(8,128)(2,1)} %copy-done.33, ...), custom_call_target="tpu_custom_call" | custom-call | flops 5368709120 | bytes 16777216 | tf_op jit(solution)/shard_map/rows_back/pallas_call | solution.py:810
  675.6 10.1 %states_back.3 = (bf16[512,1280]{1,0:T(8,128)(2,1)}, bf16[512,1280]{1,0:T(8,128)(2,1)}, bf16[512,1280]{1,0:T(8,128)(2,1)}) custom-call(s32[1]{0:T(128)} %bitcast.13.line_ref, bf16[2048,640]{1,0:T(8,128)(2,1)} %get-tuple-element.390.d0_ref.refs_4_, bf16[2048,384]{1,0:T(8,128)(2,1)} %get-tuple-element.391.d1_ref.refs_5_, bf16[1280,1024]{1,0:T(8,128)(2,1)} %bitcast.227), custom_call_target="tpu_custom_call" | custom-call | bytes 1048576 | tf_op jit(solution)/shard_map/states_back/pallas_call | solution.py:727
  703.7 15.4 %collective-permute-done.68 = bf16[2,80,2304]{2,1,0:T(8,128)(2,1)S(1)} collective-permute-done((bf16[2,80,2304]{2,1,0:T(8,128)(2,1)S(1)}, bf16[2,80,2304]{2,1,0:T(8,128)(2,1)S(1)}, u32[]{:S(2)}, u32[]{:S(2)}) %collective-permute-start.68) | collective-permute-done | bytes 737312 | tf_op jit(solution)/shard_map/ppermute | solution.py:287
  722.6 7.4 collective-permute-done.69
  745.3 16.3 %collective-permute-done.66 = f32[4,128]{1,0:T(4,128)S(1)} collective-permute-done((f32[4,128]{1,0:T(4,128)S(1)}, f32[4,128]{1,0:T(4,128)S(1)}, u32[]{:S(2)}, u32[]{:S(2)}) %collective-permute-start.66) | collective-permute-done | bytes 2080 | tf_op jit(solution)/shard_map/ppermute | solution.py:291
  (478 shorter events, 340.7 us)
Async XLA Ops:
  19.6 39.1 %collective-permute-start.3 = (bf16[6,40,2560]{2,1,0:T(8,128)(2,1)S(1)}, bf16[6,40,2560]{2,1,0:T(8,128)(2,1)S(1)}, u32[]{:S(2)}, u32[]{:S(2)}) collective-permute-start(bf16[6,40,2560]{2,1,0:T(8,128)(2,1)S(1)} %bitcast.236), channel_id=1, source_target_pairs={{0,1},{1,0},{2,3},{3,2},{4,5},{5,4},{6,7},{7,6},{8,9},{9,8},{10,11... | collective-permute-start | bytes 3686408 | tf_op jit(solution)/shard_map/ppermute | solution.py:291
  61.9 60.6 %collective-permute-start.4 = (bf16[13,40,2560]{2,1,0:T(8,128)(2,1)S(1)}, bf16[13,40,2560]{2,1,0:T(8,128)(2,1)S(1)}, u32[]{:S(2)}, u32[]{:S(2)}) collective-permute-start(bf16[13,40,2560]{2,1,0:T(8,128)(2,1)S(1)} %get-tuple-element.442), channel_id=1, source_target_pairs={{0,8},{4,12},{8,0},{12,4},{16,24},{20,28},{24,16},{28,20},{1,9},{5... | collective-permute-start | bytes 7987208 | tf_op jit(solution)/shard_map/ppermute | solution.py:287
  63.4 59.1 %collective-permute-start.5 = (bf16[13,40,2560]{2,1,0:T(8,128)(2,1)S(1)}, bf16[13,40,2560]{2,1,0:T(8,128)(2,1)S(1)}, u32[]{:S(2)}, u32[]{:S(2)}) collective-permute-start(bf16[13,40,2560]{2,1,0:T(8,128)(2,1)S(1)} %get-tuple-element.441), channel_id=1, source_target_pairs={{0,16},{4,20},{8,24},{12,28},{16,0},{20,4},{24,8},{28,12},{1,17},{... | collective-permute-start | bytes 7987208 | tf_op jit(solution)/shard_map/ppermute | solution.py:287
  65.0 57.5 %collective-permute-start.6 = (bf16[512,1280]{1,0:T(8,128)(2,1)S(1)}, bf16[512,1280]{1,0:T(8,128)(2,1)S(1)}, u32[]{:S(2)}, u32[]{:S(2)}) collective-permute-start(bf16[512,1280]{1,0:T(8,128)(2,1)S(1)} %bitcast.230), channel_id=1, source_target_pairs={{0,1},{1,0},{2,3},{3,2},{4,5},{5,4},{6,7},{7,6},{8,9},{9,8},{10,11... | collective-permute-start | bytes 3932168 | tf_op jit(solution)/shard_map/ppermute | solution.py:291
  65.3 57.2 %collective-permute-start.7 = (bf16[512,1280]{1,0:T(8,128)(2,1)S(1)}, bf16[512,1280]{1,0:T(8,128)(2,1)S(1)}, u32[]{:S(2)}, u32[]{:S(2)}) collective-permute-start(bf16[512,1280]{1,0:T(8,128)(2,1)S(1)} %bitcast.231), channel_id=1, source_target_pairs={{0,2},{1,3},{2,0},{3,1},{4,6},{5,7},{6,4},{7,5},{8,10},{9,11},{10,... | collective-permute-start | bytes 3932168 | tf_op jit(solution)/shard_map/ppermute | solution.py:291
  125.3 44.9 %collective-permute-start.12 = (bf16[12,40,2560]{2,1,0:T(8,128)(2,1)S(1)}, bf16[12,40,2560]{2,1,0:T(8,128)(2,1)S(1)}, u32[]{:S(2)}, u32[]{:S(2)}) collective-permute-start(bf16[12,40,2560]{2,1,0:T(8,128)(2,1)S(1)} %pad_maximum_fusion.4), channel_id=1, source_target_pairs={{0,4},{4,0},{8,12},{12,8},{16,20},{20,16},{24,28},{28,24},{1,5},{5... | collective-permute-start | bytes 7372808 | tf_op jit(solution)/shard_map/ppermute | solution.py:287
  125.6 42.4 %collective-permute-start.11 = (bf16[5,40,2560]{2,1,0:T(8,128)(2,1)S(1)}, bf16[5,40,2560]{2,1,0:T(8,128)(2,1)S(1)}, u32[]{:S(2)}, u32[]{:S(2)}) collective-permute-start(bf16[5,40,2560]{2,1,0:T(8,128)(2,1)S(1)} %pad_maximum_fusion.11), channel_id=1, source_target_pairs={{0,16},{4,20},{8,24},{12,28},{16,0},{20,4},{24,8},{28,12},{1,17},{... | collective-permute-start | bytes 3072008 | tf_op jit(solution)/shard_map/ppermute | solution.py:287
  126.2 44.1 %collective-permute-start.9 = (bf16[512,1280]{1,0:T(8,128)(2,1)S(1)}, bf16[512,1280]{1,0:T(8,128)(2,1)S(1)}, u32[]{:S(2)}, u32[]{:S(2)}) collective-permute-start(bf16[512,1280]{1,0:T(8,128)(2,1)S(1)} %collective-permute-done.7.refs_2_), channel_id=1, source_target_pairs={{0,1},{1,0},{2,3},{3,2},{4,5},{5,4},{6,7},{7,6},{8,9},{9,8},{10,11... | collective-permute-start | bytes 3932168 | tf_op jit(solution)/shard_map/ppermute | solution.py:291
  128.1 40.0 %collective-permute-start.10 = (bf16[5,40,2560]{2,1,0:T(8,128)(2,1)S(1)}, bf16[5,40,2560]{2,1,0:T(8,128)(2,1)S(1)}, u32[]{:S(2)}, u32[]{:S(2)}) collective-permute-start(bf16[5,40,2560]{2,1,0:T(8,128)(2,1)S(1)} %pad_maximum_fusion.10), channel_id=1, source_target_pairs={{0,8},{4,12},{8,0},{12,4},{16,24},{20,28},{24,16},{28,20},{1,9},{5... | collective-permute-start | bytes 3072008 | tf_op jit(solution)/shard_map/ppermute | solution.py:287
  128.9 39.1 %collective-permute-start.8 = (bf16[3,40,2560]{2,1,0:T(8,128)(2,1)S(1)}, bf16[3,40,2560]{2,1,0:T(8,128)(2,1)}, u32[]{:S(2)}, u32[]{:S(2)}) collective-permute-start(bf16[3,40,2560]{2,1,0:T(8,128)(2,1)S(1)} %slice.240), channel_id=1, source_target_pairs={{0,2},{1,3},{2,0},{3,1},{4,6},{5,7},{6,4},{7,5},{8,10},{9,11},{10,... | collective-permute-start | bytes 1843208 | tf_op jit(solution)/shard_map/ppermute | solution.py:291
  376.4 37.6 %collective-permute-start.34 = (bf16[640,640]{1,0:T(8,128)(2,1)}, bf16[640,640]{1,0:T(8,128)(2,1)}, u32[]{:S(2)}, u32[]{:S(2)}) collective-permute-start(bf16[640,640]{1,0:T(8,128)(2,1)} %get-tuple-element.297), channel_id=1, source_target_pairs={{0,8},{4,12},{8,0},{12,4},{16,24},{20,28},{24,16},{28,20},{1,9},{5... | collective-permute-start | bytes 2457608 | tf_op jit(solution)/shard_map/ppermute | solution.py:287
  377.7 36.7 %collective-permute-start.35 = (bf16[640,640]{1,0:T(8,128)(2,1)}, bf16[640,640]{1,0:T(8,128)(2,1)S(1)}, u32[]{:S(2)}, u32[]{:S(2)}) collective-permute-start(bf16[640,640]{1,0:T(8,128)(2,1)} %get-tuple-element.298), channel_id=1, source_target_pairs={{0,16},{4,20},{8,24},{12,28},{16,0},{20,4},{24,8},{28,12},{1,17},{... | collective-permute-start | bytes 2457608 | tf_op jit(solution)/shard_map/ppermute | solution.py:287
  551.8 53.4 %collective-permute-start.56 = (bf16[160,2560]{1,0:T(8,128)(2,1)}, bf16[160,2560]{1,0:T(8,128)(2,1)}, u32[]{:S(2)}, u32[]{:S(2)}) collective-permute-start(bf16[160,2560]{1,0:T(8,128)(2,1)} %add_convert_fusion.4), channel_id=1, source_target_pairs={{0,8},{4,12},{8,0},{12,4},{16,24},{20,28},{24,16},{28,20},{1,9},{5... | collective-permute-start | bytes 2457608 | tf_op jit(solution)/shard_map/ppermute | solution.py:287
  555.2 50.0 %collective-permute-start.55 = (bf16[160,2560]{1,0:T(8,128)(2,1)}, bf16[160,2560]{1,0:T(8,128)(2,1)}, u32[]{:S(2)}, u32[]{:S(2)}) collective-permute-start(bf16[160,2560]{1,0:T(8,128)(2,1)} %add_convert_fusion.5), channel_id=1, source_target_pairs={{0,16},{4,20},{8,24},{12,28},{16,0},{20,4},{24,8},{28,12},{1,17},{... | collective-permute-start | bytes 2457608 | tf_op jit(solution)/shard_map/ppermute | solution.py:287
  555.8 49.4 %collective-permute-start.53 = (bf16[160,2560]{1,0:T(8,128)(2,1)}, bf16[160,2560]{1,0:T(8,128)(2,1)}, u32[]{:S(2)}, u32[]{:S(2)}) collective-permute-start(bf16[160,2560]{1,0:T(8,128)(2,1)} %get-tuple-element.360), channel_id=1, source_target_pairs={{0,8},{4,12},{8,0},{12,4},{16,24},{20,28},{24,16},{28,20},{1,9},{5... | collective-permute-start | bytes 2457608 | tf_op jit(solution)/shard_map/ppermute | solution.py:287
  556.5 48.7 %collective-permute-start.54 = (bf16[160,2560]{1,0:T(8,128)(2,1)}, bf16[160,2560]{1,0:T(8,128)(2,1)}, u32[]{:S(2)}, u32[]{:S(2)}) collective-permute-start(bf16[160,2560]{1,0:T(8,128)(2,1)} %get-tuple-element.361), channel_id=1, source_target_pairs={{0,16},{4,20},{8,24},{12,28},{16,0},{20,4},{24,8},{28,12},{1,17},{... | collective-permute-start | bytes 2457608 | tf_op jit(solution)/shard_map/ppermute | solution.py:287
  558.0 47.1 %all-to-all-start.4 = ((bf16[4,512,128]{1,2,0:T(8,128)(2,1)}), bf16[4,512,128]{1,2,0:T(8,128)(2,1)}, u32[]{:S(2)}, u32[]{:S(2)}) async-start(bf16[4,512,128]{1,2,0:T(8,128)(2,1)} %slice.320), calls=%async_computation.4 | async-start | bytes 1048576 | tf_op jit(solution)/shard_map/all_to_all | solution.py:944
  564.9 40.3 %collective-permute-start.57 = (bf16[2,40,2560]{2,1,0:T(8,128)(2,1)}, bf16[2,40,2560]{2,1,0:T(8,128)(2,1)}, u32[]{:S(2)}, u32[]{:S(2)}) collective-permute-start(bf16[2,40,2560]{2,1,0:T(8,128)(2,1)} %dynamic-slice_bitcast_fusion.2), channel_id=1, source_target_pairs={{0,1},{1,0},{2,3},{3,2},{4,5},{5,4},{6,7},{7,6},{8,9},{9,8},{10,11... | collective-permute-start | bytes 1228808 | tf_op jit(solution)/shard_map/ppermute | solution.py:291
  605.2 40.1 %collective-permute-start.62 = (f32[4,4,128]{2,1,0:T(4,128)S(1)}, f32[4,4,128]{2,1,0:T(4,128)S(1)}, u32[]{:S(2)}, u32[]{:S(2)}) collective-permute-start(f32[4,4,128]{2,1,0:T(4,128)S(1)} %fusion.29), channel_id=1, source_target_pairs={{0,16},{4,20},{8,24},{12,28},{16,0},{20,4},{24,8},{28,12},{1,17},{... | collective-permute-start | bytes 24584 | tf_op jit(solution)/shard_map/ppermute | solution.py:287
  656.2 35.7 %collective-permute-start.63 = (bf16[512,1280]{1,0:T(8,128)(2,1)}, bf16[512,1280]{1,0:T(8,128)(2,1)}, u32[]{:S(2)}, u32[]{:S(2)}) collective-permute-start(bf16[512,1280]{1,0:T(8,128)(2,1)} %states_back.2), channel_id=1, source_target_pairs={{0,1},{1,0},{2,3},{3,2},{4,5},{5,4},{6,7},{7,6},{8,9},{9,8},{10,11... | collective-permute-start | bytes 3932168 | tf_op jit(solution)/shard_map/ppermute | solution.py:291
  694.6 70.2 %collective-permute-start.74 = (f32[2,40,2560]{2,1,0:T(8,128)}, f32[2,40,2560]{2,1,0:T(8,128)}, u32[]{:S(2)}, u32[]{:S(2)}) collective-permute-start(f32[2,40,2560]{2,1,0:T(8,128)} %get-tuple-element.443), channel_id=1, source_target_pairs={{0,4},{4,0},{8,12},{12,8},{16,20},{20,16},{24,28},{28,24},{1,5},{5... | collective-permute-start | bytes 2457608 | tf_op jit(solution)/shard_map/ppermute | solution.py:287
  697.7 81.7 %collective-permute-start.72 = (bf16[512,1280]{1,0:T(8,128)(2,1)}, bf16[512,1280]{1,0:T(8,128)(2,1)}, u32[]{:S(2)}, u32[]{:S(2)}) collective-permute-start(bf16[512,1280]{1,0:T(8,128)(2,1)} %add_convert_fusion), channel_id=1, source_target_pairs={{0,2},{1,3},{2,0},{3,1},{4,6},{5,7},{6,4},{7,5},{8,10},{9,11},{10,... | collective-permute-start | bytes 3932168 | tf_op jit(solution)/shard_map/ppermute | solution.py:291
  699.1 80.4 %collective-permute-start.73 = (bf16[512,1280]{1,0:T(8,128)(2,1)}, bf16[512,1280]{1,0:T(8,128)(2,1)}, u32[]{:S(2)}, u32[]{:S(2)}) collective-permute-start(bf16[512,1280]{1,0:T(8,128)(2,1)} %get-tuple-element.407), channel_id=1, source_target_pairs={{0,1},{1,0},{2,3},{3,2},{4,5},{5,4},{6,7},{7,6},{8,9},{9,8},{10,11... | collective-permute-start | bytes 3932168 | tf_op jit(solution)/shard_map/ppermute | solution.py:291
  719.1 42.5 %collective-permute-start.66 = (f32[4,128]{1,0:T(4,128)S(1)}, f32[4,128]{1,0:T(4,128)S(1)}, u32[]{:S(2)}, u32[]{:S(2)}) collective-permute-start(f32[4,128]{1,0:T(4,128)S(1)} %slice_bitcast_fusion.15), channel_id=1, source_target_pairs={{0,1},{1,0},{2,3},{3,2},{4,5},{5,4},{6,7},{7,6},{8,9},{9,8},{10,11... | collective-permute-start | bytes 6152 | tf_op jit(solution)/shard_map/ppermute | solution.py:291
  (134 other events, 2185.8 us)

commit v4 on v3

--- a/solution.py
+++ b/solution.py
@@ -855,6 +855,114 @@
     )(c.astype(jnp.int32).reshape(1), own, other)
 
 
+def row_mean(v):
+    return jnp.mean(v, axis=-1, keepdims=True)
+
+
+def loss_back(inside, scale, lower, lower_got, middle, teacher, mstep):
+    rows, width = lower.shape
+    tile = rows // 4
+    f32, low = jnp.float32, jnp.bfloat16
+
+    def kernel(inside_ref, scale_ref, lower_ref, got_ref, middle_ref, teacher_ref, step_ref,
+               final_ref, d_lower_ref, d_middle_ref, sum_ref, err_ref):
+        at = pl.program_id(0)
+        lower = lower_ref[...] + got_ref[...].astype(f32)
+        middle, mstep = middle_ref[...], step_ref[...]
+        factor = lax.rsqrt(row_mean(lower * lower) + eps)
+        normed = lower * factor
+        second = middle + mstep * (normed - middle)
+        factor_end = lax.rsqrt(row_mean(second * second) + eps)
+        final = second * factor_end
+        final_ref[...] = final.astype(low)
+        diff = final - teacher_ref[...].astype(f32)
+        valid = (lax.broadcasted_iota(jnp.int32, (tile, 1), 0) + at * tile < inside_ref[0]).astype(f32)
+        diff = valid * diff
+        cot = scale_ref[0] * diff
+        d_second = factor_end * (cot - final * row_mean(cot * final))
+        d_middle_ref[...] = d_second * (1.0 - mstep)
+        grad = d_second * mstep
+        d_lower_ref[...] = (factor * (grad - normed * row_mean(grad * normed))).astype(low)
+        sums = jnp.sum(d_second * (normed - middle), axis=0, keepdims=True)
+        errs = jnp.sum(diff * diff, axis=0, keepdims=True)
+
+        @pl.when(at == 0)
+        def _():
+            sum_ref[...] = sums
+            err_ref[...] = errs
+
+        @pl.when(at > 0)
+        def _():
+            sum_ref[...] += sums
+            err_ref[...] += errs
+
+    by_row = pl.BlockSpec((tile, width), lambda i: (i, 0))
+    flat = pl.BlockSpec((1, width), lambda i: (0, 0))
+    smem = pl.BlockSpec(memory_space=pltpu.SMEM)
+    return pl.pallas_call(
+        kernel,
+        out_shape=(
+            jax.ShapeDtypeStruct((rows, width), low),
+            jax.ShapeDtypeStruct((rows, width), low),
+            jax.ShapeDtypeStruct((rows, width), f32),
+            jax.ShapeDtypeStruct((1, width), f32),
+            jax.ShapeDtypeStruct((1, width), f32),
+        ),
+        grid=(rows // tile,),
+        in_specs=[smem, smem, by_row, by_row, by_row, by_row, flat],
+        out_specs=(by_row, by_row, by_row, flat, flat),
+        compiler_params=pltpu.CompilerParams(vmem_limit_bytes=BIG),
+        cost_estimate=small_cost(),
+        name="loss_back",
+    )(inside, scale, lower, lower_got, middle, teacher, mstep)
+
+
+def branch_back(d_middle, d_own, d_got, branch, states, astep):
+    rows, width = branch.shape
+    tile = rows // 4
+    f32, low = jnp.float32, jnp.bfloat16
+
+    def kernel(d_middle_ref, own_ref, got_ref, branch_ref, states_ref, step_ref, grad_ref, d_branch_ref, sum_ref):
+        at = pl.program_id(0)
+        d_middle = d_middle_ref[...] + own_ref[...] + got_ref[...].astype(f32)
+        branch, resid, astep = branch_ref[...], states_ref[...].astype(f32), step_ref[...]
+        factor_branch = lax.rsqrt(row_mean(branch * branch) + eps)
+        normed = branch * factor_branch
+        first = resid + astep * (normed - resid)
+        factor = lax.rsqrt(row_mean(first * first) + eps)
+        middle = first * factor
+        d_first = factor * (d_middle - middle * row_mean(d_middle * middle))
+        grad_ref[...] = d_first * (1.0 - astep)
+        grad = d_first * astep
+        d_branch_ref[...] = (factor_branch * (grad - normed * row_mean(grad * normed))).astype(low)
+        sums = jnp.sum(d_first * (normed - resid), axis=0, keepdims=True)
+
+        @pl.when(at == 0)
+        def _():
+            sum_ref[...] = sums
+
+        @pl.when(at > 0)
+        def _():
+            sum_ref[...] += sums
+
+    by_row = pl.BlockSpec((tile, width), lambda i: (i, 0))
+    flat = pl.BlockSpec((1, width), lambda i: (0, 0))
+    return pl.pallas_call(
+        kernel,
+        out_shape=(
+            jax.ShapeDtypeStruct((rows, width), f32),
+            jax.ShapeDtypeStruct((rows, width), low),
+            jax.ShapeDtypeStruct((1, width), f32),
+        ),
+        grid=(rows // tile,),
+        in_specs=[by_row, by_row, by_row, by_row, by_row, flat],
+        out_specs=(by_row, by_row, flat),
+        compiler_params=pltpu.CompilerParams(vmem_limit_bytes=BIG),
+        cost_estimate=small_cost(),
+        name="branch_back",
+    )(d_middle, d_own, d_got, branch, states, astep)
+
+
 def middle_back(d_up, d_gate, up, gate):
     tokens, hidden = d_up.shape
     width = up.shape[0]
@@ -924,29 +1032,27 @@
     line = z.astype(jnp.int32).reshape(1)
     states = inputs.reshape(local, width)
 
+    half = up_weight.shape[1] // 2
+    ug_own, ug_other, dw = prepare(c, up_weight, gate_weight, down_weight.reshape(4, share, width))
+    def on_x(*v):
+        return swap_dp(jnp.concatenate(v) if len(v) > 1 else v[0], XAX)
+
+    def on_y(*v):
+        return swap_dp(jnp.concatenate(v) if len(v) > 1 else v[0], YAX)
+
+    def exchange(blocks):
+        return lax.all_to_all(blocks, "ctx", 0, 0, tiled=True)
+
+    ug_sib = swap_dp(ug_other, CORE)
+    ug_sib, ug_own, score_gain, query_weight = fence(ug_sib, ug_own, score_gain, query_weight)
+    f0 = jnp.concatenate([by_core(c, ug_own, ug_sib), dw[:, None]], 1).reshape(6, share, half)
     length_parts = jnp.stack([lengths[0] // 64, lengths[0] % 64]).astype(low)
     small = jnp.concatenate([score_gain, attention_step, up_scale, gate_scale, swiglu_step, length_parts])
     cuts = [0]
     for size in (share, share, hidden_share, hidden_share, share, 2):
         cuts.append(cuts[-1] + size)
     small = jnp.pad(small, (0, 512 - small.shape[0])).reshape(2, 256)
-    half = up_weight.shape[1] // 2
-    ug_own, ug_other, dw = prepare(c, up_weight, gate_weight, down_weight.reshape(4, share, width))
-    q0 = prepare_heads(query_weight, key_weight, value_projection, output_weight, small, half)
-
-    def on_x(*v):
-        return swap_dp(jnp.concatenate(v) if len(v) > 1 else v[0], XAX)
-
-    def on_y(*v):
-        return swap_dp(jnp.concatenate(v) if len(v) > 1 else v[0], YAX)
-
-    def exchange(blocks):
-        return lax.all_to_all(blocks, "ctx", 0, 0, tiled=True)
-
-    ug_sib = swap_dp(ug_other, CORE)
-    ug_sib, ug_own = fence(ug_sib, ug_own)
-    f0 = jnp.concatenate([by_core(c, ug_own, ug_sib), dw[:, None]], 1).reshape(6, share, half)
-    q0 = exchange(q0)
+    q0 = exchange(prepare_heads(query_weight, key_weight, value_projection, output_weight, small, half))
     f0x, f0y, f1 = on_x(f0), on_y(f0), swap_z(f0, 1)
     f0, f0x, f0y, f1, q0, states = fence(f0, f0x, f0y, f1, q0, states)
     xb, yb = on_x(f1, f0y[:3], q0), on_y(f1, f0x[3:], q0)
@@ -1036,21 +1142,16 @@
     upper, gating, hidden, lower, lower_other, turned = ff_forward(
         middle_low, middle_other, full_up, full_gate, full_down, flat_up, flat_gate
     )
-    lower = lower + swap_dp(lower_other, CORE).astype(f32)
-    lower_norm = normalize(lower)
-    second = middle + mstep * (lower_norm - middle)
-    final = normalize(second)
-
-    query_pos = z * local + jnp.arange(local, dtype=jnp.int32)
-    valid = (query_pos < lengths[0]).astype(f32).reshape(local, 1)
-    diff = final - teacher.reshape(local, width).astype(f32)
-    err_local = jnp.sum(valid * diff * diff)
-    cot = loss_scale * 2.0 / count * valid * diff
-
-    d_second = norm_back(second, final, cot)
-    d_middle = d_second * (1.0 - mstep)
-    grad_mstep = jnp.sum(d_second * (lower_norm - middle), axis=0)
-    d_lower = norm_back(lower, lower_norm, d_second * mstep).astype(low)
+    final, d_lower, d_middle, grad_mstep, err_sums = loss_back(
+        (lengths - z * local).astype(jnp.int32),
+        (loss_scale * 2.0 / count).reshape(1),
+        lower,
+        swap_dp(lower_other, CORE),
+        middle,
+        teacher.reshape(local, width),
+        mstep.reshape(1, width),
+    )
+    err_local = jnp.sum(err_sums)
     d_lower_other = swap_dp(d_lower, CORE)
     downs = cells(down_back(chip, hidden, d_lower, d_lower_other))
     downs[0].corner, downs[1].corner, d_lower, d_lower_other = fence(downs[0].corner, downs[1].corner, d_lower, d_lower_other)
@@ -1059,21 +1160,19 @@
     d_up, d_gate, grad_uscale, grad_gscale = hidden_back(
         d_lower, d_lower_other, full_down, upper, gating, flat_up, flat_gate
     )
-    d_up, d_gate, down_corner, down_side = fence(d_up, d_gate, down_corner, down_side)
+    d_up, d_gate, down_corner = fence(d_up, d_gate, down_corner)
     down_relay = [p.second(v) for p, v in zip(downs, down_corner)]
     ups = cells(wide_back(chip, turned, d_up))
-    ups[0].corner, ups[1].corner, down_relay, d_up, d_gate = fence(ups[0].corner, ups[1].corner, down_relay, d_up, d_gate)
+    ups[0].corner, ups[1].corner, down_side, d_up, d_gate = fence(ups[0].corner, ups[1].corner, down_side, d_up, d_gate)
     up_corner = [p.first(p.corner) for p in ups]
     d_both, d_both_other = middle_back(d_up, d_gate, full_up, full_gate)
-    up_corner, d_both, d_both_other, ups[0].side, ups[1].side = fence(
-        up_corner, d_both, d_both_other, ups[0].side, ups[1].side
+    down_relay, d_both, d_both_other, ups[0].side, ups[1].side = fence(
+        down_relay, d_both, d_both_other, ups[0].side, ups[1].side
     )
     up_side = [p.first(p.side) for p in ups]
-    d_middle = d_middle + d_both + swap_dp(d_both_other, CORE).astype(f32)
-    d_first = norm_back(first, middle, d_middle)
-    input_grad = d_first * (1.0 - astep)
-    grad_astep = jnp.sum(d_first * (branch_norm - resid), axis=0)
-    d_branch = norm_back(branch, branch_norm, d_first * astep).astype(low)
+    input_grad, d_branch, grad_astep = branch_back(
+        d_middle, d_both, swap_dp(d_both_other, CORE), branch, states, astep.reshape(1, width)
+    )
     d_mixed = right_tdot(d_branch, full_output).astype(low)
     blocks = d_mixed.reshape(local, 4, heads_width).transpose(1, 0, 2)
     blocks = [blocks[:, :, a * HD : b * HD] for a, b in GROUPS]
@@ -1086,25 +1185,23 @@
     packed = pick(packed, c, 2) + swap_dp(pick(packed, 1 - c, 2), CORE)
     down = jnp.concatenate([p.total(v, r) for p, v, r in zip(downs, down_side, down_relay)], 1)
     down = down.reshape(4, hidden_share, width)
-    down_far = swap_z(pick(down, z ^ 3), 1)
-    blocks, d_branch, up_side, d_gate, up_corner, packed, down, down_far = fence(
-        blocks, d_branch, up_side, d_gate, up_corner, packed, down, down_far
-    )
+    blocks, d_branch, d_gate, up_corner, packed, down = fence(blocks, d_branch, d_gate, up_corner, packed, down)
     parts0 = exchange(blocks[0])
     up_relay = [p.second(v) for p, v in zip(ups, up_corner)]
     gates = cells(wide_back(chip, turned, d_gate))
+    down_far = swap_z(pick(down, z ^ 3), 1)
+    parts0, up_relay, up_side, gates[0].corner, gates[1].corner, block1, d_branch, packed = fence(
+        parts0, up_relay, up_side, gates[0].corner, gates[1].corner, blocks[1], d_branch, packed
+    )
     packed = pick(packed, x, 1) + swap_dp(pick(packed, 1 - x, 1), XAX)
-    up_relay, gates[0].corner, gates[1].corner, block1, d_branch, packed = fence(
-        up_relay, gates[0].corner, gates[1].corner, blocks[1], d_branch, packed
-    )
     gate_corner = [p.first(p.corner) for p in gates]
     up = jnp.stack([p.total(v, r) for p, v, r in zip(ups, up_side, up_relay)]).reshape(2, 4, share, hidden_half)
     down_far, down_near = swap_z(add_low(pick(down, z ^ 2), down_far), 2), swap_z(pick(down, z ^ 1), 1)
     g_out = left_tdot(mixed_low, d_branch).astype(low).reshape(2, 2, 2, 2, 2 * share, width)
     out_c = swap_dp(pick(g_out, 1 - c, 2), CORE)
     g_out = add_low(pick(g_out, c, 2), out_c)
-    parts0, gate_corner, up, g_out, gates[0].side, gates[1].side, down_far, down_near = fence(
-        parts0, gate_corner, up, g_out, gates[0].side, gates[1].side, down_far, down_near
+    parts0, gate_corner, up, g_out, gates[0].side, gates[1].side, down_near, packed = fence(
+        parts0, gate_corner, up, g_out, gates[0].side, gates[1].side, down_near, packed
     )
     parts1 = exchange(block1)
     gate_side = [p.first(p.side) for p in gates]
@@ -1112,8 +1209,8 @@
     up_far = swap_z(pick(up, z ^ 3, 1), 1)
     d_heads0 = parts0.reshape(tokens, -1)
     d_qkv0, gain_grad0 = attend_back(qkv0, gains[0], lengths, mixed0, d_heads0, qa0, ka0, va0)
-    d_qkv0, gain_grad0, parts1, gate_side, gate_relay, up_far, up, packed = fence(
-        d_qkv0, gain_grad0, parts1, gate_side, gate_relay, up_far, up, packed
+    d_qkv0, gain_grad0, parts1, gate_side, gate_relay, up_far, up, packed, down_far = fence(
+        d_qkv0, gain_grad0, parts1, gate_side, gate_relay, up_far, up, packed, down_far
     )
     gate = jnp.stack([p.total(v, r) for p, v, r in zip(gates, gate_side, gate_relay)]).reshape(2, 4, share, hidden_half)
     up_far, up_near = swap_z(add_low(pick(up, z ^ 2, 1), up_far), 2), swap_z(pick(up, z ^ 1, 1), 1)
@@ -1172,7 +1269,7 @@
     )
     input_grad = input_grad + total3(states_own, states_near, states_far)
     return (
-        final.astype(low)[None],
+        final[None],
         packed[cuts[5] - cuts[1]] / count,
         input_grad[None],
         columns[0],

time: 797 us -> 759 us (0.952)
  waiting for transfers between devices: 253 us -> 228 us
  other arithmetic: 80.7 us -> 59.4 us
  Pallas kernels: 274 us -> 289 us
    pallas_call x0 -> x2, Pallas kernels: none -> 15.6 us  [the longest x1 8 us: branch_back(): pl.pallas_call(kernel, out_shape=(jax.ShapeDtypeStruct((rows, width), f32...]
    all_to_all x6, waiting for transfers between devices: 27.3 us -> 12.7 us  [exchange(): return lax.all_to_all(blocks, 'ctx', 0, 0, tiled=True)]
    ppermute x22, waiting for transfers between devices: 141 us -> 131 us  [swap_z(): return lax.ppermute(v, 'ctx', [(i, i ^ mask) for i in range(4)])]
  transfers between devices with their start and end apart: 81 -> 81, of which waited for: 33 -> 28; matrix products, arithmetic and copies ran while one was open for 11% -> 11% of each run, Pallas kernels for 28% -> 30%
where the time goes in v4:
time: 759 us; the launch traced here: 748 us
  Pallas kernels  289 us (38%)
  waiting for transfers between devices  228 us (30%)
  starting transfers between devices  104 us (14%)
  other arithmetic  59.4 us (8%)
  local copies, waits for them, and re-layouts  48.8 us (6%)
  matrix products  13 us (2%)
    ppermute x22, waiting for transfers between devices, swap_z(): return lax.ppermute(v, 'ctx', [(i, i ^ mask) for i in range(4)])  131 us
    ppermute x53, waiting for transfers between devices, swap_dp(): return lax.ppermute(v, 'dp', [(i, i ^ bit) for i in range(8)])  84.3 us
    pallas_call x2, Pallas kernels, attend_back(): pl.pallas_call(functools.partial(attend_back_kernel, heads), out_shape=(j...  57.6 us
    ppermute x53, starting transfers between devices, swap_dp(): return lax.ppermute(v, 'dp', [(i, i ^ bit) for i in range(8)])  47.4 us
    pallas_call x1, Pallas kernels, ff_forward(): pl.pallas_call(kernel, out_shape=(jax.ShapeDtypeStruct((2 * rows, hidden)...  34 us
    pallas_call x2, Pallas kernels, attend(): pl.pallas_call(functools.partial(attend_kernel, heads), out_shape=(jax.Sh...  32.1 us
    ppermute x22, starting transfers between devices, swap_z(): return lax.ppermute(v, 'ctx', [(i, i ^ mask) for i in range(4)])  31.7 us
    all_to_all x6, starting transfers between devices, exchange(): return lax.all_to_all(blocks, 'ctx', 0, 0, tiled=True)  25 us
  transfers between devices with their start and end apart: 81, of which 28 were waited for; matrix products, arithmetic and copies ran while one was open for 11% of the time, Pallas kernels for 30%

profile of v4, /device:TPU:0, one launch (start us, length us, event | category | flops | bytes accessed | tf_op | source)
XLA Modules:
  0.0 748.4 jit_solution(6660568065762977681)
XLA Ops:
  19.2 17.7 %collective-permute-done.1.refs_1_ = bf16[6,40,2560]{2,1,0:T(8,128)(2,1)} collective-permute-done((bf16[6,40,2560]{2,1,0:T(8,128)(2,1)S(1)}, bf16[6,40,2560]{2,1,0:T(8,128)(2,1)}, u32[]{:S(2)}, u32[]{:S(2)}) %collective-permute-start.1) | collective-permute-done | bytes 1228832 | tf_op jit(solution)/shard_map/ppermute | solution.py:287
  38.3 11.5 %collective-permute-done.3.refs_3_ = bf16[6,40,2560]{2,1,0:T(8,128)(2,1)} collective-permute-done((bf16[6,40,2560]{2,1,0:T(8,128)(2,1)S(1)}, bf16[6,40,2560]{2,1,0:T(8,128)(2,1)}, u32[]{:S(2)}, u32[]{:S(2)}) %collective-permute-start.3) | collective-permute-done | bytes 1228832 | tf_op jit(solution)/shard_map/ppermute | solution.py:291
  62.2 52.3 %collective-permute-done.6.refs_1_ = bf16[512,1280]{1,0:T(8,128)(2,1)S(1)} collective-permute-done((bf16[512,1280]{1,0:T(8,128)(2,1)S(1)}, bf16[512,1280]{1,0:T(8,128)(2,1)S(1)}, u32[]{:S(2)}, u32[]{:S(2)}) %collective-permute-start.6) | collective-permute-done | bytes 1310752 | tf_op jit(solution)/shard_map/ppermute | solution.py:291
  126.9 36.4 %collective-permute-done.8.refs_8_ = bf16[3,40,2560]{2,1,0:T(8,128)(2,1)} collective-permute-done((bf16[3,40,2560]{2,1,0:T(8,128)(2,1)S(1)}, bf16[3,40,2560]{2,1,0:T(8,128)(2,1)}, u32[]{:S(2)}, u32[]{:S(2)}) %collective-permute-start.8) | collective-permute-done | bytes 614432 | tf_op jit(solution)/shard_map/ppermute | solution.py:291
  179.8 10.9 %project.1 = (f32[2048,640]{1,0:T(8,128)}, f32[2048,384]{1,0:T(8,128)}) custom-call(s32[1]{0:T(128)} %bitcast.16.line_ref, bf16[512,1280]{1,0:T(8,128)(2,1)} %bitcast.218, bf16[512,1280]{1,0:T(8,128)(2,1)} %copy-done.18, bf16[512,1280]{1,0:T(8,128)(2,1)} %copy-done.19, bf16[512,1280]{1,0:T(8,128)(2,1)} %copy-done.20, bf16[1280,1024]{1,0:T(8,128)(2,1)} %bitcast.215), custom_call_target="tpu_custom_call" | custom-call | bytes 1048576 | tf_op jit(solution)/shard_map/project/pallas_call | solution.py:764
  205.6 19.2 %attend.2 = (f32[2048,192]{1,0:T(8,128)}, bf16[2048,192]{1,0:T(8,128)(2,1)}, bf16[3,2048,128]{2,1,0:T(8,128)(2,1)}, bf16[3,2048,128]{2,1,0:T(8,128)(2,1)}, bf16[3,2048,128]{2,1,0:T(8,128)(2,1)}) custom-call(s32[1]{0:T(128)} %copy.74.length_ref, f32[2048,640]{1,0:T(8,128)} %get-tuple-element.258.qkv_ref, f32[1,192]{1,0:T(1,128)} %slice.314.gain_ref), custom_call_target="tpu_custom_call" | custom-call | flops 12582912 | bytes 8388608 | tf_op jit(solution)/shard_map/attend/pallas_call | solution.py:147
  239.5 12.9 %attend.3 = (f32[2048,128]{1,0:T(8,128)}, bf16[2048,128]{1,0:T(8,128)(2,1)}, bf16[2,2048,128]{2,1,0:T(8,128)(2,1)}, bf16[2,2048,128]{2,1,0:T(8,128)(2,1)}, bf16[2,2048,128]{2,1,0:T(8,128)(2,1)}) custom-call(s32[1]{0:T(128)} %copy.74.length_ref, f32[2048,384]{1,0:T(8,128)} %get-tuple-element.263.qkv_ref, f32[1,128]{1,0:T(1,128)} %slice.315.gain_ref), custom_call_target="tpu_custom_call" | custom-call | flops 8388608 | bytes 8388608 | tf_op jit(solution)/shard_map/attend/pallas_call | solution.py:147
  252.4 9.8 %collective-permute-done.23.refs_20_ = bf16[3,40,2560]{2,1,0:T(8,128)(2,1)S(1)} collective-permute-done((bf16[3,40,2560]{2,1,0:T(8,128)(2,1)}, bf16[3,40,2560]{2,1,0:T(8,128)(2,1)S(1)}, u32[]{:S(2)}, u32[]{:S(2)}) %collective-permute-start.23) | collective-permute-done | bytes 614432 | tf_op jit(solution)/shard_map/ppermute | solution.py:287
  272.5 14.8 %spread.1 = (bf16[2,2,2,4,40,2560]{5,4,3,2,1,0:T(8,128)(2,1)}, bf16[2,2,2,4,40,2560]{5,4,3,2,1,0:T(8,128)(2,1)}, bf16[2,2,4,2,2,40,1280]{6,5,4,3,2,1,0:T(8,128)(2,1)}) custom-call(s32[3]{0:T(128)} %pad_add_fusion.2.coord_ref, bf16[6,40,2560]{2,1,0:T(8,128)(2,1)} %bitcast.228, bf16[6,40,2560]{2,1,0:T(8,128)(2,1)} %collective-permute-done.1.refs_1_, ...), custom_call_target="tpu_custom_call" | custom-call | bytes 41943040 | tf_op jit(solution)/shard_map/spread/pallas_call | solution.py:446
  302.1 34.0 %ff_forward.1 = (f32[1024,2560]{1,0:T(8,128)}, f32[1024,2560]{1,0:T(8,128)}, bf16[1024,2560]{1,0:T(8,128)(2,1)}, f32[512,1280]{1,0:T(8,128)}, bf16[512,1280]{1,0:T(8,128)(2,1)}, /*index=5*/bf16[1280,1024]{1,0:T(8,128)(2,1)}) custom-call(bf16[512,1280]{1,0:T(8,128)(2,1)} %get-tuple-element.445.own_ref, bf16[512,1280]{1,0:T(8,128)(2,1)} %copy-done.24, ...), custom_call_target="tpu_custom_call" | custom-call | bytes 1048576 | tf_op jit(solution)/shard_map/ff_forward/pallas_call | solution.py:553
  352.5 14.2 %down_back.1 = (bf16[640,640]{1,0:T(8,128)(2,1)}, bf16[640,640]{1,0:T(8,128)(2,1)}, bf16[640,640]{1,0:T(8,128)(2,1)}, bf16[640,640]{1,0:T(8,128)(2,1)}, bf16[640...) custom-call(s32[3]{0:T(128)} %pad_add_fusion.2.coord_ref, ...), custom_call_target="tpu_custom_call" | custom-call | bytes 1048576 | tf_op jit(solution)/shard_map/down_back/pallas_call | solution.py:607
  370.8 20.2 %hidden_back.1 = (bf16[1024,2560]{1,0:T(8,128)(2,1)}, bf16[1024,2560]{1,0:T(8,128)(2,1)}, f32[1,2560]{1,0:T(1,128)}, f32[1,2560]{1,0:T(1,128)}) custom-call(bf16[512,1280]{1,0:T(8,128)(2,1)} %get-tuple-element.303.own_ref, bf16[512,1280]{1,0:T(8,128)(2,1)} %copy-done.11, bf16[2560,1280]{1,0:T(8,128)(2,1)} %bitcast.210, ...), custom_call_target="tpu_custom_call" | custom-call | bytes 1048576 | tf_op jit(solution)/shard_map/hidden_back/pallas_call | solution.py:649
  397.6 10.9 %wide_back.2 = (bf16[160,2560]{1,0:T(8,128)(2,1)}, bf16[160,2560]{1,0:T(8,128)(2,1)}, bf16[160,2560]{1,0:T(8,128)(2,1)}, bf16[160,2560]{1,0:T(8,128)(2,1)}, bf16...) custom-call(s32[3]{0:T(128)} %pad_add_fusion.2.coord_ref, ...), custom_call_target="tpu_custom_call" | custom-call | bytes 1048576 | tf_op jit(solution)/shard_map/wide_back/pallas_call | solution.py:690
  409.5 21.7 %middle_back.1 = (f32[512,1280]{1,0:T(8,128)}, bf16[512,1280]{1,0:T(8,128)(2,1)}) custom-call(bf16[1024,2560]{1,0:T(8,128)(2,1)} %get-tuple-element.321.d_ref.d_up_ref, bf16[1024,2560]{1,0:T(8,128)(2,1)} %get-tuple-element.350.d_gate_ref.d_ref, bf16[1280,2560]{1,0:T(8,128)(2,1)} %bitcast.212, bf16[1280,2560]{1,0:T(8,128)(2,1)} %bitcast.214), custom_call_target="tpu_custom_call" | custom-call | bytes 1048576 | tf_op jit(solution)/shard_map/middle_back/pallas_call | solution.py:990
  442.7 8.0 %branch_back.1 = (f32[512,1280]{1,0:T(8,128)}, bf16[512,1280]{1,0:T(8,128)(2,1)}, f32[1,1280]{1,0:T(1,128)}) custom-call(f32[512,1280]{1,0:T(8,128)} %get-tuple-element.297.d_middle_ref, f32[512,1280]{1,0:T(8,128)} %get-tuple-element.327.own_ref, bf16[512,1280]{1,0:T(8,128)(2,1)} %copy-done.16, f32[512,1280]{1,0:T(8,128)} %copy-done, ...), custom_call_target="tpu_custom_call" | custom-call | bytes 1048576 | tf_op jit(solution)/shard_map/branch_back/pallas_call | solution.py:950
  472.6 11.0 %wide_back.3 = (bf16[160,2560]{1,0:T(8,128)(2,1)}, bf16[160,2560]{1,0:T(8,128)(2,1)}, bf16[160,2560]{1,0:T(8,128)(2,1)}, bf16[160,2560]{1,0:T(8,128)(2,1)}, bf16...) custom-call(s32[3]{0:T(128)} %pad_add_fusion.2.coord_ref, ...), custom_call_target="tpu_custom_call" | custom-call | bytes 1048576 | tf_op jit(solution)/shard_map/wide_back/pallas_call | solution.py:690
  507.4 11.1 %collective-permute-done.46 = bf16[160,2560]{1,0:T(8,128)(2,1)S(1)} collective-permute-done((bf16[160,2560]{1,0:T(8,128)(2,1)S(1)}, bf16[160,2560]{1,0:T(8,128)(2,1)S(1)}, u32[]{:S(2)}, u32[]{:S(2)}) %collective-permute-start.46) | collective-permute-done | bytes 819232 | tf_op jit(solution)/shard_map/ppermute | solution.py:287
  537.0 34.2 %attend_back.2 = (bf16[2048,640]{1,0:T(8,128)(2,1)}, f32[1,192]{1,0:T(1,128)}) custom-call(s32[1]{0:T(128)} %copy.74.length_ref, f32[2048,640]{1,0:T(8,128)} %get-tuple-element.258.qkv_ref, f32[1,192]{1,0:T(1,128)} %slice.314.gain_ref, f32[2048,192]{1,0:T(8,128)} %get-tuple-element.296.mixed_ref, bf16[2048,192]{1,0:T(8,128)(2,1)} %bitcast.240, ...), custom_call_target="tpu_custom_call" | custom-call | flops 12582912 | bytes 8388608 | tf_op jit(solution)/shard_map/attend_back/pallas_call | solution.py:258
  588.4 23.3 %attend_back.3 = (bf16[2048,384]{1,0:T(8,128)(2,1)}, f32[1,128]{1,0:T(1,128)}) custom-call(s32[1]{0:T(128)} %copy.74.length_ref, f32[2048,384]{1,0:T(8,128)} %get-tuple-element.263.qkv_ref, f32[1,128]{1,0:T(1,128)} %slice.315.gain_ref, f32[2048,128]{1,0:T(8,128)} %get-tuple-element.295.mixed_ref, bf16[2048,128]{1,0:T(8,128)(2,1)} %bitcast.245, ...), custom_call_target="tpu_custom_call" | custom-call | flops 8388608 | bytes 8388608 | tf_op jit(solution)/shard_map/attend_back/pallas_call | solution.py:258
  628.8 13.3 %rows_back.1 = (bf16[4,160,1024]{2,1,0:T(8,128)(2,1)}, bf16[4,160,1024]{2,1,0:T(8,128)(2,1)}) custom-call(s32[4]{0:T(128)} %pad_add_fusion.3.coord_ref, bf16[512,1280]{1,0:T(8,128)(2,1)} %bitcast.220, bf16[512,1280]{1,0:T(8,128)(2,1)} %copy-done.18, bf16[512,1280]{1,0:T(8,128)(2,1)} %copy-done.19, bf16[512,1280]{1,0:T(8,128)(2,1)} %copy-done.20, ...), custom_call_target="tpu_custom_call" | custom-call | flops 5368709120 | bytes 16777216 | tf_op jit(solution)/shard_map/rows_back/pallas_call | solution.py:810
  642.1 10.1 %states_back.3 = (bf16[512,1280]{1,0:T(8,128)(2,1)}, bf16[512,1280]{1,0:T(8,128)(2,1)}, bf16[512,1280]{1,0:T(8,128)(2,1)}) custom-call(s32[1]{0:T(128)} %bitcast.16.line_ref, bf16[2048,640]{1,0:T(8,128)(2,1)} %get-tuple-element.407.d0_ref.refs_4_, bf16[2048,384]{1,0:T(8,128)(2,1)} %get-tuple-element.408.d1_ref.refs_5_, bf16[1280,1024]{1,0:T(8,128)(2,1)} %bitcast.217), custom_call_target="tpu_custom_call" | custom-call | bytes 1048576 | tf_op jit(solution)/shard_map/states_back/pallas_call | solution.py:727
  669.7 14.9 %collective-permute-done.68 = bf16[2,80,2304]{2,1,0:T(8,128)(2,1)S(1)} collective-permute-done((bf16[2,80,2304]{2,1,0:T(8,128)(2,1)S(1)}, bf16[2,80,2304]{2,1,0:T(8,128)(2,1)S(1)}, u32[]{:S(2)}, u32[]{:S(2)}) %collective-permute-start.68) | collective-permute-done | bytes 737312 | tf_op jit(solution)/shard_map/ppermute | solution.py:287
  711.3 11.5 %collective-permute-done.66 = f32[4,128]{1,0:T(4,128)S(1)} collective-permute-done((f32[4,128]{1,0:T(4,128)S(1)}, f32[4,128]{1,0:T(4,128)S(1)}, u32[]{:S(2)}, u32[]{:S(2)}) %collective-permute-start.66) | collective-permute-done | bytes 2080 | tf_op jit(solution)/shard_map/ppermute | solution.py:291
  728.6 9.9 %all-to-all-done.5 = bf16[4,40,2304]{2,1,0:T(8,128)(2,1)S(1)} async-done(((bf16[4,40,2304]{2,1,0:T(8,128)(2,1)}), bf16[4,40,2304]{2,1,0:T(8,128)(2,1)S(1)}, u32[]{:S(2)}, u32[]{:S(2)}) %all-to-all-start.5) | async-done | bytes 737312 | tf_op jit(solution)/shard_map/all_to_all | solution.py:1044
  (456 shorter events, 308.3 us)
Async XLA Ops:
  11.0 38.8 %collective-permute-start.3 = (bf16[6,40,2560]{2,1,0:T(8,128)(2,1)S(1)}, bf16[6,40,2560]{2,1,0:T(8,128)(2,1)}, u32[]{:S(2)}, u32[]{:S(2)}) collective-permute-start(bf16[6,40,2560]{2,1,0:T(8,128)(2,1)S(1)} %bitcast.227), channel_id=1, source_target_pairs={{0,1},{1,0},{2,3},{3,2},{4,5},{5,4},{6,7},{7,6},{8,9},{9,8},{10,11... | collective-permute-start | bytes 3686408 | tf_op jit(solution)/shard_map/ppermute | solution.py:291
  56.9 61.2 %collective-permute-start.4 = (bf16[13,40,2560]{2,1,0:T(8,128)(2,1)S(1)}, bf16[13,40,2560]{2,1,0:T(8,128)(2,1)S(1)}, u32[]{:S(2)}, u32[]{:S(2)}) collective-permute-start(bf16[13,40,2560]{2,1,0:T(8,128)(2,1)S(1)} %get-tuple-element.448), channel_id=1, source_target_pairs={{0,8},{4,12},{8,0},{12,4},{16,24},{20,28},{24,16},{28,20},{1,9},{5... | collective-permute-start | bytes 7987208 | tf_op jit(solution)/shard_map/ppermute | solution.py:287
  57.5 60.6 %collective-permute-start.5 = (bf16[13,40,2560]{2,1,0:T(8,128)(2,1)S(1)}, bf16[13,40,2560]{2,1,0:T(8,128)(2,1)S(1)}, u32[]{:S(2)}, u32[]{:S(2)}) collective-permute-start(bf16[13,40,2560]{2,1,0:T(8,128)(2,1)S(1)} %get-tuple-element.447), channel_id=1, source_target_pairs={{0,16},{4,20},{8,24},{12,28},{16,0},{20,4},{24,8},{28,12},{1,17},{... | collective-permute-start | bytes 7987208 | tf_op jit(solution)/shard_map/ppermute | solution.py:287
  57.8 56.6 %collective-permute-start.6 = (bf16[512,1280]{1,0:T(8,128)(2,1)S(1)}, bf16[512,1280]{1,0:T(8,128)(2,1)S(1)}, u32[]{:S(2)}, u32[]{:S(2)}) collective-permute-start(bf16[512,1280]{1,0:T(8,128)(2,1)S(1)} %bitcast.221), channel_id=1, source_target_pairs={{0,1},{1,0},{2,3},{3,2},{4,5},{5,4},{6,7},{7,6},{8,9},{9,8},{10,11... | collective-permute-start | bytes 3932168 | tf_op jit(solution)/shard_map/ppermute | solution.py:291
  60.6 57.5 %collective-permute-start.7 = (bf16[512,1280]{1,0:T(8,128)(2,1)S(1)}, bf16[512,1280]{1,0:T(8,128)(2,1)S(1)}, u32[]{:S(2)}, u32[]{:S(2)}) collective-permute-start(bf16[512,1280]{1,0:T(8,128)(2,1)S(1)} %bitcast.222), channel_id=1, source_target_pairs={{0,2},{1,3},{2,0},{3,1},{4,6},{5,7},{6,4},{7,5},{8,10},{9,11},{10,... | collective-permute-start | bytes 3932168 | tf_op jit(solution)/shard_map/ppermute | solution.py:291
  118.6 47.0 %collective-permute-start.12 = (bf16[12,40,2560]{2,1,0:T(8,128)(2,1)S(1)}, bf16[12,40,2560]{2,1,0:T(8,128)(2,1)S(1)}, u32[]{:S(2)}, u32[]{:S(2)}) collective-permute-start(bf16[12,40,2560]{2,1,0:T(8,128)(2,1)S(1)} %pad_maximum_fusion.4), channel_id=1, source_target_pairs={{0,4},{4,0},{8,12},{12,8},{16,20},{20,16},{24,28},{28,24},{1,5},{5... | collective-permute-start | bytes 7372808 | tf_op jit(solution)/shard_map/ppermute | solution.py:287
  121.7 41.7 %collective-permute-start.11 = (bf16[5,40,2560]{2,1,0:T(8,128)(2,1)S(1)}, bf16[5,40,2560]{2,1,0:T(8,128)(2,1)S(1)}, u32[]{:S(2)}, u32[]{:S(2)}) collective-permute-start(bf16[5,40,2560]{2,1,0:T(8,128)(2,1)S(1)} %pad_maximum_fusion.11), channel_id=1, source_target_pairs={{0,16},{4,20},{8,24},{12,28},{16,0},{20,4},{24,8},{28,12},{1,17},{... | collective-permute-start | bytes 3072008 | tf_op jit(solution)/shard_map/ppermute | solution.py:287
  123.3 42.3 %collective-permute-start.9 = (bf16[512,1280]{1,0:T(8,128)(2,1)S(1)}, bf16[512,1280]{1,0:T(8,128)(2,1)S(1)}, u32[]{:S(2)}, u32[]{:S(2)}) collective-permute-start(bf16[512,1280]{1,0:T(8,128)(2,1)S(1)} %collective-permute-done.7.refs_2_), channel_id=1, source_target_pairs={{0,1},{1,0},{2,3},{3,2},{4,5},{5,4},{6,7},{7,6},{8,9},{9,8},{10,11... | collective-permute-start | bytes 3932168 | tf_op jit(solution)/shard_map/ppermute | solution.py:291
  123.4 40.0 %collective-permute-start.10 = (bf16[5,40,2560]{2,1,0:T(8,128)(2,1)S(1)}, bf16[5,40,2560]{2,1,0:T(8,128)(2,1)S(1)}, u32[]{:S(2)}, u32[]{:S(2)}) collective-permute-start(bf16[5,40,2560]{2,1,0:T(8,128)(2,1)S(1)} %pad_maximum_fusion.10), channel_id=1, source_target_pairs={{0,8},{4,12},{8,0},{12,4},{16,24},{20,28},{24,16},{28,20},{1,9},{5... | collective-permute-start | bytes 3072008 | tf_op jit(solution)/shard_map/ppermute | solution.py:287
  125.0 38.4 %collective-permute-start.8 = (bf16[3,40,2560]{2,1,0:T(8,128)(2,1)S(1)}, bf16[3,40,2560]{2,1,0:T(8,128)(2,1)}, u32[]{:S(2)}, u32[]{:S(2)}) collective-permute-start(bf16[3,40,2560]{2,1,0:T(8,128)(2,1)S(1)} %slice.240), channel_id=1, source_target_pairs={{0,2},{1,3},{2,0},{3,1},{4,6},{5,7},{6,4},{7,5},{8,10},{9,11},{10,... | collective-permute-start | bytes 1843208 | tf_op jit(solution)/shard_map/ppermute | solution.py:291
  369.9 38.6 %collective-permute-start.36 = (bf16[640,640]{1,0:T(8,128)(2,1)}, bf16[640,640]{1,0:T(8,128)(2,1)S(1)}, u32[]{:S(2)}, u32[]{:S(2)}) collective-permute-start(bf16[640,640]{1,0:T(8,128)(2,1)} %get-tuple-element.318), channel_id=1, source_target_pairs={{0,8},{4,12},{8,0},{12,4},{16,24},{20,28},{24,16},{28,20},{1,9},{5... | collective-permute-start | bytes 2457608 | tf_op jit(solution)/shard_map/ppermute | solution.py:287
  436.1 51.4 %collective-permute-start.44 = (bf16[160,2560]{1,0:T(8,128)(2,1)}, bf16[160,2560]{1,0:T(8,128)(2,1)}, u32[]{:S(2)}, u32[]{:S(2)}) collective-permute-start(bf16[160,2560]{1,0:T(8,128)(2,1)} %get-tuple-element.348), channel_id=1, source_target_pairs={{0,8},{4,12},{8,0},{12,4},{16,24},{20,28},{24,16},{28,20},{1,9},{5... | collective-permute-start | bytes 2457608 | tf_op jit(solution)/shard_map/ppermute | solution.py:287
  437.5 50.0 %collective-permute-start.45 = (bf16[160,2560]{1,0:T(8,128)(2,1)}, bf16[160,2560]{1,0:T(8,128)(2,1)}, u32[]{:S(2)}, u32[]{:S(2)}) collective-permute-start(bf16[160,2560]{1,0:T(8,128)(2,1)} %get-tuple-element.349), channel_id=1, source_target_pairs={{0,16},{4,20},{8,24},{12,28},{16,0},{20,4},{24,8},{28,12},{1,17},{... | collective-permute-start | bytes 2457608 | tf_op jit(solution)/shard_map/ppermute | solution.py:287
  519.9 52.5 %collective-permute-start.54 = (bf16[160,2560]{1,0:T(8,128)(2,1)}, bf16[160,2560]{1,0:T(8,128)(2,1)}, u32[]{:S(2)}, u32[]{:S(2)}) collective-permute-start(bf16[160,2560]{1,0:T(8,128)(2,1)} %add_convert_fusion.4), channel_id=1, source_target_pairs={{0,8},{4,12},{8,0},{12,4},{16,24},{20,28},{24,16},{28,20},{1,9},{5... | collective-permute-start | bytes 2457608 | tf_op jit(solution)/shard_map/ppermute | solution.py:287
  522.5 49.9 %collective-permute-start.53 = (bf16[160,2560]{1,0:T(8,128)(2,1)}, bf16[160,2560]{1,0:T(8,128)(2,1)}, u32[]{:S(2)}, u32[]{:S(2)}) collective-permute-start(bf16[160,2560]{1,0:T(8,128)(2,1)} %add_convert_fusion.5), channel_id=1, source_target_pairs={{0,16},{4,20},{8,24},{12,28},{16,0},{20,4},{24,8},{28,12},{1,17},{... | collective-permute-start | bytes 2457608 | tf_op jit(solution)/shard_map/ppermute | solution.py:287
  522.7 49.6 %collective-permute-start.51 = (bf16[160,2560]{1,0:T(8,128)(2,1)}, bf16[160,2560]{1,0:T(8,128)(2,1)}, u32[]{:S(2)}, u32[]{:S(2)}) collective-permute-start(bf16[160,2560]{1,0:T(8,128)(2,1)} %get-tuple-element.377), channel_id=1, source_target_pairs={{0,8},{4,12},{8,0},{12,4},{16,24},{20,28},{24,16},{28,20},{1,9},{5... | collective-permute-start | bytes 2457608 | tf_op jit(solution)/shard_map/ppermute | solution.py:287
  523.3 49.0 %collective-permute-start.52 = (bf16[160,2560]{1,0:T(8,128)(2,1)}, bf16[160,2560]{1,0:T(8,128)(2,1)}, u32[]{:S(2)}, u32[]{:S(2)}) collective-permute-start(bf16[160,2560]{1,0:T(8,128)(2,1)} %get-tuple-element.378), channel_id=1, source_target_pairs={{0,16},{4,20},{8,24},{12,28},{16,0},{20,4},{24,8},{28,12},{1,17},{... | collective-permute-start | bytes 2457608 | tf_op jit(solution)/shard_map/ppermute | solution.py:287
  525.0 47.3 %all-to-all-start.4 = ((bf16[4,512,128]{1,2,0:T(8,128)(2,1)}), bf16[4,512,128]{1,2,0:T(8,128)(2,1)}, u32[]{:S(2)}, u32[]{:S(2)}) async-start(bf16[4,512,128]{1,2,0:T(8,128)(2,1)} %slice.320), calls=%async_computation.4 | async-start | bytes 1048576 | tf_op jit(solution)/shard_map/all_to_all | solution.py:1044
  532.0 40.3 %collective-permute-start.55 = (bf16[2,40,2560]{2,1,0:T(8,128)(2,1)}, bf16[2,40,2560]{2,1,0:T(8,128)(2,1)}, u32[]{:S(2)}, u32[]{:S(2)}) collective-permute-start(bf16[2,40,2560]{2,1,0:T(8,128)(2,1)} %dynamic-slice_bitcast_fusion.3), channel_id=1, source_target_pairs={{0,1},{1,0},{2,3},{3,2},{4,5},{5,4},{6,7},{7,6},{8,9},{9,8},{10,11... | collective-permute-start | bytes 1228808 | tf_op jit(solution)/shard_map/ppermute | solution.py:291
  572.4 39.4 %collective-permute-start.62 = (f32[4,4,128]{2,1,0:T(4,128)S(1)}, f32[4,4,128]{2,1,0:T(4,128)S(1)}, u32[]{:S(2)}, u32[]{:S(2)}) collective-permute-start(f32[4,4,128]{2,1,0:T(4,128)S(1)} %fusion.31), channel_id=1, source_target_pairs={{0,16},{4,20},{8,24},{12,28},{16,0},{20,4},{24,8},{28,12},{1,17},{... | collective-permute-start | bytes 24584 | tf_op jit(solution)/shard_map/ppermute | solution.py:287
  659.0 67.0 %collective-permute-start.74 = (f32[2,40,2560]{2,1,0:T(8,128)S(1)}, f32[2,40,2560]{2,1,0:T(8,128)}, u32[]{:S(2)}, u32[]{:S(2)}) collective-permute-start(f32[2,40,2560]{2,1,0:T(8,128)S(1)} %get-tuple-element.449), channel_id=1, source_target_pairs={{0,4},{4,0},{8,12},{12,8},{16,20},{20,16},{24,28},{28,24},{1,5},{5... | collective-permute-start | bytes 2457608 | tf_op jit(solution)/shard_map/ppermute | solution.py:287
  662.3 79.2 %collective-permute-start.72 = (bf16[512,1280]{1,0:T(8,128)(2,1)}, bf16[512,1280]{1,0:T(8,128)(2,1)}, u32[]{:S(2)}, u32[]{:S(2)}) collective-permute-start(bf16[512,1280]{1,0:T(8,128)(2,1)} %add_convert_fusion), channel_id=1, source_target_pairs={{0,2},{1,3},{2,0},{3,1},{4,6},{5,7},{6,4},{7,5},{8,10},{9,11},{10,... | collective-permute-start | bytes 3932168 | tf_op jit(solution)/shard_map/ppermute | solution.py:291
  663.9 77.6 %collective-permute-start.73 = (bf16[512,1280]{1,0:T(8,128)(2,1)}, bf16[512,1280]{1,0:T(8,128)(2,1)}, u32[]{:S(2)}, u32[]{:S(2)}) collective-permute-start(bf16[512,1280]{1,0:T(8,128)(2,1)} %get-tuple-element.425), channel_id=1, source_target_pairs={{0,1},{1,0},{2,3},{3,2},{4,5},{5,4},{6,7},{7,6},{8,9},{9,8},{10,11... | collective-permute-start | bytes 3932168 | tf_op jit(solution)/shard_map/ppermute | solution.py:291
  684.6 38.2 %collective-permute-start.66 = (f32[4,128]{1,0:T(4,128)S(1)}, f32[4,128]{1,0:T(4,128)S(1)}, u32[]{:S(2)}, u32[]{:S(2)}) collective-permute-start(f32[4,128]{1,0:T(4,128)S(1)} %slice_bitcast_fusion.15), channel_id=1, source_target_pairs={{0,1},{1,0},{2,3},{3,2},{4,5},{5,4},{6,7},{7,6},{8,9},{9,8},{10,11... | collective-permute-start | bytes 6152 | tf_op jit(solution)/shard_map/ppermute | solution.py:291
  (133 other events, 2015.9 us)

commit v5 on v4

--- a/solution.py
+++ b/solution.py
@@ -1197,11 +1197,8 @@
     gate_corner = [p.first(p.corner) for p in gates]
     up = jnp.stack([p.total(v, r) for p, v, r in zip(ups, up_side, up_relay)]).reshape(2, 4, share, hidden_half)
     down_far, down_near = swap_z(add_low(pick(down, z ^ 2), down_far), 2), swap_z(pick(down, z ^ 1), 1)
-    g_out = left_tdot(mixed_low, d_branch).astype(low).reshape(2, 2, 2, 2, 2 * share, width)
-    out_c = swap_dp(pick(g_out, 1 - c, 2), CORE)
-    g_out = add_low(pick(g_out, c, 2), out_c)
-    parts0, gate_corner, up, g_out, gates[0].side, gates[1].side, down_near, packed = fence(
-        parts0, gate_corner, up, g_out, gates[0].side, gates[1].side, down_near, packed
+    parts0, gate_corner, up, gates[0].side, gates[1].side, down_near, packed, d_branch = fence(
+        parts0, gate_corner, up, gates[0].side, gates[1].side, down_near, packed, d_branch
     )
     parts1 = exchange(block1)
     gate_side = [p.first(p.side) for p in gates]
@@ -1209,8 +1206,8 @@
     up_far = swap_z(pick(up, z ^ 3, 1), 1)
     d_heads0 = parts0.reshape(tokens, -1)
     d_qkv0, gain_grad0 = attend_back(qkv0, gains[0], lengths, mixed0, d_heads0, qa0, ka0, va0)
-    d_qkv0, gain_grad0, parts1, gate_side, gate_relay, up_far, up, packed, down_far = fence(
-        d_qkv0, gain_grad0, parts1, gate_side, gate_relay, up_far, up, packed, down_far
+    d_qkv0, gain_grad0, parts1, gate_side, gate_relay, up_far, up, packed, down_far, d_branch = fence(
+        d_qkv0, gain_grad0, parts1, gate_side, gate_relay, up_far, up, packed, down_far, d_branch
     )
     gate = jnp.stack([p.total(v, r) for p, v, r in zip(gates, gate_side, gate_relay)]).reshape(2, 4, share, hidden_half)
     up_far, up_near = swap_z(add_low(pick(up, z ^ 2, 1), up_far), 2), swap_z(pick(up, z ^ 1, 1), 1)
@@ -1235,12 +1232,15 @@
     qkv_keep, qkv_send = rows_back(
         jnp.stack([y, x, c, z]).astype(jnp.int32), pieces, d_qkv0, d_qkv1, gain_all.reshape(width, 1), spare
     )
-    states_relay, qkv_send, qkv_keep, states_far, states_near, states_own, packed, gate_far = fence(
-        states_relay, qkv_send, qkv_keep, states_far, states_near, states_own, packed, gate_far
+    states_relay, qkv_send, qkv_keep, states_far, states_near, states_own, packed, gate_far, d_branch = fence(
+        states_relay, qkv_send, qkv_keep, states_far, states_near, states_own, packed, gate_far, d_branch
     )
     states_far = swap_z(add_low(states_far, states_relay), 2)
     states_near = swap_z(states_near, 1)
     qkv_sum = add_low(qkv_keep, swap_dp(qkv_send, CORE))
+    g_out = left_tdot(mixed_low, d_branch).astype(low).reshape(2, 2, 2, 2, 2 * share, width)
+    out_c = swap_dp(pick(g_out, 1 - c, 2), CORE)
+    g_out = add_low(pick(g_out, c, 2), out_c)
     out_sum = [lax.dynamic_slice(g_out, (y ^ (at // 2), x ^ (at % 2), 0, 0, 0), (1, 1) + g_out.shape[2:]) for at in range(4)]
     out_sum = [v.reshape(2 * 2 * share, width) for v in out_sum]
     cell = lambda at, unit: jnp.concatenate(

time: 759 us -> 753 us (level)
  transfers between devices with their start and end apart: 81 -> 81, of which waited for: 28 -> 28; matrix products, arithmetic and copies ran while one was open for 11% -> 10% of each run, Pallas kernels for 30% -> 30%
where the time goes in v5:
time: 753 us; the launch traced here: 742 us
  Pallas kernels  289 us (38%)
  waiting for transfers between devices  228 us (30%)
  starting transfers between devices  103 us (14%)
  other arithmetic  58.6 us (8%)
  local copies, waits for them, and re-layouts  44.7 us (6%)
  matrix products  12.5 us (2%)
    ppermute x22, waiting for transfers between devices, swap_z(): return lax.ppermute(v, 'ctx', [(i, i ^ mask) for i in range(4)])  136 us
    ppermute x53, waiting for transfers between devices, swap_dp(): return lax.ppermute(v, 'dp', [(i, i ^ bit) for i in range(8)])  79.7 us
    pallas_call x2, Pallas kernels, attend_back(): pl.pallas_call(functools.partial(attend_back_kernel, heads), out_shape=(j...  57.6 us
    ppermute x53, starting transfers between devices, swap_dp(): return lax.ppermute(v, 'dp', [(i, i ^ bit) for i in range(8)])  46.6 us
    pallas_call x1, Pallas kernels, ff_forward(): pl.pallas_call(kernel, out_shape=(jax.ShapeDtypeStruct((2 * rows, hidden)...  34 us
    pallas_call x2, Pallas kernels, attend(): pl.pallas_call(functools.partial(attend_kernel, heads), out_shape=(jax.Sh...  32.1 us
    ppermute x22, starting transfers between devices, swap_z(): return lax.ppermute(v, 'ctx', [(i, i ^ mask) for i in range(4)])  31.8 us
    all_to_all x6, starting transfers between devices, exchange(): return lax.all_to_all(blocks, 'ctx', 0, 0, tiled=True)  24.8 us
  transfers between devices with their start and end apart: 81, of which 28 were waited for; matrix products, arithmetic and copies ran while one was open for 10% of the time, Pallas kernels for 30%

profile of v5, /device:TPU:0, one launch (start us, length us, event | category | flops | bytes accessed | tf_op | source)
XLA Modules:
  0.0 742.3 jit_solution(15068905126969373977)
XLA Ops:
  19.2 17.7 %collective-permute-done.1.refs_1_ = bf16[6,40,2560]{2,1,0:T(8,128)(2,1)} collective-permute-done((bf16[6,40,2560]{2,1,0:T(8,128)(2,1)S(1)}, bf16[6,40,2560]{2,1,0:T(8,128)(2,1)}, u32[]{:S(2)}, u32[]{:S(2)}) %collective-permute-start.1) | collective-permute-done | bytes 1228832 | tf_op jit(solution)/shard_map/ppermute | solution.py:287
  38.3 11.5 %collective-permute-done.3.refs_3_ = bf16[6,40,2560]{2,1,0:T(8,128)(2,1)} collective-permute-done((bf16[6,40,2560]{2,1,0:T(8,128)(2,1)S(1)}, bf16[6,40,2560]{2,1,0:T(8,128)(2,1)}, u32[]{:S(2)}, u32[]{:S(2)}) %collective-permute-start.3) | collective-permute-done | bytes 1228832 | tf_op jit(solution)/shard_map/ppermute | solution.py:291
  62.2 52.3 %collective-permute-done.6.refs_1_ = bf16[512,1280]{1,0:T(8,128)(2,1)S(1)} collective-permute-done((bf16[512,1280]{1,0:T(8,128)(2,1)S(1)}, bf16[512,1280]{1,0:T(8,128)(2,1)S(1)}, u32[]{:S(2)}, u32[]{:S(2)}) %collective-permute-start.6) | collective-permute-done | bytes 1310752 | tf_op jit(solution)/shard_map/ppermute | solution.py:291
  126.9 36.4 %collective-permute-done.8.refs_8_ = bf16[3,40,2560]{2,1,0:T(8,128)(2,1)} collective-permute-done((bf16[3,40,2560]{2,1,0:T(8,128)(2,1)S(1)}, bf16[3,40,2560]{2,1,0:T(8,128)(2,1)}, u32[]{:S(2)}, u32[]{:S(2)}) %collective-permute-start.8) | collective-permute-done | bytes 614432 | tf_op jit(solution)/shard_map/ppermute | solution.py:291
  179.8 10.9 %project.1 = (f32[2048,640]{1,0:T(8,128)}, f32[2048,384]{1,0:T(8,128)}) custom-call(s32[1]{0:T(128)} %bitcast.16.line_ref, bf16[512,1280]{1,0:T(8,128)(2,1)} %bitcast.218, bf16[512,1280]{1,0:T(8,128)(2,1)} %copy-done.18, bf16[512,1280]{1,0:T(8,128)(2,1)} %copy-done.19, bf16[512,1280]{1,0:T(8,128)(2,1)} %copy-done.20, bf16[1280,1024]{1,0:T(8,128)(2,1)} %bitcast.215), custom_call_target="tpu_custom_call" | custom-call | bytes 1048576 | tf_op jit(solution)/shard_map/project/pallas_call | solution.py:764
  205.6 19.2 %attend.2 = (f32[2048,192]{1,0:T(8,128)}, bf16[2048,192]{1,0:T(8,128)(2,1)}, bf16[3,2048,128]{2,1,0:T(8,128)(2,1)}, bf16[3,2048,128]{2,1,0:T(8,128)(2,1)}, bf16[3,2048,128]{2,1,0:T(8,128)(2,1)}) custom-call(s32[1]{0:T(128)} %copy.74.length_ref, f32[2048,640]{1,0:T(8,128)} %get-tuple-element.260.qkv_ref, f32[1,192]{1,0:T(1,128)} %slice.314.gain_ref), custom_call_target="tpu_custom_call" | custom-call | flops 12582912 | bytes 8388608 | tf_op jit(solution)/shard_map/attend/pallas_call | solution.py:147
  239.6 12.9 %attend.3 = (f32[2048,128]{1,0:T(8,128)}, bf16[2048,128]{1,0:T(8,128)(2,1)}, bf16[2,2048,128]{2,1,0:T(8,128)(2,1)}, bf16[2,2048,128]{2,1,0:T(8,128)(2,1)}, bf16[2,2048,128]{2,1,0:T(8,128)(2,1)}) custom-call(s32[1]{0:T(128)} %copy.74.length_ref, f32[2048,384]{1,0:T(8,128)} %get-tuple-element.265.qkv_ref, f32[1,128]{1,0:T(1,128)} %slice.315.gain_ref), custom_call_target="tpu_custom_call" | custom-call | flops 8388608 | bytes 8388608 | tf_op jit(solution)/shard_map/attend/pallas_call | solution.py:147
  252.4 9.8 %collective-permute-done.23.refs_20_ = bf16[3,40,2560]{2,1,0:T(8,128)(2,1)S(1)} collective-permute-done((bf16[3,40,2560]{2,1,0:T(8,128)(2,1)}, bf16[3,40,2560]{2,1,0:T(8,128)(2,1)S(1)}, u32[]{:S(2)}, u32[]{:S(2)}) %collective-permute-start.23) | collective-permute-done | bytes 614432 | tf_op jit(solution)/shard_map/ppermute | solution.py:287
  272.5 14.8 %spread.1 = (bf16[2,2,2,4,40,2560]{5,4,3,2,1,0:T(8,128)(2,1)}, bf16[2,2,2,4,40,2560]{5,4,3,2,1,0:T(8,128)(2,1)}, bf16[2,2,4,2,2,40,1280]{6,5,4,3,2,1,0:T(8,128)(2,1)}) custom-call(s32[3]{0:T(128)} %pad_add_fusion.2.coord_ref, bf16[6,40,2560]{2,1,0:T(8,128)(2,1)} %bitcast.228, bf16[6,40,2560]{2,1,0:T(8,128)(2,1)} %collective-permute-done.1.refs_1_, ...), custom_call_target="tpu_custom_call" | custom-call | bytes 41943040 | tf_op jit(solution)/shard_map/spread/pallas_call | solution.py:446
  302.0 34.0 %ff_forward.1 = (f32[1024,2560]{1,0:T(8,128)}, f32[1024,2560]{1,0:T(8,128)}, bf16[1024,2560]{1,0:T(8,128)(2,1)}, f32[512,1280]{1,0:T(8,128)}, bf16[512,1280]{1,0:T(8,128)(2,1)}, /*index=5*/bf16[1280,1024]{1,0:T(8,128)(2,1)}) custom-call(bf16[512,1280]{1,0:T(8,128)(2,1)} %get-tuple-element.449.own_ref, bf16[512,1280]{1,0:T(8,128)(2,1)} %copy-done.24, ...), custom_call_target="tpu_custom_call" | custom-call | bytes 1048576 | tf_op jit(solution)/shard_map/ff_forward/pallas_call | solution.py:553
  352.5 14.2 %down_back.1 = (bf16[640,640]{1,0:T(8,128)(2,1)}, bf16[640,640]{1,0:T(8,128)(2,1)}, bf16[640,640]{1,0:T(8,128)(2,1)}, bf16[640,640]{1,0:T(8,128)(2,1)}, bf16[640...) custom-call(s32[3]{0:T(128)} %pad_add_fusion.2.coord_ref, ...), custom_call_target="tpu_custom_call" | custom-call | bytes 1048576 | tf_op jit(solution)/shard_map/down_back/pallas_call | solution.py:607
  370.8 20.3 %hidden_back.1 = (bf16[1024,2560]{1,0:T(8,128)(2,1)}, bf16[1024,2560]{1,0:T(8,128)(2,1)}, f32[1,2560]{1,0:T(1,128)}, f32[1,2560]{1,0:T(1,128)}) custom-call(bf16[512,1280]{1,0:T(8,128)(2,1)} %get-tuple-element.305.own_ref, bf16[512,1280]{1,0:T(8,128)(2,1)} %copy-done.10, bf16[2560,1280]{1,0:T(8,128)(2,1)} %bitcast.210, ...), custom_call_target="tpu_custom_call" | custom-call | bytes 1048576 | tf_op jit(solution)/shard_map/hidden_back/pallas_call | solution.py:649
  397.7 10.9 %wide_back.2 = (bf16[160,2560]{1,0:T(8,128)(2,1)}, bf16[160,2560]{1,0:T(8,128)(2,1)}, bf16[160,2560]{1,0:T(8,128)(2,1)}, bf16[160,2560]{1,0:T(8,128)(2,1)}, bf16...) custom-call(s32[3]{0:T(128)} %pad_add_fusion.2.coord_ref, ...), custom_call_target="tpu_custom_call" | custom-call | bytes 1048576 | tf_op jit(solution)/shard_map/wide_back/pallas_call | solution.py:690
  409.5 21.7 %middle_back.1 = (f32[512,1280]{1,0:T(8,128)}, bf16[512,1280]{1,0:T(8,128)(2,1)}) custom-call(bf16[1024,2560]{1,0:T(8,128)(2,1)} %get-tuple-element.323.d_ref.d_up_ref, bf16[1024,2560]{1,0:T(8,128)(2,1)} %get-tuple-element.352.d_gate_ref.d_ref, bf16[1280,2560]{1,0:T(8,128)(2,1)} %bitcast.212, bf16[1280,2560]{1,0:T(8,128)(2,1)} %bitcast.214), custom_call_target="tpu_custom_call" | custom-call | bytes 1048576 | tf_op jit(solution)/shard_map/middle_back/pallas_call | solution.py:990
  442.7 8.0 %branch_back.1 = (f32[512,1280]{1,0:T(8,128)}, bf16[512,1280]{1,0:T(8,128)(2,1)}, f32[1,1280]{1,0:T(1,128)}) custom-call(f32[512,1280]{1,0:T(8,128)} %get-tuple-element.299.d_middle_ref, f32[512,1280]{1,0:T(8,128)} %get-tuple-element.329.own_ref, bf16[512,1280]{1,0:T(8,128)(2,1)} %copy-done.15, f32[512,1280]{1,0:T(8,128)} %copy-done, ...), custom_call_target="tpu_custom_call" | custom-call | bytes 1048576 | tf_op jit(solution)/shard_map/branch_back/pallas_call | solution.py:950
  472.5 11.0 %wide_back.3 = (bf16[160,2560]{1,0:T(8,128)(2,1)}, bf16[160,2560]{1,0:T(8,128)(2,1)}, bf16[160,2560]{1,0:T(8,128)(2,1)}, bf16[160,2560]{1,0:T(8,128)(2,1)}, bf16...) custom-call(s32[3]{0:T(128)} %pad_add_fusion.2.coord_ref, ...), custom_call_target="tpu_custom_call" | custom-call | bytes 1048576 | tf_op jit(solution)/shard_map/wide_back/pallas_call | solution.py:690
  503.5 9.7 %collective-permute-done.46 = bf16[160,2560]{1,0:T(8,128)(2,1)S(1)} collective-permute-done((bf16[160,2560]{1,0:T(8,128)(2,1)}, bf16[160,2560]{1,0:T(8,128)(2,1)S(1)}, u32[]{:S(2)}, u32[]{:S(2)}) %collective-permute-start.46) | collective-permute-done | bytes 819232 | tf_op jit(solution)/shard_map/ppermute | solution.py:287
  530.3 34.2 %attend_back.2 = (bf16[2048,640]{1,0:T(8,128)(2,1)}, f32[1,192]{1,0:T(1,128)}) custom-call(s32[1]{0:T(128)} %copy.74.length_ref, f32[2048,640]{1,0:T(8,128)} %get-tuple-element.260.qkv_ref, f32[1,192]{1,0:T(1,128)} %slice.314.gain_ref, f32[2048,192]{1,0:T(8,128)} %get-tuple-element.298.mixed_ref, bf16[2048,192]{1,0:T(8,128)(2,1)} %bitcast.240, ...), custom_call_target="tpu_custom_call" | custom-call | flops 12582912 | bytes 8388608 | tf_op jit(solution)/shard_map/attend_back/pallas_call | solution.py:258
  580.7 23.3 %attend_back.3 = (bf16[2048,384]{1,0:T(8,128)(2,1)}, f32[1,128]{1,0:T(1,128)}) custom-call(s32[1]{0:T(128)} %copy.74.length_ref, f32[2048,384]{1,0:T(8,128)} %get-tuple-element.265.qkv_ref, f32[1,128]{1,0:T(1,128)} %slice.315.gain_ref, f32[2048,128]{1,0:T(8,128)} %get-tuple-element.297.mixed_ref, bf16[2048,128]{1,0:T(8,128)(2,1)} %bitcast.245, ...), custom_call_target="tpu_custom_call" | custom-call | flops 8388608 | bytes 8388608 | tf_op jit(solution)/shard_map/attend_back/pallas_call | solution.py:258
  619.6 13.4 %rows_back.1 = (bf16[4,160,1024]{2,1,0:T(8,128)(2,1)}, bf16[4,160,1024]{2,1,0:T(8,128)(2,1)}) custom-call(s32[4]{0:T(128)} %pad_add_fusion.3.coord_ref, bf16[512,1280]{1,0:T(8,128)(2,1)} %bitcast.220, bf16[512,1280]{1,0:T(8,128)(2,1)} %copy-done.18, bf16[512,1280]{1,0:T(8,128)(2,1)} %copy-done.19, bf16[512,1280]{1,0:T(8,128)(2,1)} %copy-done.20, ...), custom_call_target="tpu_custom_call" | custom-call | flops 5368709120 | bytes 16777216 | tf_op jit(solution)/shard_map/rows_back/pallas_call | solution.py:810
  633.0 10.5 %states_back.3 = (bf16[512,1280]{1,0:T(8,128)(2,1)}, bf16[512,1280]{1,0:T(8,128)(2,1)}, bf16[512,1280]{1,0:T(8,128)(2,1)}) custom-call(s32[1]{0:T(128)} %bitcast.16.line_ref, bf16[2048,640]{1,0:T(8,128)(2,1)} %get-tuple-element.410.d0_ref.refs_4_, bf16[2048,384]{1,0:T(8,128)(2,1)} %get-tuple-element.411.d1_ref.refs_5_, bf16[1280,1024]{1,0:T(8,128)(2,1)} %bitcast.217), custom_call_target="tpu_custom_call" | custom-call | bytes 1048576 | tf_op jit(solution)/shard_map/states_back/pallas_call | solution.py:727
  663.9 14.9 %collective-permute-done.68 = bf16[2,80,2304]{2,1,0:T(8,128)(2,1)S(1)} collective-permute-done((bf16[2,80,2304]{2,1,0:T(8,128)(2,1)S(1)}, bf16[2,80,2304]{2,1,0:T(8,128)(2,1)S(1)}, u32[]{:S(2)}, u32[]{:S(2)}) %collective-permute-start.68) | collective-permute-done | bytes 737312 | tf_op jit(solution)/shard_map/ppermute | solution.py:287
  703.9 12.2 %collective-permute-done.65 = f32[4,128]{1,0:T(4,128)S(1)} collective-permute-done((f32[4,128]{1,0:T(4,128)S(1)}, f32[4,128]{1,0:T(4,128)S(1)}, u32[]{:S(2)}, u32[]{:S(2)}) %collective-permute-start.65) | collective-permute-done | bytes 2080 | tf_op jit(solution)/shard_map/ppermute | solution.py:291
  722.8 9.6 %all-to-all-done.5 = bf16[4,40,2304]{2,1,0:T(8,128)(2,1)S(1)} async-done(((bf16[4,40,2304]{2,1,0:T(8,128)(2,1)}), bf16[4,40,2304]{2,1,0:T(8,128)(2,1)S(1)}, u32[]{:S(2)}, u32[]{:S(2)}) %all-to-all-start.5) | async-done | bytes 737312 | tf_op jit(solution)/shard_map/all_to_all | solution.py:1044
  (440 shorter events, 302.7 us)
Async XLA Ops:
  11.0 38.8 %collective-permute-start.3 = (bf16[6,40,2560]{2,1,0:T(8,128)(2,1)S(1)}, bf16[6,40,2560]{2,1,0:T(8,128)(2,1)}, u32[]{:S(2)}, u32[]{:S(2)}) collective-permute-start(bf16[6,40,2560]{2,1,0:T(8,128)(2,1)S(1)} %bitcast.227), channel_id=1, source_target_pairs={{0,1},{1,0},{2,3},{3,2},{4,5},{5,4},{6,7},{7,6},{8,9},{9,8},{10,11... | collective-permute-start | bytes 3686408 | tf_op jit(solution)/shard_map/ppermute | solution.py:291
  56.9 61.2 %collective-permute-start.4 = (bf16[13,40,2560]{2,1,0:T(8,128)(2,1)S(1)}, bf16[13,40,2560]{2,1,0:T(8,128)(2,1)S(1)}, u32[]{:S(2)}, u32[]{:S(2)}) collective-permute-start(bf16[13,40,2560]{2,1,0:T(8,128)(2,1)S(1)} %get-tuple-element.452), channel_id=1, source_target_pairs={{0,8},{4,12},{8,0},{12,4},{16,24},{20,28},{24,16},{28,20},{1,9},{5... | collective-permute-start | bytes 7987208 | tf_op jit(solution)/shard_map/ppermute | solution.py:287
  57.5 60.6 %collective-permute-start.5 = (bf16[13,40,2560]{2,1,0:T(8,128)(2,1)S(1)}, bf16[13,40,2560]{2,1,0:T(8,128)(2,1)S(1)}, u32[]{:S(2)}, u32[]{:S(2)}) collective-permute-start(bf16[13,40,2560]{2,1,0:T(8,128)(2,1)S(1)} %get-tuple-element.451), channel_id=1, source_target_pairs={{0,16},{4,20},{8,24},{12,28},{16,0},{20,4},{24,8},{28,12},{1,17},{... | collective-permute-start | bytes 7987208 | tf_op jit(solution)/shard_map/ppermute | solution.py:287
  57.8 56.6 %collective-permute-start.6 = (bf16[512,1280]{1,0:T(8,128)(2,1)S(1)}, bf16[512,1280]{1,0:T(8,128)(2,1)S(1)}, u32[]{:S(2)}, u32[]{:S(2)}) collective-permute-start(bf16[512,1280]{1,0:T(8,128)(2,1)S(1)} %bitcast.221), channel_id=1, source_target_pairs={{0,1},{1,0},{2,3},{3,2},{4,5},{5,4},{6,7},{7,6},{8,9},{9,8},{10,11... | collective-permute-start | bytes 3932168 | tf_op jit(solution)/shard_map/ppermute | solution.py:291
  60.6 57.5 %collective-permute-start.7 = (bf16[512,1280]{1,0:T(8,128)(2,1)S(1)}, bf16[512,1280]{1,0:T(8,128)(2,1)S(1)}, u32[]{:S(2)}, u32[]{:S(2)}) collective-permute-start(bf16[512,1280]{1,0:T(8,128)(2,1)S(1)} %bitcast.222), channel_id=1, source_target_pairs={{0,2},{1,3},{2,0},{3,1},{4,6},{5,7},{6,4},{7,5},{8,10},{9,11},{10,... | collective-permute-start | bytes 3932168 | tf_op jit(solution)/shard_map/ppermute | solution.py:291
  118.6 47.0 %collective-permute-start.12 = (bf16[12,40,2560]{2,1,0:T(8,128)(2,1)S(1)}, bf16[12,40,2560]{2,1,0:T(8,128)(2,1)S(1)}, u32[]{:S(2)}, u32[]{:S(2)}) collective-permute-start(bf16[12,40,2560]{2,1,0:T(8,128)(2,1)S(1)} %pad_maximum_fusion.4), channel_id=1, source_target_pairs={{0,4},{4,0},{8,12},{12,8},{16,20},{20,16},{24,28},{28,24},{1,5},{5... | collective-permute-start | bytes 7372808 | tf_op jit(solution)/shard_map/ppermute | solution.py:287
  121.7 41.7 %collective-permute-start.11 = (bf16[5,40,2560]{2,1,0:T(8,128)(2,1)S(1)}, bf16[5,40,2560]{2,1,0:T(8,128)(2,1)S(1)}, u32[]{:S(2)}, u32[]{:S(2)}) collective-permute-start(bf16[5,40,2560]{2,1,0:T(8,128)(2,1)S(1)} %pad_maximum_fusion.11), channel_id=1, source_target_pairs={{0,16},{4,20},{8,24},{12,28},{16,0},{20,4},{24,8},{28,12},{1,17},{... | collective-permute-start | bytes 3072008 | tf_op jit(solution)/shard_map/ppermute | solution.py:287
  123.3 42.3 %collective-permute-start.9 = (bf16[512,1280]{1,0:T(8,128)(2,1)S(1)}, bf16[512,1280]{1,0:T(8,128)(2,1)S(1)}, u32[]{:S(2)}, u32[]{:S(2)}) collective-permute-start(bf16[512,1280]{1,0:T(8,128)(2,1)S(1)} %collective-permute-done.7.refs_2_), channel_id=1, source_target_pairs={{0,1},{1,0},{2,3},{3,2},{4,5},{5,4},{6,7},{7,6},{8,9},{9,8},{10,11... | collective-permute-start | bytes 3932168 | tf_op jit(solution)/shard_map/ppermute | solution.py:291
  123.4 40.0 %collective-permute-start.10 = (bf16[5,40,2560]{2,1,0:T(8,128)(2,1)S(1)}, bf16[5,40,2560]{2,1,0:T(8,128)(2,1)S(1)}, u32[]{:S(2)}, u32[]{:S(2)}) collective-permute-start(bf16[5,40,2560]{2,1,0:T(8,128)(2,1)S(1)} %pad_maximum_fusion.10), channel_id=1, source_target_pairs={{0,8},{4,12},{8,0},{12,4},{16,24},{20,28},{24,16},{28,20},{1,9},{5... | collective-permute-start | bytes 3072008 | tf_op jit(solution)/shard_map/ppermute | solution.py:287
  125.0 38.4 %collective-permute-start.8 = (bf16[3,40,2560]{2,1,0:T(8,128)(2,1)S(1)}, bf16[3,40,2560]{2,1,0:T(8,128)(2,1)}, u32[]{:S(2)}, u32[]{:S(2)}) collective-permute-start(bf16[3,40,2560]{2,1,0:T(8,128)(2,1)S(1)} %slice.240), channel_id=1, source_target_pairs={{0,2},{1,3},{2,0},{3,1},{4,6},{5,7},{6,4},{7,5},{8,10},{9,11},{10,... | collective-permute-start | bytes 1843208 | tf_op jit(solution)/shard_map/ppermute | solution.py:291
  369.9 38.7 %collective-permute-start.36 = (bf16[640,640]{1,0:T(8,128)(2,1)}, bf16[640,640]{1,0:T(8,128)(2,1)S(1)}, u32[]{:S(2)}, u32[]{:S(2)}) collective-permute-start(bf16[640,640]{1,0:T(8,128)(2,1)} %get-tuple-element.320), channel_id=1, source_target_pairs={{0,8},{4,12},{8,0},{12,4},{16,24},{20,28},{24,16},{28,20},{1,9},{5... | collective-permute-start | bytes 2457608 | tf_op jit(solution)/shard_map/ppermute | solution.py:287
  370.4 38.1 %collective-permute-start.37 = (bf16[640,640]{1,0:T(8,128)(2,1)}, bf16[640,640]{1,0:T(8,128)(2,1)S(1)}, u32[]{:S(2)}, u32[]{:S(2)}) collective-permute-start(bf16[640,640]{1,0:T(8,128)(2,1)} %get-tuple-element.321), channel_id=1, source_target_pairs={{0,16},{4,20},{8,24},{12,28},{16,0},{20,4},{24,8},{28,12},{1,17},{... | collective-permute-start | bytes 2457608 | tf_op jit(solution)/shard_map/ppermute | solution.py:287
  436.1 51.3 %collective-permute-start.44 = (bf16[160,2560]{1,0:T(8,128)(2,1)}, bf16[160,2560]{1,0:T(8,128)(2,1)}, u32[]{:S(2)}, u32[]{:S(2)}) collective-permute-start(bf16[160,2560]{1,0:T(8,128)(2,1)} %get-tuple-element.350), channel_id=1, source_target_pairs={{0,8},{4,12},{8,0},{12,4},{16,24},{20,28},{24,16},{28,20},{1,9},{5... | collective-permute-start | bytes 2457608 | tf_op jit(solution)/shard_map/ppermute | solution.py:287
  437.5 52.3 %collective-permute-start.45 = (bf16[160,2560]{1,0:T(8,128)(2,1)}, bf16[160,2560]{1,0:T(8,128)(2,1)}, u32[]{:S(2)}, u32[]{:S(2)}) collective-permute-start(bf16[160,2560]{1,0:T(8,128)(2,1)} %get-tuple-element.351), channel_id=1, source_target_pairs={{0,16},{4,20},{8,24},{12,28},{16,0},{20,4},{24,8},{28,12},{1,17},{... | collective-permute-start | bytes 2457608 | tf_op jit(solution)/shard_map/ppermute | solution.py:287
  514.3 50.2 %collective-permute-start.53 = (bf16[160,2560]{1,0:T(8,128)(2,1)}, bf16[160,2560]{1,0:T(8,128)(2,1)}, u32[]{:S(2)}, u32[]{:S(2)}) collective-permute-start(bf16[160,2560]{1,0:T(8,128)(2,1)} %add_convert_fusion.4), channel_id=1, source_target_pairs={{0,8},{4,12},{8,0},{12,4},{16,24},{20,28},{24,16},{28,20},{1,9},{5... | collective-permute-start | bytes 2457608 | tf_op jit(solution)/shard_map/ppermute | solution.py:287
  517.0 47.6 %collective-permute-start.52 = (bf16[160,2560]{1,0:T(8,128)(2,1)}, bf16[160,2560]{1,0:T(8,128)(2,1)}, u32[]{:S(2)}, u32[]{:S(2)}) collective-permute-start(bf16[160,2560]{1,0:T(8,128)(2,1)} %add_convert_fusion.5), channel_id=1, source_target_pairs={{0,16},{4,20},{8,24},{12,28},{16,0},{20,4},{24,8},{28,12},{1,17},{... | collective-permute-start | bytes 2457608 | tf_op jit(solution)/shard_map/ppermute | solution.py:287
  517.3 47.3 %collective-permute-start.50 = (bf16[160,2560]{1,0:T(8,128)(2,1)}, bf16[160,2560]{1,0:T(8,128)(2,1)}, u32[]{:S(2)}, u32[]{:S(2)}) collective-permute-start(bf16[160,2560]{1,0:T(8,128)(2,1)} %get-tuple-element.379), channel_id=1, source_target_pairs={{0,8},{4,12},{8,0},{12,4},{16,24},{20,28},{24,16},{28,20},{1,9},{5... | collective-permute-start | bytes 2457608 | tf_op jit(solution)/shard_map/ppermute | solution.py:287
  517.8 46.8 %collective-permute-start.51 = (bf16[160,2560]{1,0:T(8,128)(2,1)}, bf16[160,2560]{1,0:T(8,128)(2,1)}, u32[]{:S(2)}, u32[]{:S(2)}) collective-permute-start(bf16[160,2560]{1,0:T(8,128)(2,1)} %get-tuple-element.380), channel_id=1, source_target_pairs={{0,16},{4,20},{8,24},{12,28},{16,0},{20,4},{24,8},{28,12},{1,17},{... | collective-permute-start | bytes 2457608 | tf_op jit(solution)/shard_map/ppermute | solution.py:287
  519.5 45.1 %all-to-all-start.4 = ((bf16[4,512,128]{1,2,0:T(8,128)(2,1)}), bf16[4,512,128]{1,2,0:T(8,128)(2,1)}, u32[]{:S(2)}, u32[]{:S(2)}) async-start(bf16[4,512,128]{1,2,0:T(8,128)(2,1)} %slice.320), calls=%async_computation.4 | async-start | bytes 1048576 | tf_op jit(solution)/shard_map/all_to_all | solution.py:1044
  525.5 39.1 %collective-permute-start.54 = (bf16[2,40,2560]{2,1,0:T(8,128)(2,1)}, bf16[2,40,2560]{2,1,0:T(8,128)(2,1)}, u32[]{:S(2)}, u32[]{:S(2)}) collective-permute-start(bf16[2,40,2560]{2,1,0:T(8,128)(2,1)} %dynamic-slice_bitcast_fusion.3), channel_id=1, source_target_pairs={{0,1},{1,0},{2,3},{3,2},{4,5},{5,4},{6,7},{7,6},{8,9},{9,8},{10,11... | collective-permute-start | bytes 1228808 | tf_op jit(solution)/shard_map/ppermute | solution.py:291
  564.6 39.4 %collective-permute-start.61 = (f32[4,4,128]{2,1,0:T(4,128)S(1)}, f32[4,4,128]{2,1,0:T(4,128)S(1)}, u32[]{:S(2)}, u32[]{:S(2)}) collective-permute-start(f32[4,4,128]{2,1,0:T(4,128)S(1)} %fusion.31), channel_id=1, source_target_pairs={{0,16},{4,20},{8,24},{12,28},{16,0},{20,4},{24,8},{28,12},{1,17},{... | collective-permute-start | bytes 24584 | tf_op jit(solution)/shard_map/ppermute | solution.py:287
  653.3 66.0 %collective-permute-start.74 = (f32[2,40,2560]{2,1,0:T(8,128)}, f32[2,40,2560]{2,1,0:T(8,128)S(1)}, u32[]{:S(2)}, u32[]{:S(2)}) collective-permute-start(f32[2,40,2560]{2,1,0:T(8,128)} %get-tuple-element.453), channel_id=1, source_target_pairs={{0,4},{4,0},{8,12},{12,8},{16,20},{20,16},{24,28},{28,24},{1,5},{5... | collective-permute-start | bytes 2457608 | tf_op jit(solution)/shard_map/ppermute | solution.py:287
  656.6 78.8 %collective-permute-start.72 = (bf16[512,1280]{1,0:T(8,128)(2,1)}, bf16[512,1280]{1,0:T(8,128)(2,1)}, u32[]{:S(2)}, u32[]{:S(2)}) collective-permute-start(bf16[512,1280]{1,0:T(8,128)(2,1)} %add_convert_fusion), channel_id=1, source_target_pairs={{0,2},{1,3},{2,0},{3,1},{4,6},{5,7},{6,4},{7,5},{8,10},{9,11},{10,... | collective-permute-start | bytes 3932168 | tf_op jit(solution)/shard_map/ppermute | solution.py:291
  658.5 76.9 %collective-permute-start.73 = (bf16[512,1280]{1,0:T(8,128)(2,1)}, bf16[512,1280]{1,0:T(8,128)(2,1)}, u32[]{:S(2)}, u32[]{:S(2)}) collective-permute-start(bf16[512,1280]{1,0:T(8,128)(2,1)} %get-tuple-element.429), channel_id=1, source_target_pairs={{0,1},{1,0},{2,3},{3,2},{4,5},{5,4},{6,7},{7,6},{8,9},{9,8},{10,11... | collective-permute-start | bytes 3932168 | tf_op jit(solution)/shard_map/ppermute | solution.py:291
  (125 other events, 1944.5 us)
